TPU v7x, 32 devices: a whole 2x2x4 slice. The times are simulated.
32 devices in a mesh: row: 8 (over z, core), col: 4 (over y, x).
Axes of the slice: x: 2, y: 2, z: 4, core: 2. Of those that a mesh axis runs over, the one named last changes fastest.
Arguments:
- inputs: bfloat16 [512, 8192], P('col', 'row'), may hold values from -6 to 6
- weight: bfloat16 [8192, 28672], P('row', 'col'), may hold values from -0.09375 to 0.09375
- mask: int32 [64, 224], P('row', 'col'), may hold values 0 or 1
- cotangent: bfloat16 [512, 28672], P('row', 'col'), may hold values from -6 to 6
Outputs:
- outputs: bfloat16 [512, 28672], P('row', 'col')
- input_grad: bfloat16 [512, 8192], P('col', 'row')
- weight_grad: bfloat16 [8192, 28672], P('row', 'col')
Inputs may be any that keep to these rules, and one draw needn't show every extreme that they name: mask holds only zeros and ones.
All inputs are finite; a program needn't handle non-finite values. No bound on the sum of `mask` on one device may be relied on, other than what follows from the above.
Results may differ from a plain program's by a relative error of at most 0.022.
Values may be sent and summed in bfloat16 or wider, within the bound.
No kernel may reach another device: no remote copies, remote signals or barrier semaphores. Data moves between devices by JAX's collectives and lax.ppermute only.
A program may use at most 128 MiB of HBM per device.

v0:
```python
import jax
import jax.numpy as jnp
from jax import lax
from jax.sharding import PartitionSpec as P

BLOCK = 128


def expand_mask(mask_tile):
    tile_rows, tile_cols = mask_tile.shape
    mask_bf16 = mask_tile.astype(jnp.bfloat16)
    widened = jnp.broadcast_to(mask_bf16[:, None, :, None], (tile_rows, BLOCK, tile_cols, BLOCK))
    return widened.reshape(tile_rows * BLOCK, tile_cols * BLOCK)


def local(inputs, weight, mask, cotangent):
    keep_mask = expand_mask(mask)
    masked = weight * keep_mask
    whole = lax.all_gather(inputs, "col", axis=0, tiled=True)
    token_total = whole.shape[0]
    chosen = whole
    outputs = lax.psum_scatter(
        jnp.dot(chosen, masked, preferred_element_type=jnp.float32).astype(jnp.bfloat16),
        "row",
        scatter_dimension=0,
        tiled=True,
    )
    shard_rows = lax.all_gather(cotangent, "row", axis=0, tiled=True)
    partial_value = lax.dot_general(
        shard_rows, masked, (((1,), (1,)), ((), ())), preferred_element_type=jnp.float32
    )
    grad_parts = partial_value.astype(jnp.bfloat16)
    chosen = whole
    weight_acc = lax.dot_general(
        chosen, shard_rows, (((0,), (0,)), ((), ())), preferred_element_type=jnp.float32
    )
    grad_parts, weight_acc = (grad_parts, weight_acc)
    summed = lax.psum_scatter(
        grad_parts.astype(jnp.float32).astype(jnp.bfloat16), "col", scatter_dimension=0, tiled=True
    )
    grad_scale = token_total ** (-0.5)
    weight_grad = (weight_acc * keep_mask.astype(jnp.float32) * grad_scale).astype(jnp.bfloat16)
    return (outputs, summed, weight_grad)


def solution(mesh):
    placed = (P("col", "row"), P("row", "col"), P("row", "col"), P("row", "col"))
    return jax.shard_map(
        local,
        mesh=mesh,
        in_specs=placed,
        out_specs=(P("row", "col"), P("col", "row"), P("row", "col")),
        check_vma=False,
    )
```

profile of v0, /device:TPU:1, one launch (start us, length us, event | category | flops | bytes accessed | tf_op | source)
XLA Modules:
  0.0 230.5 jit_solution(8012165218406694025)
XLA Ops:
  7.2 0.0 all-gather.5.cloned.1.call-start
  7.2 0.7 all-gather.5.cloned.1.call-update
  7.9 0.0 all-gather.3.cloned.1.call-start
  7.9 0.7 all-gather.3.cloned.1.call-update
  8.6 0.0 reduce-scatter.9.cloned.1.call-start
  8.7 0.7 convert_element_type.23
  9.4 76.2 %all-gather.5.cloned.1.call-done = bf16[512,7168]{1,0:T(8,128)(2,1)} async-done(((bf16[64,7168]{1,0:T(8,128)(2,1)}), bf16[512,7168]{1,0:T(8,128)(2,1)}) %all-gather.5.cloned.1.call-update) | async-done | bytes 7340048 | tf_op jit(solution)/shard_map/all_gather | solution.py:28
  85.6 7.2 %broadcast_in_dim.2 = bf16[8,128,56,128]{3,2,1,0:T(8,128)(2,1)} broadcast(bf16[8,56]{1,0:T(8,128)(2,1)S(1)} %convert_element_type.23), dimensions={0,2} | broadcast | bytes 14680960 | tf_op jit(solution)/shard_map/broadcast_in_dim | solution.py:12
  92.7 15.6 %fusion.3 = bf16[512,1024]{0,1:T(8,128)(2,1)S(1)} fusion(bf16[512,7168]{1,0:T(8,128)(2,1)} %all-gather.5.cloned.1.call-done, bf16[1024,7168]{1,0:T(8,128)(2,1)} %param.5, bf16[128,8,56,128]{3,2,1,0:T(8,128)(2,1)} %bitcast.21), kind=kOutput, calls=%fused_computation.6 | convolution fusion | flops 7524057088 | bytes 37748736 | tf_op jit(solution)/shard_map/dot_general | solution.py:29
  108.3 1.3 copy.13
  109.6 0.0 reduce-scatter.9.cloned.1.call-update
  109.7 0.2 reduce-scatter.7.cloned.1.call-start
  109.9 2.4 %all-gather.3.cloned.1.call-done = bf16[512,1024]{1,0:T(8,128)(2,1)} async-done(((bf16[128,1024]{1,0:T(8,128)(2,1)}), bf16[512,1024]{1,0:T(8,128)(2,1)}) %all-gather.3.cloned.1.call-update) | async-done | bytes 1048592 | tf_op jit(solution)/shard_map/all_gather | solution.py:19
  112.3 23.5 %fusion = bf16[512,7168]{0,1:T(8,128)(2,1)} fusion(bf16[512,1024]{1,0:T(8,128)(2,1)} %all-gather.3.cloned.1.call-done, bf16[1024,7168]{1,0:T(8,128)(2,1)} %param.5, bf16[128,8,56,128]{3,2,1,0:T(8,128)(2,1)} %bitcast.22), kind=kOutput, calls=%fused_computation.3 | convolution fusion | flops 7527202816 | bytes 37748736 | tf_op jit(solution)/shard_map/dot_general | solution.py:23
  135.8 0.0 copy-start
  135.8 10.2 %copy.11 = bf16[512,7168]{1,0:T(8,128)(2,1)} copy(bf16[512,7168]{0,1:T(8,128)(2,1)} %fusion) | data formatting | bytes 14680064
  145.9 0.0 reduce-scatter.7.cloned.1.call-update
  146.0 0.0 copy-done
  146.0 19.3 %multiply_convert_fusion = bf16[1024,7168]{1,0:T(8,128)(2,1)} fusion(bf16[512,1024]{1,0:T(8,128)(2,1)S(1)} %copy-done, bf16[512,7168]{1,0:T(8,128)(2,1)} %all-gather.5.cloned.1.call-done, bf16[128,8,56,128]{3,2,1,0:T(8,128)(2,1)} %bitcast.23), kind=kOutput, calls=%fused_computation | convolution fusion | flops 7545552896 | bytes 37748736 | tf_op jit(solution)/shard_map/dot_general | solution.py:34
  165.3 0.0 reduce-scatter.9.cloned.1.call-done
  165.3 58.6 %reduce-scatter.7.cloned.1.call-done = bf16[64,7168]{1,0:T(8,128)(2,1)} async-done(((bf16[512,7168]{1,0:T(8,128)(2,1)}), bf16[64,7168]{1,0:T(8,128)(2,1)}) %reduce-scatter.7.cloned.1.call-update) | async-done | bytes 917520
Async XLA Ops:
  7.2 78.4 %all-gather.5.cloned.1.call-start = ((), (), s32[]{:S(2)}) async-start(), calls=%async_computation.3 | async-start | bytes 8257536 | tf_op jit(solution)/shard_map/all_gather | solution.py:28
  7.9 104.4 %all-gather.3.cloned.1.call-start = ((), (), s32[]{:S(2)}) async-start(), calls=%async_computation.2 | async-start | bytes 1310720 | tf_op jit(solution)/shard_map/all_gather | solution.py:19
  8.6 156.7 %reduce-scatter.9.cloned.1.call-start = ((), (), s32[]{:S(2)}) async-start(), calls=%async_computation.5 | async-start | bytes 1310720
  109.7 114.3 %reduce-scatter.7.cloned.1.call-start = ((), (), s32[]{:S(2)}) async-start(), calls=%async_computation.4 | async-start | bytes 8257536
  135.8 10.2 %copy-start = (bf16[512,1024]{1,0:T(8,128)(2,1)S(1)}, bf16[512,1024]{1,0:T(8,128)(2,1)}, u32[]{:S(2)}) copy-start(bf16[512,1024]{1,0:T(8,128)(2,1)} %all-gather.3.cloned.1.call-done) | copy-start | bytes 3145732
Sparse Core Ops, SparseCore 0:
  9.6 75.8 all-gather.4
  87.4 24.8 all-gather.2
  115.7 27.7 reduce-scatter.8
  146.3 77.5 reduce-scatter.6
where the time goes:
time: 234 us; the launch traced here: 230 us
  waiting for transfers between devices  139 us (59%)
  matrix products  58.4 us (25%)
  local copies, waits for them, and re-layouts  18.7 us (8%)
  between operations  13.8 us (6%)
    all_gather x1, waiting for transfers between devices, local(): shard_rows = lax.all_gather(cotangent, 'row', axis=0, tiled=True)  76.2 us
    unnamed x6, waiting for transfers between devices  60.1 us
    dot_general x1, matrix products, local(): jnp.dot(chosen, masked, preferred_element_type=jnp.float32)  23.5 us
    dot_general x1, matrix products, local(): lax.dot_general(chosen, shard_rows, (((0,), (0,)), ((), ())), preferred_e...  19.3 us
    dot_general x1, matrix products, local(): lax.dot_general(shard_rows, masked, (((1,), (1,)), ((), ())), preferred_e...  15.6 us
    unnamed x4, local copies, waits for them, and re-layouts  11.5 us
    broadcast_in_dim x1, local copies, waits for them, and re-layouts, expand_mask(): jnp.broadcast_to(mask_bf16[:, None, :, None], (tile_rows, BLOCK, tile_col...  7.15 us
  transfers between devices with their start and end apart: 4, of which 3 were waited for; matrix products, arithmetic and copies ran while one was open for 34% of the time, Pallas kernels for 0%

commit v1 on v0

v1 whole, which is shorter than its diff:
```python
import functools

import jax
import jax.numpy as jnp
from jax import lax
from jax.experimental import pallas as pl
from jax.experimental.pallas import tpu as pltpu
from jax.sharding import PartitionSpec as P

BLOCK = 128
PARTS = 2
VMEM_LIMIT = 48 * 1024 * 1024


def tile_of(width):
    return next(t for t in (512, 256, 128) if width % t == 0)


def masked_tile(w_ref, keep_ref, wm_ref):
    for a in range(w_ref.shape[0] // BLOCK):
        rows = slice(a * BLOCK, (a + 1) * BLOCK)
        keep = keep_ref[a : a + 1, :].astype(jnp.bfloat16)
        wm_ref[rows, :] = w_ref[rows, :] * keep


def forward_kernel(n, cols, place_ref, *refs):
    x_refs, (w_ref, keep_ref), (mine_ref, other_ref, whole_ref), (xs, wm) = (
        refs[:cols],
        refs[cols : cols + 2],
        refs[cols + 2 : cols + 5],
        refs[cols + 5 :],
    )
    core, col = place_ref[1], place_ref[2]
    own = x_refs[0].shape[0]
    tr = xs.shape[0] // (2 * n)
    half = n * tr

    @pl.when(pl.program_id(0) == 0)
    def _():
        for k in range(cols):
            at = pl.multiple_of((col ^ k) * own, own)
            whole_ref[pl.ds(at, own), :] = x_refs[k][...]
        for z in range(n):
            for p in range(2):
                at = pl.multiple_of((2 * z + (core ^ p)) * tr, tr)
                xs[pl.ds(p * half + z * tr, tr), :] = whole_ref[pl.ds(at, tr), :]

    masked_tile(w_ref, keep_ref, wm)
    acc = jnp.dot(xs[...], wm[...], preferred_element_type=jnp.float32)
    mine_ref[...] = acc[:half].astype(jnp.bfloat16)
    other_ref[...] = acc[half:].astype(jnp.bfloat16)


def forward(place, xs, weight, keep, part, n):
    depth, width = weight.shape
    tokens = xs[0].shape[0] * len(xs)
    pw = width // PARTS
    t = tile_of(pw)
    steps = pw // t
    const = lambda j, s: (0, 0)
    moving = lambda j, s: (0, part * steps + j)
    out = lambda j, s: (0, j)
    return pl.pallas_call(
        functools.partial(forward_kernel, n, len(xs)),
        grid_spec=pltpu.PrefetchScalarGridSpec(
            num_scalar_prefetch=1,
            grid=(steps,),
            in_specs=[pl.BlockSpec(x.shape, const) for x in xs]
            + [pl.BlockSpec((depth, t), moving), pl.BlockSpec((depth // BLOCK, t), moving)],
            out_specs=[
                pl.BlockSpec((tokens // 2, t), out),
                pl.BlockSpec((tokens // 2, t), out),
                pl.BlockSpec((tokens, depth), const),
            ],
            scratch_shapes=[
                pltpu.VMEM((tokens, depth), jnp.bfloat16),
                pltpu.VMEM((depth, t), jnp.bfloat16),
            ],
        ),
        out_shape=[
            jax.ShapeDtypeStruct((tokens // 2, pw), jnp.bfloat16),
            jax.ShapeDtypeStruct((tokens // 2, pw), jnp.bfloat16),
            jax.ShapeDtypeStruct((tokens, depth), jnp.bfloat16),
        ],
        compiler_params=pltpu.CompilerParams(vmem_limit_bytes=VMEM_LIMIT),
        cost_estimate=pl.CostEstimate(
            flops=2 * tokens * depth * pw, bytes_accessed=2 * pw * (depth + tokens), transcendentals=0
        ),
        name="forward",
    )(place, *xs, weight, keep)


def start_pieces(n, place_ref, pieces, refs, held, sems):
    steps, tokens, t = held.shape
    tr = tokens // (2 * n)
    z, core = place_ref[0], place_ref[1]
    for (kind, s, flip), ref in zip(pieces, refs):
        if kind == "up":
            origin, valid = z - s, z >= s
        elif kind == "down":
            origin, valid = z + s, z + s < n
        else:
            origin = jnp.where(z >= s, z - s, z + s)
            valid = (z >= s) | (z + s < n)

        @pl.when(valid)
        def _():
            at = pl.multiple_of((2 * origin + (core ^ flip)) * tr, tr)

            @pl.loop(0, steps)
            def _(j):
                pltpu.make_async_copy(
                    ref.at[:, pl.ds(pl.multiple_of(j * t, t), t)],
                    held.at[j, pl.ds(at, tr), :],
                    sems.at[j],
                ).start()


def wait_tile(held, sems, j):
    pltpu.make_async_copy(held.at[j], held.at[j], sems.at[j]).wait()


def input_grad_kernel(n, cols, pieces, first, last, place_ref, *refs):
    np_ = len(pieces)
    piece_refs, refs = refs[:np_], refs[np_:]
    (w_ref, keep_ref), refs = refs[:2], refs[2:]
    if not first:
        before_ref, refs = refs[0], refs[1:]
    n_out = cols if last else 1
    out_refs, (held, wm, acc, sems) = refs[:n_out], refs[n_out:]
    j = pl.program_id(0)

    @pl.when(j == 0)
    def _():
        start_pieces(n, place_ref, pieces, piece_refs, held, sems)
        acc[...] = jnp.zeros_like(acc) if first else before_ref[...]

    masked_tile(w_ref, keep_ref, wm)
    wait_tile(held, sems, j)
    acc[...] += lax.dot_general(
        held[j], wm[...], (((1,), (1,)), ((), ())), preferred_element_type=jnp.float32
    )

    @pl.when(j == pl.num_programs(0) - 1)
    def _():
        if last:
            own = out_refs[0].shape[0]
            for k in range(cols):
                at = pl.multiple_of((place_ref[2] ^ k) * own, own)
                out_refs[k][...] = acc[pl.ds(at, own), :].astype(jnp.bfloat16)
        else:
            out_refs[0][...] = acc[...]


def input_grad_part(place, pieces, arrays, weight, keep, before, part, n, cols, tokens):
    depth, width = weight.shape
    pw = width // PARTS
    t = tile_of(pw)
    steps = pw // t
    first, last = before is None, part == PARTS - 1
    const = lambda j, s: (0, 0)
    moving = lambda j, s: (0, part * steps + j)
    if last:
        out_shape = [jax.ShapeDtypeStruct((tokens // cols, depth), jnp.bfloat16)] * cols
    else:
        out_shape = [jax.ShapeDtypeStruct((tokens, depth), jnp.float32)]
    return pl.pallas_call(
        functools.partial(input_grad_kernel, n, cols, pieces, first, last),
        grid_spec=pltpu.PrefetchScalarGridSpec(
            num_scalar_prefetch=1,
            grid=(steps,),
            in_specs=[pl.BlockSpec(memory_space=pl.ANY) for _ in arrays]
            + [pl.BlockSpec((depth, t), moving), pl.BlockSpec((depth // BLOCK, t), moving)]
            + ([] if first else [pl.BlockSpec((tokens, depth), const)]),
            out_specs=[pl.BlockSpec(o.shape, const) for o in out_shape],
            scratch_shapes=[
                pltpu.VMEM((steps, tokens, t), jnp.bfloat16),
                pltpu.VMEM((depth, t), jnp.bfloat16),
                pltpu.VMEM((tokens, depth), jnp.float32),
                pltpu.SemaphoreType.DMA((steps,)),
            ],
        ),
        out_shape=out_shape,
        compiler_params=pltpu.CompilerParams(vmem_limit_bytes=VMEM_LIMIT),
        cost_estimate=pl.CostEstimate(
            flops=2 * tokens * depth * pw, bytes_accessed=2 * pw * (depth + tokens), transcendentals=0
        ),
        name="input_grad",
    )(place, *arrays, weight, keep, *([] if first else [before]))


def weight_grad_kernel(n, pieces, scale, first, place_ref, *refs):
    np_ = len(pieces)
    piece_refs, refs = refs[:np_], refs[np_:]
    (xt_ref, keep_ref), refs = refs[:2], refs[2:]
    if not first:
        refs = refs[1:]
    out_ref, held, sems = refs
    j = pl.program_id(0)

    @pl.when(j == 0)
    def _():
        start_pieces(n, place_ref, pieces, piece_refs, held, sems)

    wait_tile(held, sems, j)
    for a in range(out_ref.shape[0] // BLOCK):
        rows = slice(a * BLOCK, (a + 1) * BLOCK)
        keep = keep_ref[a : a + 1, :] * scale
        acc = jnp.dot(xt_ref[rows, :], held[j], preferred_element_type=jnp.float32)
        out_ref[rows, :] = (acc * keep).astype(jnp.bfloat16)


def weight_grad_part(place, pieces, arrays, xt, keep, before, part, n, width):
    depth, tokens = xt.shape
    pw = width // PARTS
    t = tile_of(pw)
    steps = pw // t
    first = before is None
    const = lambda j, s: (0, 0)
    moving = lambda j, s: (0, part * steps + j)
    return pl.pallas_call(
        functools.partial(weight_grad_kernel, n, pieces, tokens ** (-0.5), first),
        grid_spec=pltpu.PrefetchScalarGridSpec(
            num_scalar_prefetch=1,
            grid=(steps,),
            in_specs=[pl.BlockSpec(memory_space=pl.ANY) for _ in arrays]
            + [pl.BlockSpec((depth, tokens), const), pl.BlockSpec((depth // BLOCK, t), moving)]
            + ([] if first else [pl.BlockSpec(memory_space=pl.ANY)]),
            out_specs=pl.BlockSpec((depth, t), moving),
            scratch_shapes=[
                pltpu.VMEM((steps, tokens, t), jnp.bfloat16),
                pltpu.SemaphoreType.DMA((steps,)),
            ],
        ),
        out_shape=jax.ShapeDtypeStruct((depth, width), jnp.bfloat16),
        input_output_aliases={} if first else {len(arrays) + 3: 0},
        compiler_params=pltpu.CompilerParams(vmem_limit_bytes=VMEM_LIMIT),
        cost_estimate=pl.CostEstimate(
            flops=2 * tokens * depth * pw, bytes_accessed=2 * pw * (depth + tokens), transcendentals=0
        ),
        name="weight_grad",
    )(place, *arrays, xt, keep, *([] if first else [before]))


def local(n, cols, inputs, weight, mask, cotangent):
    row, col = lax.axis_index("row"), lax.axis_index("col")
    z, core = row // 2, row % 2
    place = jnp.stack([z, core, col]).astype(jnp.int32)
    width = weight.shape[1]
    pw = width // PARTS
    tr = cotangent.shape[0]
    tokens = tr * 2 * n

    line = lambda zs, d: [(2 * i + c, 2 * (i + d) + c) for i in zs if 0 <= i + d < n for c in range(2)]
    swap = lambda v: lax.ppermute(v, "row", [(i, i ^ 1) for i in range(2 * n)])
    across = lambda v, k: lax.ppermute(v, "col", [(i, i ^ k) for i in range(cols)])

    cots = [cotangent[:, p * pw : (p + 1) * pw] for p in range(PARTS)]
    xs = [inputs] + [across(inputs, k) for k in range(1, cols)]
    keep = jnp.repeat(mask.astype(jnp.float32), BLOCK, axis=1)

    pieces = [[] for _ in range(PARTS)]
    for p in range(PARTS):
        pieces[p] += [(("up", 0, 0), cots[p]), (("up", 0, 1), swap(cots[p]))]
    ups, downs = list(cots), list(cots)
    for s in range(1, n):
        for p in range(PARTS):
            ups[p] = lax.ppermute(ups[p], "row", line(range(s - 1, n), 1))
            downs[p] = lax.ppermute(downs[p], "row", line(range(0, n - s + 1), -1))
            if 2 * s < n:
                got = [("up", ups[p]), ("down", downs[p])]
            else:
                got = [("either", jnp.where(z >= s, ups[p], downs[p]))]
            for kind, v in got:
                pieces[p] += [((kind, s, 0), v), ((kind, s, 1), swap(v))]

    f32 = jnp.float32
    outs = []
    whole = None
    for p in range(PARTS):
        mine, other, whole_p = forward(place, xs, weight, keep, p, n)
        whole = whole_p if whole is None else whole
        got = swap(other)

        def term(d, mine=mine, got=got):
            at = jnp.clip(d, 0, n - 1) * tr
            cut = lambda v: lax.dynamic_slice_in_dim(v, at, tr, 0).astype(f32)
            return cut(mine) + cut(got)

        up = down = None
        for s in range(1, n):
            u, v = term(z + n - s), term(z - n + s)
            if up is not None:
                u, v = u + up.astype(f32), v + down.astype(f32)
            up = lax.ppermute(u.astype(jnp.bfloat16), "row", line(range(0, s), 1))
            down = lax.ppermute(v.astype(jnp.bfloat16), "row", line(range(n - s, n), -1))
        outs.append((term(z) + up.astype(f32) + down.astype(f32)).astype(jnp.bfloat16))
    outputs = jnp.concatenate(outs, axis=1)

    xt = whole.T
    acc = wg = None
    for p in range(PARTS):
        kinds = [k for k, _ in pieces[p]]
        arrays = [a for _, a in pieces[p]]
        acc = input_grad_part(place, kinds, arrays, weight, keep, acc, p, n, cols, tokens)
        if p < PARTS - 1:
            acc = acc[0]
        wg = weight_grad_part(place, kinds, arrays, xt, keep, wg, p, n, width)
    total = acc[0].astype(f32)
    for k in range(1, cols):
        total = total + across(acc[k], k).astype(f32)
    return outputs, total.astype(jnp.bfloat16), wg


def solution(mesh):
    n, cols = mesh.shape["row"] // 2, mesh.shape["col"]
    return jax.shard_map(
        functools.partial(local, n, cols),
        mesh=mesh,
        in_specs=(P("col", "row"), P("row", "col"), P("row", "col"), P("row", "col")),
        out_specs=(P("row", "col"), P("col", "row"), P("row", "col")),
        check_vma=False,
    )
```

time: 234 us -> 246 us (1.051)
  the two profiles are of different devices: /device:TPU:1 before, /device:TPU:18 now
where the time goes in v1:
time: 246 us; the launch traced here: 244 us
  waiting for transfers between devices  85.2 us (35%)
  starting transfers between devices  65.9 us (27%)
  Pallas kernels  60.2 us (24%)
  local copies, waits for them, and re-layouts  18.5 us (8%)
  other arithmetic  13 us (5%)
    ppermute x6, waiting for transfers between devices, local(): lax.ppermute(v.astype(jnp.bfloat16), 'row', line(range(n - s, n), -1))  31.2 us
    ppermute x6, waiting for transfers between devices, local(): up = lax.ppermute(u.astype(jnp.bfloat16), 'row', line(range(0, s), 1))  25.5 us
    pallas_call x2, Pallas kernels, input_grad_part(): pl.pallas_call(functools.partial(input_grad_kernel, n, cols, pieces, firs...  23 us
    pallas_call x2, Pallas kernels, forward(): pl.pallas_call(functools.partial(forward_kernel, n, len(xs)), grid_spec=p...  19.2 us
    ppermute x6, starting transfers between devices, local(): ups[p] = lax.ppermute(ups[p], 'row', line(range(s - 1, n), 1))  18.9 us
    ppermute x6, waiting for transfers between devices, local(): ups[p] = lax.ppermute(ups[p], 'row', line(range(s - 1, n), 1))  18.4 us
    pallas_call x2, Pallas kernels, weight_grad_part(): pl.pallas_call(functools.partial(weight_grad_kernel, n, pieces, tokens **...  18 us
    ppermute x6, starting transfers between devices, local(): lax.ppermute(v.astype(jnp.bfloat16), 'row', line(range(n - s, n), -1))  17.9 us
  transfers between devices with their start and end apart: 42, of which 14 were waited for; matrix products, arithmetic and copies ran while one was open for 6% of the time, Pallas kernels for 25%

profile of v1, /device:TPU:18, one launch (start us, length us, event | category | flops | bytes accessed | tf_op | source)
XLA Modules:
  0.0 244.2 jit_solution(1897626575696438453)
XLA Ops:
  0.7 1.6 collective-permute-start.2
  2.7 1.5 collective-permute-start
  5.4 2.4 collective-permute-start.31
  7.8 4.3 %collective-permute-start.29 = (bf16[64,3584]{1,0:T(8,128)(2,1)S(1)}, bf16[64,3584]{1,0:T(8,128)(2,1)}, u32[]{:S(2)}, u32[]{:S(2)}) collective-permute-start(bf16[64,3584]{1,0:T(8,128)(2,1)S(1)} %get-tuple-element.25.refs_0_), channel_id=1, source_target_pairs={{0,8},{4,12},{8,16},{12,20},{16,24},{20,28},{1,9},{5,13},{9,17},{1... | collective-permute-start | bytes 1376264 | tf_op jit(solution)/shard_map/ppermute | solution.py:268
  13.1 1.9 collective-permute-start.20
  16.2 3.5 %collective-permute-start.18 = (bf16[64,3584]{1,0:T(8,128)(2,1)S(1)}, bf16[64,3584]{1,0:T(8,128)(2,1)}, u32[]{:S(2)}, u32[]{:S(2)}) collective-permute-start(bf16[64,3584]{1,0:T(8,128)(2,1)S(1)} %get-tuple-element.26.refs_0_), channel_id=1, source_target_pairs={{0,8},{4,12},{8,16},{12,20},{16,24},{20,28},{1,9},{5,13},{9,17},{1... | collective-permute-start | bytes 1376264 | tf_op jit(solution)/shard_map/ppermute | solution.py:268
  19.7 1.2 collective-permute-done.31.refs_4_
  20.9 2.4 collective-permute-start.34
  23.3 2.7 %collective-permute-start.33 = (bf16[64,3584]{1,0:T(8,128)(2,1)}, bf16[64,3584]{1,0:T(8,128)(2,1)S(1)}, u32[]{:S(2)}, u32[]{:S(2)}) collective-permute-start(bf16[64,3584]{1,0:T(8,128)(2,1)} %collective-permute-done.29.refs_2_), channel_id=1, source_target_pairs={{8,16},{12,20},{16,24},{20,28},{9,17},{13,21},{17,25},{21,29},{10,... | collective-permute-start | bytes 1376264 | tf_op jit(solution)/shard_map/ppermute | solution.py:268
  29.6 9.6 %forward.2 = (bf16[256,3584]{1,0:T(8,128)(2,1)S(1)}, bf16[256,3584]{1,0:T(8,128)(2,1)}, bf16[512,1024]{1,0:T(8,128)(2,1)S(1)}) custom-call(s32[3]{0:T(128)S(1)} %pad_add_fusion.place_ref, bf16[128,1024]{1,0:T(8,128)(2,1)S(1)} %copy-done.25, bf16[128,1024]{1,0:T(8,128)(2,1)S(1)} %copy-done.32, bf16[128,1024]{1,0:T(8,128)(2,1)S(1)} %copy-done.29, ...), custom_call_target="tpu_custom_call" | custom-call | flops 3758096384 | bytes 11010048 | tf_op jit(solution)/shard_map/forward/pallas_call | solution.py:63
  41.0 3.2 %collective-permute-start.23 = (bf16[64,3584]{1,0:T(8,128)(2,1)S(1)}, bf16[64,3584]{1,0:T(8,128)(2,1)S(1)}, u32[]{:S(2)}, u32[]{:S(2)}) collective-permute-start(bf16[64,3584]{1,0:T(8,128)(2,1)S(1)} %collective-permute-done.20.refs_4_), channel_id=1, source_target_pairs={{8,0},{12,4},{16,8},{20,12},{9,1},{13,5},{17,9},{21,13},{10,2},{14... | collective-permute-start | bytes 1376264 | tf_op jit(solution)/shard_map/ppermute | solution.py:269
  44.2 1.9 collective-permute-start.22
  46.2 8.3 %collective-permute-done.23 = bf16[64,3584]{1,0:T(8,128)(2,1)S(1)} collective-permute-done((bf16[64,3584]{1,0:T(8,128)(2,1)S(1)}, bf16[64,3584]{1,0:T(8,128)(2,1)S(1)}, u32[]{:S(2)}, u32[]{:S(2)}) %collective-permute-start.23) | collective-permute-done | bytes 458784 | tf_op jit(solution)/shard_map/ppermute | solution.py:269
  55.2 3.7 %collective-permute-done.22 = bf16[64,3584]{1,0:T(8,128)(2,1)S(1)} collective-permute-done((bf16[64,3584]{1,0:T(8,128)(2,1)}, bf16[64,3584]{1,0:T(8,128)(2,1)S(1)}, u32[]{:S(2)}, u32[]{:S(2)}) %collective-permute-start.22) | collective-permute-done | bytes 458784 | tf_op jit(solution)/shard_map/ppermute | solution.py:268
  58.9 2.2 collective-permute-start.36
  62.6 8.0 %collective-permute-done.36 = bf16[64,3584]{1,0:T(8,128)(2,1)S(1)} collective-permute-done((bf16[64,3584]{1,0:T(8,128)(2,1)S(1)}, bf16[64,3584]{1,0:T(8,128)(2,1)S(1)}, u32[]{:S(2)}, u32[]{:S(2)}) %collective-permute-start.36) | collective-permute-done | bytes 458784 | tf_op jit(solution)/shard_map/ppermute | solution.py:268
  70.6 4.4 %collective-permute-start.25 = (bf16[64,3584]{1,0:T(8,128)(2,1)S(1)}, bf16[64,3584]{1,0:T(8,128)(2,1)S(1)}, u32[]{:S(2)}, u32[]{:S(2)}) collective-permute-start(bf16[64,3584]{1,0:T(8,128)(2,1)S(1)} %collective-permute-done.22), channel_id=1, source_target_pairs={{16,24},{20,28},{17,25},{21,29},{18,26},{22,30},{19,27},{23,31}} | collective-permute-start | bytes 1376264 | tf_op jit(solution)/shard_map/ppermute | solution.py:268
  77.0 6.7 %collective-permute-done.25 = bf16[64,3584]{1,0:T(8,128)(2,1)S(1)} collective-permute-done((bf16[64,3584]{1,0:T(8,128)(2,1)S(1)}, bf16[64,3584]{1,0:T(8,128)(2,1)S(1)}, u32[]{:S(2)}, u32[]{:S(2)}) %collective-permute-start.25) | collective-permute-done | bytes 458784 | tf_op jit(solution)/shard_map/ppermute | solution.py:268
  86.4 9.6 %forward.3 = (bf16[256,3584]{1,0:T(8,128)(2,1)S(1)}, bf16[256,3584]{1,0:T(8,128)(2,1)S(1)}, bf16[512,1024]{1,0:T(8,128)(2,1)}) custom-call(s32[3]{0:T(128)S(1)} %pad_add_fusion.place_ref, bf16[128,1024]{1,0:T(8,128)(2,1)S(1)} %copy-done.25, bf16[128,1024]{1,0:T(8,128)(2,1)S(1)} %copy-done.33, bf16[128,1024]{1,0:T(8,128)(2,1)S(1)} %copy-done.30, ...), custom_call_target="tpu_custom_call" | custom-call | flops 3758096384 | bytes 11010048 | tf_op jit(solution)/shard_map/forward/pallas_call | solution.py:63
  96.0 1.3 copy-done
  97.3 1.3 copy-done.35
  98.6 1.5 copy.9
  106.5 11.6 %input_grad.2.refs_12_ = f32[512,1024]{1,0:T(8,128)} custom-call(s32[3]{0:T(128)S(1)} %pad_add_fusion.place_ref, bf16[64,3584]{1,0:T(8,128)(2,1)S(1)} %copy-done.5, bf16[64,3584]{1,0:T(8,128)(2,1)S(1)} %copy-done.16, bf16[64,3584]{1,0:T(8,128)(2,1)} %collective-permute-done.29.refs_2_, bf16[64,3584]{1,0:T(8,128)(2,1)S(1)} %copy-done.20, ...), custom_call_target="tpu_custom_call" | custom-call | flops 3758096384 | bytes 11010048 | tf_op jit(solution)/shard_map/input_grad/pallas_call | solution.py:167
  118.2 11.4 %input_grad.3 = (bf16[128,1024]{1,0:T(8,128)(2,1)S(1)}, bf16[128,1024]{1,0:T(8,128)(2,1)S(1)}, bf16[128,1024]{1,0:T(8,128)(2,1)S(1)}, bf16[128,1024]{1,0:T(8,128)(2,1)S(1)}) custom-call(s32[3]{0:T(128)S(1)} %pad_add_fusion.place_ref, bf16[64,3584]{1,0:T(8,128)(2,1)S(1)} %copy-done.3, bf16[64,3584]{1,0:T(8,128)(2,1)S(1)} %copy-done.12, ...), custom_call_target="tpu_custom_call" | custom-call | flops 3758096384 | bytes 11010048 | tf_op jit(solution)/shard_map/input_grad/pallas_call | solution.py:167
  130.2 1.5 collective-permute-start.40
  131.7 1.4 collective-permute-start.41
  133.2 8.8 %weight_grad.2.refs_12_ = bf16[1024,7168]{1,0:T(8,128)(2,1)} custom-call(s32[3]{0:T(128)S(1)} %pad_add_fusion.place_ref, bf16[64,3584]{1,0:T(8,128)(2,1)S(1)} %copy-done.5, bf16[64,3584]{1,0:T(8,128)(2,1)S(1)} %copy-done.16, bf16[64,3584]{1,0:T(8,128)(2,1)} %collective-permute-done.29.refs_2_, bf16[64,3584]{1,0:T(8,128)(2,1)S(1)} %copy-done.21, ...), custom_call_target="tpu_custom_call" | custom-call | flops 3758096384 | bytes 11010048 | tf_op jit(solution)/shard_map/weight_grad/pallas_call | solution.py:221
  142.0 9.2 %weight_grad.3 = bf16[1024,7168]{1,0:T(8,128)(2,1)} custom-call(s32[3]{0:T(128)S(1)} %pad_add_fusion.place_ref, bf16[64,3584]{1,0:T(8,128)(2,1)S(1)} %copy-done.3, bf16[64,3584]{1,0:T(8,128)(2,1)S(1)} %copy-done.12, bf16[64,3584]{1,0:T(8,128)(2,1)} %collective-permute-done.18.refs_2_, ...), custom_call_target="tpu_custom_call", output_to_operand_aliasing={{}: (13, {})} | custom-call | flops 3758096384 | bytes 11010048 | tf_op jit(solution)/shard_map/weight_grad/pallas_call | solution.py:221
  156.0 1.3 collective-permute-start.5
  157.5 1.3 collective-permute-start.12
  158.8 21.3 %collective-permute-done.5 = bf16[64,3584]{1,0:T(8,128)(2,1)S(1)} collective-permute-done((bf16[64,3584]{1,0:T(8,128)(2,1)S(1)}, bf16[64,3584]{1,0:T(8,128)(2,1)S(1)}, u32[]{:S(2)}, u32[]{:S(2)}) %collective-permute-start.5) | collective-permute-done | bytes 458784 | tf_op jit(solution)/shard_map/ppermute | solution.py:295
  180.1 1.4 add_convert_fusion.11
  181.5 1.9 collective-permute-start.6
  183.4 1.3 collective-permute-start.7
  184.7 4.2 %collective-permute-done.12 = bf16[64,3584]{1,0:T(8,128)(2,1)S(1)} collective-permute-done((bf16[64,3584]{1,0:T(8,128)(2,1)S(1)}, bf16[64,3584]{1,0:T(8,128)(2,1)S(1)}, u32[]{:S(2)}, u32[]{:S(2)}) %collective-permute-start.12) | collective-permute-done | bytes 458784 | tf_op jit(solution)/shard_map/ppermute | solution.py:295
  189.2 1.9 collective-permute-start.13
  191.2 1.3 collective-permute-start.14
  192.5 1.8 collective-permute-done.7
  195.4 8.2 %collective-permute-start.8 = (bf16[64,3584]{1,0:T(8,128)(2,1)S(1)}, bf16[64,3584]{1,0:T(8,128)(2,1)S(1)}, u32[]{:S(2)}, u32[]{:S(2)}) collective-permute-start(bf16[64,3584]{1,0:T(8,128)(2,1)S(1)} %add_convert_fusion.9), channel_id=1, source_target_pairs={{16,8},{20,12},{24,16},{28,20},{17,9},{21,13},{25,17},{29,21},{18,... | collective-permute-start | bytes 1376264 | tf_op jit(solution)/shard_map/ppermute | solution.py:296
  203.6 2.9 %collective-permute-done.14 = bf16[64,3584]{1,0:T(8,128)(2,1)S(1)} collective-permute-done((bf16[64,3584]{1,0:T(8,128)(2,1)S(1)}, bf16[64,3584]{1,0:T(8,128)(2,1)S(1)}, u32[]{:S(2)}, u32[]{:S(2)}) %collective-permute-start.14) | collective-permute-done | bytes 458784 | tf_op jit(solution)/shard_map/ppermute | solution.py:296
  206.7 1.9 collective-permute-start.15
  208.6 7.7 %collective-permute-done.8 = bf16[64,3584]{1,0:T(8,128)(2,1)S(1)} collective-permute-done((bf16[64,3584]{1,0:T(8,128)(2,1)S(1)}, bf16[64,3584]{1,0:T(8,128)(2,1)S(1)}, u32[]{:S(2)}, u32[]{:S(2)}) %collective-permute-start.8) | collective-permute-done | bytes 458784 | tf_op jit(solution)/shard_map/ppermute | solution.py:296
  217.5 2.6 %collective-permute-start.9 = (bf16[64,3584]{1,0:T(8,128)(2,1)S(1)}, bf16[64,3584]{1,0:T(8,128)(2,1)S(1)}, u32[]{:S(2)}, u32[]{:S(2)}) collective-permute-start(bf16[64,3584]{1,0:T(8,128)(2,1)S(1)} %add_convert_fusion.8), channel_id=1, source_target_pairs={{8,0},{12,4},{16,8},{20,12},{24,16},{28,20},{9,1},{13,5},{17,9},{2... | collective-permute-start | bytes 1376264 | tf_op jit(solution)/shard_map/ppermute | solution.py:296
  220.2 6.0 %collective-permute-done.15 = bf16[64,3584]{1,0:T(8,128)(2,1)S(1)} collective-permute-done((bf16[64,3584]{1,0:T(8,128)(2,1)S(1)}, bf16[64,3584]{1,0:T(8,128)(2,1)S(1)}, u32[]{:S(2)}, u32[]{:S(2)}) %collective-permute-start.15) | collective-permute-done | bytes 458784 | tf_op jit(solution)/shard_map/ppermute | solution.py:296
  226.4 2.6 %collective-permute-start.16 = (bf16[64,3584]{1,0:T(8,128)(2,1)S(1)}, bf16[64,3584]{1,0:T(8,128)(2,1)S(1)}, u32[]{:S(2)}, u32[]{:S(2)}) collective-permute-start(bf16[64,3584]{1,0:T(8,128)(2,1)S(1)} %add_convert_fusion.1), channel_id=1, source_target_pairs={{8,0},{12,4},{16,8},{20,12},{24,16},{28,20},{9,1},{13,5},{17,9},{2... | collective-permute-start | bytes 1376264 | tf_op jit(solution)/shard_map/ppermute | solution.py:296
  229.0 7.0 %collective-permute-done.9 = bf16[64,3584]{1,0:T(8,128)(2,1)S(1)} collective-permute-done((bf16[64,3584]{1,0:T(8,128)(2,1)S(1)}, bf16[64,3584]{1,0:T(8,128)(2,1)S(1)}, u32[]{:S(2)}, u32[]{:S(2)}) %collective-permute-start.9) | collective-permute-done | bytes 458784 | tf_op jit(solution)/shard_map/ppermute | solution.py:296
  236.0 1.2 add_convert_fusion.7
  237.3 5.7 %collective-permute-done.16 = bf16[64,3584]{1,0:T(8,128)(2,1)S(1)} collective-permute-done((bf16[64,3584]{1,0:T(8,128)(2,1)S(1)}, bf16[64,3584]{1,0:T(8,128)(2,1)S(1)}, u32[]{:S(2)}, u32[]{:S(2)}) %collective-permute-start.16) | collective-permute-done | bytes 458784 | tf_op jit(solution)/shard_map/ppermute | solution.py:296
  (140 shorter events, 32.1 us)
Async XLA Ops:
  0.7 11.7 %collective-permute-start.2 = (bf16[128,1024]{1,0:T(8,128)(2,1)}, bf16[128,1024]{1,0:T(8,128)(2,1)S(1)}, u32[]{:S(2)}, u32[]{:S(2)}) collective-permute-start(bf16[128,1024]{1,0:T(8,128)(2,1)} %refs_0_.3), channel_id=1, source_target_pairs={{0,3},{1,2},{2,1},{3,0},{4,7},{5,6},{6,5},{7,4},{8,11},{9,10},{10,... | collective-permute-start | bytes 786440 | tf_op jit(solution)/shard_map/ppermute | solution.py:256
  2.2 13.3 %collective-permute-start.1 = (bf16[128,1024]{1,0:T(8,128)(2,1)}, bf16[128,1024]{1,0:T(8,128)(2,1)S(1)}, u32[]{:S(2)}, u32[]{:S(2)}) collective-permute-start(bf16[128,1024]{1,0:T(8,128)(2,1)} %refs_0_.3), channel_id=1, source_target_pairs={{0,2},{1,3},{2,0},{3,1},{4,6},{5,7},{6,4},{7,5},{8,10},{9,11},{10,... | collective-permute-start | bytes 786440 | tf_op jit(solution)/shard_map/ppermute | solution.py:256
  2.7 23.3 %collective-permute-start = (bf16[128,1024]{1,0:T(8,128)(2,1)}, bf16[128,1024]{1,0:T(8,128)(2,1)S(1)}, u32[]{:S(2)}, u32[]{:S(2)}) collective-permute-start(bf16[128,1024]{1,0:T(8,128)(2,1)} %refs_0_.3), channel_id=1, source_target_pairs={{0,1},{1,0},{2,3},{3,2},{4,5},{5,4},{6,7},{7,6},{8,9},{9,8},{10,11... | collective-permute-start | bytes 786440 | tf_op jit(solution)/shard_map/ppermute | solution.py:256
  5.4 33.8 %copy-start.4 = (bf16[64,3584]{1,0:T(8,128)(2,1)}, bf16[64,3584]{1,0:T(8,128)(2,1)S(1)}, u32[]{:S(2)}) copy-start(bf16[64,3584]{1,0:T(8,128)(2,1)S(1)} %get-tuple-element.25.refs_0_) | copy-start | bytes 1376260
  5.4 34.9 %copy-start.2 = (bf16[64,3584]{1,0:T(8,128)(2,1)}, bf16[64,3584]{1,0:T(8,128)(2,1)S(1)}, u32[]{:S(2)}) copy-start(bf16[64,3584]{1,0:T(8,128)(2,1)S(1)} %get-tuple-element.26.refs_0_) | copy-start | bytes 1376260
  5.4 15.5 %collective-permute-start.31 = (bf16[64,3584]{1,0:T(8,128)(2,1)S(1)}, bf16[64,3584]{1,0:T(8,128)(2,1)}, u32[]{:S(2)}, u32[]{:S(2)}) collective-permute-start(bf16[64,3584]{1,0:T(8,128)(2,1)S(1)} %get-tuple-element.25.refs_0_), channel_id=1, source_target_pairs={{8,0},{12,4},{16,8},{20,12},{24,16},{28,20},{9,1},{13,5},{17,9},{2... | collective-permute-start | bytes 1376264 | tf_op jit(solution)/shard_map/ppermute | solution.py:269
  7.8 15.5 %collective-permute-start.29 = (bf16[64,3584]{1,0:T(8,128)(2,1)S(1)}, bf16[64,3584]{1,0:T(8,128)(2,1)}, u32[]{:S(2)}, u32[]{:S(2)}) collective-permute-start(bf16[64,3584]{1,0:T(8,128)(2,1)S(1)} %get-tuple-element.25.refs_0_), channel_id=1, source_target_pairs={{0,8},{4,12},{8,16},{12,20},{16,24},{20,28},{1,9},{5,13},{9,17},{1... | collective-permute-start | bytes 1376264 | tf_op jit(solution)/shard_map/ppermute | solution.py:268
  13.1 27.2 %collective-permute-start.20 = (bf16[64,3584]{1,0:T(8,128)(2,1)S(1)}, bf16[64,3584]{1,0:T(8,128)(2,1)S(1)}, u32[]{:S(2)}, u32[]{:S(2)}) collective-permute-start(bf16[64,3584]{1,0:T(8,128)(2,1)S(1)} %get-tuple-element.26.refs_0_), channel_id=1, source_target_pairs={{8,0},{12,4},{16,8},{20,12},{24,16},{28,20},{9,1},{13,5},{17,9},{2... | collective-permute-start | bytes 1376264 | tf_op jit(solution)/shard_map/ppermute | solution.py:269
  16.2 24.7 %collective-permute-start.18 = (bf16[64,3584]{1,0:T(8,128)(2,1)S(1)}, bf16[64,3584]{1,0:T(8,128)(2,1)}, u32[]{:S(2)}, u32[]{:S(2)}) collective-permute-start(bf16[64,3584]{1,0:T(8,128)(2,1)S(1)} %get-tuple-element.26.refs_0_), channel_id=1, source_target_pairs={{0,8},{4,12},{8,16},{12,20},{16,24},{20,28},{1,9},{5,13},{9,17},{1... | collective-permute-start | bytes 1376264 | tf_op jit(solution)/shard_map/ppermute | solution.py:268
  20.9 20.0 %collective-permute-start.34 = (bf16[64,3584]{1,0:T(8,128)(2,1)}, bf16[64,3584]{1,0:T(8,128)(2,1)S(1)}, u32[]{:S(2)}, u32[]{:S(2)}) collective-permute-start(bf16[64,3584]{1,0:T(8,128)(2,1)} %collective-permute-done.31.refs_4_), channel_id=1, source_target_pairs={{8,0},{12,4},{16,8},{20,12},{9,1},{13,5},{17,9},{21,13},{10,2},{14... | collective-permute-start | bytes 1376264 | tf_op jit(solution)/shard_map/ppermute | solution.py:269
  23.3 20.9 %collective-permute-start.33 = (bf16[64,3584]{1,0:T(8,128)(2,1)}, bf16[64,3584]{1,0:T(8,128)(2,1)S(1)}, u32[]{:S(2)}, u32[]{:S(2)}) collective-permute-start(bf16[64,3584]{1,0:T(8,128)(2,1)} %collective-permute-done.29.refs_2_), channel_id=1, source_target_pairs={{8,16},{12,20},{16,24},{20,28},{9,17},{13,21},{17,25},{21,29},{10,... | collective-permute-start | bytes 1376264 | tf_op jit(solution)/shard_map/ppermute | solution.py:268
  26.8 49.1 %collective-permute-start.28 = (bf16[64,3584]{1,0:T(8,128)(2,1)S(1)}, bf16[64,3584]{1,0:T(8,128)(2,1)S(1)}, u32[]{:S(2)}, u32[]{:S(2)}) collective-permute-start(bf16[64,3584]{1,0:T(8,128)(2,1)S(1)} %get-tuple-element.25.refs_0_), channel_id=1, source_target_pairs={{0,4},{4,0},{8,12},{12,8},{16,20},{20,16},{24,28},{28,24},{1,5},{5... | collective-permute-start | bytes 1376264 | tf_op jit(solution)/shard_map/ppermute | solution.py:255
  40.3 36.1 %copy-start.9 = (bf16[64,3584]{1,0:T(8,128)(2,1)}, bf16[64,3584]{1,0:T(8,128)(2,1)S(1)}, u32[]{:S(2)}) copy-start(bf16[64,3584]{1,0:T(8,128)(2,1)S(1)} %collective-permute-done.20.refs_4_) | copy-start | bytes 1376260
  40.3 35.6 %collective-permute-start.17 = (bf16[64,3584]{1,0:T(8,128)(2,1)S(1)}, bf16[64,3584]{1,0:T(8,128)(2,1)S(1)}, u32[]{:S(2)}, u32[]{:S(2)}) collective-permute-start(bf16[64,3584]{1,0:T(8,128)(2,1)S(1)} %get-tuple-element.26.refs_0_), channel_id=1, source_target_pairs={{0,4},{4,0},{8,12},{12,8},{16,20},{20,16},{24,28},{28,24},{1,5},{5... | collective-permute-start | bytes 1376264 | tf_op jit(solution)/shard_map/ppermute | solution.py:255
  40.9 35.5 %collective-permute-start.32 = (bf16[64,3584]{1,0:T(8,128)(2,1)}, bf16[64,3584]{1,0:T(8,128)(2,1)S(1)}, u32[]{:S(2)}, u32[]{:S(2)}) collective-permute-start(bf16[64,3584]{1,0:T(8,128)(2,1)} %collective-permute-done.31.refs_4_), channel_id=1, source_target_pairs={{0,4},{4,0},{8,12},{12,8},{16,20},{20,16},{24,28},{28,24},{1,5},{5... | collective-permute-start | bytes 1376264 | tf_op jit(solution)/shard_map/ppermute | solution.py:255
  41.0 13.6 %collective-permute-start.23 = (bf16[64,3584]{1,0:T(8,128)(2,1)S(1)}, bf16[64,3584]{1,0:T(8,128)(2,1)S(1)}, u32[]{:S(2)}, u32[]{:S(2)}) collective-permute-start(bf16[64,3584]{1,0:T(8,128)(2,1)S(1)} %collective-permute-done.20.refs_4_), channel_id=1, source_target_pairs={{8,0},{12,4},{16,8},{20,12},{9,1},{13,5},{17,9},{21,13},{10,2},{14... | collective-permute-start | bytes 1376264 | tf_op jit(solution)/shard_map/ppermute | solution.py:269
  44.2 14.7 %collective-permute-start.22 = (bf16[64,3584]{1,0:T(8,128)(2,1)}, bf16[64,3584]{1,0:T(8,128)(2,1)S(1)}, u32[]{:S(2)}, u32[]{:S(2)}) collective-permute-start(bf16[64,3584]{1,0:T(8,128)(2,1)} %collective-permute-done.18.refs_2_), channel_id=1, source_target_pairs={{8,16},{12,20},{16,24},{20,28},{9,17},{13,21},{17,25},{21,29},{10,... | collective-permute-start | bytes 1376264 | tf_op jit(solution)/shard_map/ppermute | solution.py:268
  46.2 38.4 %copy-start.6 = (bf16[64,3584]{1,0:T(8,128)(2,1)}, bf16[64,3584]{1,0:T(8,128)(2,1)S(1)}, u32[]{:S(2)}) copy-start(bf16[64,3584]{1,0:T(8,128)(2,1)S(1)} %broadcast_select_fusion.2.refs_6_) | copy-start | bytes 1376260
  46.2 40.3 %copy-start.30 = (bf16[128,1024]{1,0:T(8,128)(2,1)S(1)}, bf16[128,1024]{1,0:T(8,128)(2,1)}, u32[]{:S(2)}) copy-start(bf16[128,1024]{1,0:T(8,128)(2,1)} %copy-done.28) | copy-start | bytes 786436
  46.2 40.2 %copy-start.33 = (bf16[128,1024]{1,0:T(8,128)(2,1)S(1)}, bf16[128,1024]{1,0:T(8,128)(2,1)}, u32[]{:S(2)}) copy-start(bf16[128,1024]{1,0:T(8,128)(2,1)} %copy-done.31) | copy-start | bytes 786436
  54.5 7.4 %collective-permute-start.37 = (bf16[64,3584]{1,0:T(8,128)(2,1)S(1)}, bf16[64,3584]{1,0:T(8,128)(2,1)S(1)}, u32[]{:S(2)}, u32[]{:S(2)}) collective-permute-start(bf16[64,3584]{1,0:T(8,128)(2,1)S(1)} %collective-permute-done.34), channel_id=1, source_target_pairs={{8,0},{12,4},{9,1},{13,5},{10,2},{14,6},{11,3},{15,7}} | collective-permute-start | bytes 1376264 | tf_op jit(solution)/shard_map/ppermute | solution.py:269
  58.9 11.8 %collective-permute-start.36 = (bf16[64,3584]{1,0:T(8,128)(2,1)S(1)}, bf16[64,3584]{1,0:T(8,128)(2,1)S(1)}, u32[]{:S(2)}, u32[]{:S(2)}) collective-permute-start(bf16[64,3584]{1,0:T(8,128)(2,1)S(1)} %collective-permute-done.33), channel_id=1, source_target_pairs={{16,24},{20,28},{17,25},{21,29},{18,26},{22,30},{19,27},{23,31}} | collective-permute-start | bytes 1376264 | tf_op jit(solution)/shard_map/ppermute | solution.py:268
  61.9 14.6 %collective-permute-start.26 = (bf16[64,3584]{1,0:T(8,128)(2,1)S(1)}, bf16[64,3584]{1,0:T(8,128)(2,1)S(1)}, u32[]{:S(2)}, u32[]{:S(2)}) collective-permute-start(bf16[64,3584]{1,0:T(8,128)(2,1)S(1)} %collective-permute-done.23), channel_id=1, source_target_pairs={{8,0},{12,4},{9,1},{13,5},{10,2},{14,6},{11,3},{15,7}} | collective-permute-start | bytes 1376264 | tf_op jit(solution)/shard_map/ppermute | solution.py:269
  70.6 13.1 %collective-permute-start.25 = (bf16[64,3584]{1,0:T(8,128)(2,1)S(1)}, bf16[64,3584]{1,0:T(8,128)(2,1)S(1)}, u32[]{:S(2)}, u32[]{:S(2)}) collective-permute-start(bf16[64,3584]{1,0:T(8,128)(2,1)S(1)} %collective-permute-done.22), channel_id=1, source_target_pairs={{16,24},{20,28},{17,25},{21,29},{18,26},{22,30},{19,27},{23,31}} | collective-permute-start | bytes 1376264 | tf_op jit(solution)/shard_map/ppermute | solution.py:268
  75.9 75.3 %collective-permute-start.3 = (bf16[256,3584]{1,0:T(8,128)(2,1)}, bf16[256,3584]{1,0:T(8,128)(2,1)}, u32[]{:S(2)}, u32[]{:S(2)}) collective-permute-start(bf16[256,3584]{1,0:T(8,128)(2,1)} %get-tuple-element.13), channel_id=1, source_target_pairs={{0,4},{4,0},{8,12},{12,8},{16,20},{20,16},{24,28},{28,24},{1,5},{5... | collective-permute-start | bytes 5505032 | tf_op jit(solution)/shard_map/ppermute | solution.py:255
  75.9 8.6 %collective-permute-start.30 = (bf16[64,3584]{1,0:T(8,128)(2,1)}, bf16[64,3584]{1,0:T(8,128)(2,1)S(1)}, u32[]{:S(2)}, u32[]{:S(2)}) collective-permute-start(bf16[64,3584]{1,0:T(8,128)(2,1)} %collective-permute-done.29.refs_2_), channel_id=1, source_target_pairs={{0,4},{4,0},{8,12},{12,8},{16,20},{20,16},{24,28},{28,24},{1,5},{5... | collective-permute-start | bytes 1376264 | tf_op jit(solution)/shard_map/ppermute | solution.py:255
  76.4 8.7 %collective-permute-start.21 = (bf16[64,3584]{1,0:T(8,128)(2,1)S(1)}, bf16[64,3584]{1,0:T(8,128)(2,1)S(1)}, u32[]{:S(2)}, u32[]{:S(2)}) collective-permute-start(bf16[64,3584]{1,0:T(8,128)(2,1)S(1)} %collective-permute-done.20.refs_4_), channel_id=1, source_target_pairs={{0,4},{4,0},{8,12},{12,8},{16,20},{20,16},{24,28},{28,24},{1,5},{5... | collective-permute-start | bytes 1376264 | tf_op jit(solution)/shard_map/ppermute | solution.py:255
  76.6 8.7 %collective-permute-start.35 = (bf16[64,3584]{1,0:T(8,128)(2,1)S(1)}, bf16[64,3584]{1,0:T(8,128)(2,1)S(1)}, u32[]{:S(2)}, u32[]{:S(2)}) collective-permute-start(bf16[64,3584]{1,0:T(8,128)(2,1)S(1)} %broadcast_select_fusion.2.refs_6_), channel_id=1, source_target_pairs={{0,4},{4,0},{8,12},{12,8},{16,20},{20,16},{24,28},{28,24},{1,5},{5... | collective-permute-start | bytes 1376264 | tf_op jit(solution)/shard_map/ppermute | solution.py:255
  83.7 16.4 %collective-permute-start.38 = (bf16[64,3584]{1,0:T(8,128)(2,1)}, bf16[64,3584]{1,0:T(8,128)(2,1)}, u32[]{:S(2)}, u32[]{:S(2)}) collective-permute-start(bf16[64,3584]{1,0:T(8,128)(2,1)} %broadcast_select_fusion.refs_8_), channel_id=1, source_target_pairs={{0,4},{4,0},{8,12},{12,8},{16,20},{20,16},{24,28},{28,24},{1,5},{5... | collective-permute-start | bytes 1376264 | tf_op jit(solution)/shard_map/ppermute | solution.py:255
  84.5 33.6 %collective-permute-start.19 = (bf16[64,3584]{1,0:T(8,128)(2,1)}, bf16[64,3584]{1,0:T(8,128)(2,1)}, u32[]{:S(2)}, u32[]{:S(2)}) collective-permute-start(bf16[64,3584]{1,0:T(8,128)(2,1)} %collective-permute-done.18.refs_2_), channel_id=1, source_target_pairs={{0,4},{4,0},{8,12},{12,8},{16,20},{20,16},{24,28},{28,24},{1,5},{5... | collective-permute-start | bytes 1376264 | tf_op jit(solution)/shard_map/ppermute | solution.py:255
  85.1 33.0 %collective-permute-start.24 = (bf16[64,3584]{1,0:T(8,128)(2,1)}, bf16[64,3584]{1,0:T(8,128)(2,1)}, u32[]{:S(2)}, u32[]{:S(2)}) collective-permute-start(bf16[64,3584]{1,0:T(8,128)(2,1)} %broadcast_select_fusion.3.refs_6_), channel_id=1, source_target_pairs={{0,4},{4,0},{8,12},{12,8},{16,20},{20,16},{24,28},{28,24},{1,5},{5... | collective-permute-start | bytes 1376264 | tf_op jit(solution)/shard_map/ppermute | solution.py:255
  86.0 32.1 %collective-permute-start.27 = (bf16[64,3584]{1,0:T(8,128)(2,1)}, bf16[64,3584]{1,0:T(8,128)(2,1)}, u32[]{:S(2)}, u32[]{:S(2)}) collective-permute-start(bf16[64,3584]{1,0:T(8,128)(2,1)} %broadcast_select_fusion.1.refs_8_), channel_id=1, source_target_pairs={{0,4},{4,0},{8,12},{12,8},{16,20},{20,16},{24,28},{28,24},{1,5},{5... | collective-permute-start | bytes 1376264 | tf_op jit(solution)/shard_map/ppermute | solution.py:255
  100.1 52.9 %collective-permute-start.10 = (bf16[256,3584]{1,0:T(8,128)(2,1)}, bf16[256,3584]{1,0:T(8,128)(2,1)S(1)}, u32[]{:S(2)}, u32[]{:S(2)}) collective-permute-start(bf16[256,3584]{1,0:T(8,128)(2,1)} %copy-done.35), channel_id=1, source_target_pairs={{0,4},{4,0},{8,12},{12,8},{16,20},{20,16},{24,28},{28,24},{1,5},{5... | collective-permute-start | bytes 5505032 | tf_op jit(solution)/shard_map/ppermute | solution.py:255
  129.6 24.3 %collective-permute-start.39 = (bf16[128,1024]{1,0:T(8,128)(2,1)S(1)}, bf16[128,1024]{1,0:T(8,128)(2,1)S(1)}, u32[]{:S(2)}, u32[]{:S(2)}) collective-permute-start(bf16[128,1024]{1,0:T(8,128)(2,1)S(1)} %get-tuple-element.17), channel_id=1, source_target_pairs={{0,1},{1,0},{2,3},{3,2},{4,5},{5,4},{6,7},{7,6},{8,9},{9,8},{10,11... | collective-permute-start | bytes 786440 | tf_op jit(solution)/shard_map/ppermute | solution.py:256
  130.2 23.7 %collective-permute-start.40 = (bf16[128,1024]{1,0:T(8,128)(2,1)S(1)}, bf16[128,1024]{1,0:T(8,128)(2,1)S(1)}, u32[]{:S(2)}, u32[]{:S(2)}) collective-permute-start(bf16[128,1024]{1,0:T(8,128)(2,1)S(1)} %get-tuple-element.18), channel_id=1, source_target_pairs={{0,2},{1,3},{2,0},{3,1},{4,6},{5,7},{6,4},{7,5},{8,10},{9,11},{10,... | collective-permute-start | bytes 786440 | tf_op jit(solution)/shard_map/ppermute | solution.py:256
  131.7 22.2 %collective-permute-start.41 = (bf16[128,1024]{1,0:T(8,128)(2,1)S(1)}, bf16[128,1024]{1,0:T(8,128)(2,1)S(1)}, u32[]{:S(2)}, u32[]{:S(2)}) collective-permute-start(bf16[128,1024]{1,0:T(8,128)(2,1)S(1)} %get-tuple-element.19), channel_id=1, source_target_pairs={{0,3},{1,2},{2,1},{3,0},{4,7},{5,6},{6,5},{7,4},{8,11},{9,10},{10,... | collective-permute-start | bytes 786440 | tf_op jit(solution)/shard_map/ppermute | solution.py:256
  152.4 2.4 %collective-permute-start.4 = (bf16[64,3584]{1,0:T(8,128)(2,1)S(1)}, bf16[64,3584]{1,0:T(8,128)(2,1)S(1)}, u32[]{:S(2)}, u32[]{:S(2)}) collective-permute-start(bf16[64,3584]{1,0:T(8,128)(2,1)S(1)} %add_convert_fusion.13), channel_id=1, source_target_pairs={{0,8},{4,12},{1,9},{5,13},{2,10},{6,14},{3,11},{7,15}} | collective-permute-start | bytes 1376264 | tf_op jit(solution)/shard_map/ppermute | solution.py:295
  153.2 4.1 %collective-permute-start.11 = (bf16[64,3584]{1,0:T(8,128)(2,1)S(1)}, bf16[64,3584]{1,0:T(8,128)(2,1)S(1)}, u32[]{:S(2)}, u32[]{:S(2)}) collective-permute-start(bf16[64,3584]{1,0:T(8,128)(2,1)S(1)} %add_convert_fusion.6), channel_id=1, source_target_pairs={{0,8},{4,12},{1,9},{5,13},{2,10},{6,14},{3,11},{7,15}} | collective-permute-start | bytes 1376264 | tf_op jit(solution)/shard_map/ppermute | solution.py:295
  156.0 24.1 %collective-permute-start.5 = (bf16[64,3584]{1,0:T(8,128)(2,1)S(1)}, bf16[64,3584]{1,0:T(8,128)(2,1)S(1)}, u32[]{:S(2)}, u32[]{:S(2)}) collective-permute-start(bf16[64,3584]{1,0:T(8,128)(2,1)S(1)} %add_convert_fusion.12), channel_id=1, source_target_pairs={{0,8},{4,12},{8,16},{12,20},{1,9},{5,13},{9,17},{13,21},{2,10},{6,... | collective-permute-start | bytes 1376264 | tf_op jit(solution)/shard_map/ppermute | solution.py:295
  157.5 31.5 %collective-permute-start.12 = (bf16[64,3584]{1,0:T(8,128)(2,1)S(1)}, bf16[64,3584]{1,0:T(8,128)(2,1)S(1)}, u32[]{:S(2)}, u32[]{:S(2)}) collective-permute-start(bf16[64,3584]{1,0:T(8,128)(2,1)S(1)} %add_convert_fusion.5), channel_id=1, source_target_pairs={{0,8},{4,12},{8,16},{12,20},{1,9},{5,13},{9,17},{13,21},{2,10},{6,... | collective-permute-start | bytes 1376264 | tf_op jit(solution)/shard_map/ppermute | solution.py:295
  181.5 47.5 %collective-permute-start.6 = (bf16[64,3584]{1,0:T(8,128)(2,1)S(1)}, bf16[64,3584]{1,0:T(8,128)(2,1)S(1)}, u32[]{:S(2)}, u32[]{:S(2)}) collective-permute-start(bf16[64,3584]{1,0:T(8,128)(2,1)S(1)} %get-tuple-element.21), channel_id=1, source_target_pairs={{0,8},{4,12},{8,16},{12,20},{16,24},{20,28},{1,9},{5,13},{9,17},{1... | collective-permute-start | bytes 1376264 | tf_op jit(solution)/shard_map/ppermute | solution.py:295
  183.4 10.8 %collective-permute-start.7 = (bf16[64,3584]{1,0:T(8,128)(2,1)S(1)}, bf16[64,3584]{1,0:T(8,128)(2,1)S(1)}, u32[]{:S(2)}, u32[]{:S(2)}) collective-permute-start(bf16[64,3584]{1,0:T(8,128)(2,1)S(1)} %get-tuple-element.22), channel_id=1, source_target_pairs={{24,16},{28,20},{25,17},{29,21},{26,18},{30,22},{27,19},{31,23}} | collective-permute-start | bytes 1376264 | tf_op jit(solution)/shard_map/ppermute | solution.py:296
  189.2 48.0 %collective-permute-start.13 = (bf16[64,3584]{1,0:T(8,128)(2,1)S(1)}, bf16[64,3584]{1,0:T(8,128)(2,1)S(1)}, u32[]{:S(2)}, u32[]{:S(2)}) collective-permute-start(bf16[64,3584]{1,0:T(8,128)(2,1)S(1)} %get-tuple-element.23), channel_id=1, source_target_pairs={{0,8},{4,12},{8,16},{12,20},{16,24},{20,28},{1,9},{5,13},{9,17},{1... | collective-permute-start | bytes 1376264 | tf_op jit(solution)/shard_map/ppermute | solution.py:295
  191.2 15.4 %collective-permute-start.14 = (bf16[64,3584]{1,0:T(8,128)(2,1)S(1)}, bf16[64,3584]{1,0:T(8,128)(2,1)S(1)}, u32[]{:S(2)}, u32[]{:S(2)}) collective-permute-start(bf16[64,3584]{1,0:T(8,128)(2,1)S(1)} %get-tuple-element.24), channel_id=1, source_target_pairs={{24,16},{28,20},{25,17},{29,21},{26,18},{30,22},{27,19},{31,23}} | collective-permute-start | bytes 1376264 | tf_op jit(solution)/shard_map/ppermute | solution.py:296
  195.4 20.9 %collective-permute-start.8 = (bf16[64,3584]{1,0:T(8,128)(2,1)S(1)}, bf16[64,3584]{1,0:T(8,128)(2,1)S(1)}, u32[]{:S(2)}, u32[]{:S(2)}) collective-permute-start(bf16[64,3584]{1,0:T(8,128)(2,1)S(1)} %add_convert_fusion.9), channel_id=1, source_target_pairs={{16,8},{20,12},{24,16},{28,20},{17,9},{21,13},{25,17},{29,21},{18,... | collective-permute-start | bytes 1376264 | tf_op jit(solution)/shard_map/ppermute | solution.py:296
  206.7 19.5 %collective-permute-start.15 = (bf16[64,3584]{1,0:T(8,128)(2,1)S(1)}, bf16[64,3584]{1,0:T(8,128)(2,1)S(1)}, u32[]{:S(2)}, u32[]{:S(2)}) collective-permute-start(bf16[64,3584]{1,0:T(8,128)(2,1)S(1)} %add_convert_fusion.2), channel_id=1, source_target_pairs={{16,8},{20,12},{24,16},{28,20},{17,9},{21,13},{25,17},{29,21},{18,... | collective-permute-start | bytes 1376264 | tf_op jit(solution)/shard_map/ppermute | solution.py:296
  217.5 18.5 %collective-permute-start.9 = (bf16[64,3584]{1,0:T(8,128)(2,1)S(1)}, bf16[64,3584]{1,0:T(8,128)(2,1)S(1)}, u32[]{:S(2)}, u32[]{:S(2)}) collective-permute-start(bf16[64,3584]{1,0:T(8,128)(2,1)S(1)} %add_convert_fusion.8), channel_id=1, source_target_pairs={{8,0},{12,4},{16,8},{20,12},{24,16},{28,20},{9,1},{13,5},{17,9},{2... | collective-permute-start | bytes 1376264 | tf_op jit(solution)/shard_map/ppermute | solution.py:296
  226.4 16.6 %collective-permute-start.16 = (bf16[64,3584]{1,0:T(8,128)(2,1)S(1)}, bf16[64,3584]{1,0:T(8,128)(2,1)S(1)}, u32[]{:S(2)}, u32[]{:S(2)}) collective-permute-start(bf16[64,3584]{1,0:T(8,128)(2,1)S(1)} %add_convert_fusion.1), channel_id=1, source_target_pairs={{8,0},{12,4},{16,8},{20,12},{24,16},{28,20},{9,1},{13,5},{17,9},{2... | collective-permute-start | bytes 1376264 | tf_op jit(solution)/shard_map/ppermute | solution.py:296
  (31 other events, 212.5 us)

commit v2 on v0

v2 whole, which is shorter than its diff:
```python
import functools

import jax
import jax.numpy as jnp
from jax import lax
from jax.experimental import pallas as pl
from jax.experimental.pallas import tpu as pltpu
from jax.sharding import PartitionSpec as P

BLOCK = 128
PARTS = 2
AHEAD = 3
COST = 10 ** 11
VMEM_LIMIT = 60 * 1024 * 1024


def tile_of(width):
    return next(t for t in (512, 256, 128) if width % t == 0)


def at_tile(ref, j, t):
    return ref.at[:, pl.ds(j * t, t)]


def token_places(n, cols, tokens, place_ref):
    own, tr = tokens // cols, tokens // (2 * n)
    size = min(own, tr)
    for k in range(cols):
        for i in range(own // size):
            row = (place_ref[2] ^ k) * own + i * size
            r = row // tr
            held = ((r + place_ref[1]) % 2) * (tokens // 2) + (r // 2) * tr + row % tr
            yield k, i * size, pl.multiple_of(held, size), size


def prepare_kernel(w_ref, keep_ref, out_ref, wv, kv, sems, o_sem):
    steps, _, t = out_ref.shape
    loads = [pltpu.make_async_copy(keep_ref, kv, sems.at[0])]
    loads += [pltpu.make_async_copy(w_ref.at[pl.ds(a * BLOCK, BLOCK), :], wv.at[a], sems.at[1 + a]) for a in range(wv.shape[0])]
    for copy in loads[: 1 + AHEAD]:
        copy.start()
    loads[0].wait()
    for a in range(wv.shape[0]):
        loads[1 + a].wait()
        if 1 + a + AHEAD < len(loads):
            loads[1 + a + AHEAD].start()
        for j in range(steps):
            cols = slice(j * t, (j + 1) * t)
            wv[a, :, cols] = wv[a, :, cols] * kv[a : a + 1, cols].astype(wv.dtype)
            pltpu.make_async_copy(wv.at[a, :, pl.ds(j * t, t)], out_ref.at[j, pl.ds(a * BLOCK, BLOCK), :], o_sem).start()
    pltpu.make_async_copy(wv, wv, o_sem).wait()


def prepare(weight, keep):
    depth, width = weight.shape
    t = tile_of(width // PARTS)
    return pl.pallas_call(
        prepare_kernel,
        in_specs=[ANY, ANY],
        out_specs=ANY,
        out_shape=jax.ShapeDtypeStruct((width // t, depth, t), weight.dtype),
        scratch_shapes=[
            pltpu.VMEM((depth // BLOCK, BLOCK, width), weight.dtype),
            pltpu.VMEM((depth // BLOCK, width), jnp.float32),
            pltpu.SemaphoreType.DMA((1 + depth // BLOCK,)),
            pltpu.SemaphoreType.DMA,
        ],
        compiler_params=pltpu.CompilerParams(vmem_limit_bytes=VMEM_LIMIT),
        cost_estimate=pl.CostEstimate(flops=COST, bytes_accessed=COST, transcendentals=0),
        name="prepare",
    )(weight, keep)


def load_weight(w_ref, wv, sems, first):
    return [pltpu.make_async_copy(w_ref.at[first + j], wv.at[j], sems.at[j]) for j in range(wv.shape[0])]


def forward_kernel(n, cols, part, emit, place_ref, *refs):
    x_refs, w_ref = refs[:cols], refs[cols]
    outs, (xs, wv, ov, w_sems, o_sems, x_sem) = refs[cols + 1 : -6], refs[-6:]
    steps, _, t = wv.shape
    tokens = xs.shape[0]
    half = tokens // 2
    for k, at, held, size in token_places(n, cols, tokens, place_ref):
        pltpu.make_async_copy(x_refs[k].at[pl.ds(at, size), :], xs.at[pl.ds(held, size), :], x_sem).start()
    loads = load_weight(w_ref, wv, w_sems, part * steps)
    for copy in loads[:AHEAD]:
        copy.start()
    pltpu.make_async_copy(xs, xs, x_sem).wait()
    stores = []
    if emit:
        stores.append(pltpu.make_async_copy(xs, outs[2], x_sem))
        stores[0].start()
    for j in range(steps):
        loads[j].wait()
        if j + AHEAD < steps:
            loads[j + AHEAD].start()
        acc = jnp.dot(xs[...], wv[j], preferred_element_type=jnp.float32)
        ov[j] = acc.astype(jnp.bfloat16)
        for i in range(2):
            rows = pl.ds(i * half, half)
            stores.append(pltpu.make_async_copy(ov.at[j, rows, :], at_tile(outs[i], j, t), o_sems.at[i, j]))
            stores[-1].start()
    for copy in stores:
        copy.wait()


ANY = pl.BlockSpec(memory_space=pl.ANY)


def call(kernel, name, place, args, out_shape, scratch, aliases=None, after=()):
    held = len(args)
    body = lambda place_ref, *refs: kernel(place_ref, *refs[:held], *refs[held + len(after) :])
    return pl.pallas_call(
        body,
        grid_spec=pltpu.PrefetchScalarGridSpec(
            num_scalar_prefetch=1,
            grid=(),
            in_specs=[ANY] * (held + len(after)),
            out_specs=jax.tree.map(lambda _: ANY, out_shape),
            scratch_shapes=scratch,
        ),
        out_shape=out_shape,
        input_output_aliases=aliases or {},
        compiler_params=pltpu.CompilerParams(vmem_limit_bytes=VMEM_LIMIT),
        cost_estimate=pl.CostEstimate(flops=COST, bytes_accessed=COST, transcendentals=0),
        name=name,
    )(place, *args, *after)


def forward(place, xs, weight, part, n, emit):
    steps, depth, t = weight.shape
    steps //= PARTS
    tokens = xs[0].shape[0] * len(xs)
    bf16 = jnp.bfloat16
    outs = [jax.ShapeDtypeStruct((tokens // 2, steps * t), bf16)] * 2
    return call(
        functools.partial(forward_kernel, n, len(xs), part, emit),
        "forward",
        place,
        [*xs, weight],
        outs + ([jax.ShapeDtypeStruct((tokens, depth), bf16)] if emit else []),
        [
            pltpu.VMEM((tokens, depth), bf16),
            pltpu.VMEM((steps, depth, t), bf16),
            pltpu.VMEM((steps, tokens, t), bf16),
            pltpu.SemaphoreType.DMA((steps,)),
            pltpu.SemaphoreType.DMA((2, steps)),
            pltpu.SemaphoreType.DMA,
        ],
    )


def start_pieces(n, place_ref, pieces, refs, held, sems, first):
    steps, tokens, t = held.shape
    tr = tokens // (2 * n)
    z = place_ref[0]
    for tiles in (range(min(2, steps)), range(min(2, steps), steps)):
        for (link, s, flip, lo, hi), ref in zip(pieces, refs):
            sign = jnp.where(z % 2 == 0, s, -s)
            if link is None:
                origin = z
            elif link == 2:
                origin = jnp.where((z + sign >= 0) & (z + sign < n), z + sign, z - sign)
            else:
                origin = z + sign if link == 0 else z - sign
            mine = [j for j in tiles if lo <= (first + j) * t < hi]

            @pl.when((origin >= 0) & (origin < n))
            def _():
                at = pl.multiple_of(flip * (tokens // 2) + origin * tr, tr)
                for j in mine:
                    source = ref.at[:, pl.ds((first + j) * t - lo, t)]
                    pltpu.make_async_copy(source, held.at[j, pl.ds(at, tr), :], sems.at[j]).start()


def wait_tile(held, sems, j):
    pltpu.make_async_copy(held.at[j], held.at[j], sems.at[j]).wait()


def input_grad_kernel(n, cols, pieces, part, first, last, place_ref, *refs):
    piece_refs, w_ref, refs = refs[: len(pieces)], refs[len(pieces)], refs[len(pieces) + 1 :]
    if not first:
        before_ref, refs = refs[0], refs[1:]
    n_out = cols if last else 1
    out_refs, (held, wv, acc, ob, sems, w_sems, a_sem, o_sem) = refs[:n_out], refs[n_out:]
    steps, tokens, t = held.shape
    loads = load_weight(w_ref, wv, w_sems, part * steps)
    loads[0].start()
    start_pieces(n, place_ref, pieces, piece_refs, held, sems, part * steps)
    for copy in loads[1:AHEAD]:
        copy.start()
    if not first:
        before = pltpu.make_async_copy(before_ref, acc, a_sem)
        before.start()
    for j in range(steps):
        loads[j].wait()
        if j + AHEAD < steps:
            loads[j + AHEAD].start()
        wait_tile(held, sems, j)
        if j == 0 and not first:
            before.wait()
        product = lax.dot_general(held[j], wv[j], (((1,), (1,)), ((), ())), preferred_element_type=jnp.float32)
        if j == 0 and first:
            acc[...] = product
        else:
            acc[...] += product
    if last:
        ob[...] = acc[...].astype(jnp.bfloat16)
        for k, at, row, size in token_places(n, cols, tokens, place_ref):
            pltpu.make_async_copy(ob.at[pl.ds(row, size), :], out_refs[k].at[pl.ds(at, size), :], o_sem).start()
        pltpu.make_async_copy(ob, ob, o_sem).wait()
    else:
        store = pltpu.make_async_copy(acc, out_refs[0], o_sem)
        store.start()
        store.wait()


def input_grad_part(place, pieces, arrays, weight, before, after, part, n, cols, tokens):
    steps, depth, t = weight.shape
    steps //= PARTS
    first, last = before is None, part == PARTS - 1
    f32, bf16 = jnp.float32, jnp.bfloat16
    if last:
        out_shape = [jax.ShapeDtypeStruct((tokens // cols, depth), bf16)] * cols
    else:
        out_shape = [jax.ShapeDtypeStruct((tokens, depth), f32)]
    return call(
        functools.partial(input_grad_kernel, n, cols, pieces, part, first, last),
        "input_grad",
        place,
        [*arrays, weight] + ([] if first else [before]),
        out_shape,
        [
            pltpu.VMEM((steps, tokens, t), bf16),
            pltpu.VMEM((steps, depth, t), bf16),
            pltpu.VMEM((tokens, depth), f32),
            pltpu.VMEM((tokens, depth), bf16),
            pltpu.SemaphoreType.DMA((steps,)),
            pltpu.SemaphoreType.DMA((steps,)),
            pltpu.SemaphoreType.DMA,
            pltpu.SemaphoreType.DMA,
        ],
        after=after,
    )


def weight_grad_kernel(n, pieces, part, scale, first, place_ref, *refs):
    piece_refs, (xt_ref, keep_ref), refs = refs[: len(pieces)], refs[len(pieces) : len(pieces) + 2], refs[len(pieces) + 2 :]
    out_ref, held, xt, kv, ov, sems, x_sems, o_sems = refs[0 if first else 1 :]
    steps, _, t = held.shape
    loads = [
        pltpu.make_async_copy(xt_ref, xt, x_sems.at[0]),
        pltpu.make_async_copy(keep_ref.at[:, pl.ds(part * steps * t, steps * t)], kv, x_sems.at[1]),
    ]
    for copy in loads:
        copy.start()
    start_pieces(n, place_ref, pieces, piece_refs, held, sems, part * steps)
    for copy in loads:
        copy.wait()
    stores = []
    for j in range(steps):
        wait_tile(held, sems, j)
        acc = jnp.dot(xt[...], held[j], preferred_element_type=jnp.float32)
        for a in range(xt.shape[0] // BLOCK):
            rows = slice(a * BLOCK, (a + 1) * BLOCK)
            keep = kv[a : a + 1, j * t : (j + 1) * t] * scale
            ov[j, rows, :] = (acc[rows, :] * keep).astype(jnp.bfloat16)
        stores.append(pltpu.make_async_copy(ov.at[j], at_tile(out_ref, part * steps + j, t), o_sems.at[j]))
        stores[-1].start()
    for copy in stores:
        copy.wait()


def weight_grad_part(place, pieces, arrays, xt, keep, before, after, part, n, width):
    depth, tokens = xt.shape
    t = tile_of(width // PARTS)
    steps = width // PARTS // t
    first = before is None
    bf16 = jnp.bfloat16
    return call(
        functools.partial(weight_grad_kernel, n, pieces, part, tokens ** (-0.5), first),
        "weight_grad",
        place,
        [*arrays, xt, keep] + ([] if first else [before]),
        jax.ShapeDtypeStruct((depth, width), bf16),
        [
            pltpu.VMEM((steps, tokens, t), bf16),
            pltpu.VMEM((depth, tokens), bf16),
            pltpu.VMEM((depth // BLOCK, steps * t), jnp.float32),
            pltpu.VMEM((steps, depth, t), bf16),
            pltpu.SemaphoreType.DMA((steps,)),
            pltpu.SemaphoreType.DMA((2,)),
            pltpu.SemaphoreType.DMA((steps,)),
        ],
        {} if first else {len(arrays) + 3: 0},
        after,
    )


def local(n, cols, inputs, weight, mask, cotangent):
    row, col = lax.axis_index("row"), lax.axis_index("col")
    z, core = row // 2, row % 2
    place = jnp.stack([z, core, col]).astype(jnp.int32)
    width = weight.shape[1]
    pw = width // PARTS
    tr = cotangent.shape[0]
    tokens = tr * 2 * n

    even = z % 2 == 0
    up = [(2 * i + c, 2 * (i + 1) + c) for i in range(n - 1) for c in range(2)]
    links = [[e for i, j in up if (i // 2) % 2 == odd for e in ((i, j), (j, i))] for odd in range(2)]
    for pairs in links:
        pairs += [(i, i ^ 1) for i in sorted(set(range(2 * n)) - {i for i, _ in pairs})]
    other_side = jnp.where(even, z - 1, z + 1)
    has = [jnp.where(even, z + 1, z - 1) < n, (other_side >= 0) & (other_side < n)]
    exchange = lambda v, link: lax.ppermute(v, "row", links[link])
    swap = lambda v: lax.ppermute(v, "row", [(i, i ^ 1) for i in range(2 * n)])
    across = lambda v, k: lax.ppermute(v, "col", [(i, i ^ k) for i in range(cols)])

    f32, bf16 = jnp.float32, jnp.bfloat16
    xs = [inputs] + [across(inputs, k) for k in range(1, cols)]
    got = [exchange(cotangent, link) for link in range(2)]
    keep = jnp.repeat(mask.astype(f32), BLOCK, axis=1)
    pieces = [((None, 0, 0, 0, width), cotangent), ((None, 0, 1, 0, width), swap(cotangent))]

    def keep_pieces(s, lo, pair):
        hi = lo + pair[0].shape[1]
        if 2 * s < n:
            held = list(enumerate(pair))
        else:
            origin = jnp.where(even, z + s, z - s)
            first = (origin >= 0) & (origin < n)
            held = [(2, jnp.where(first, *pair))]
        for link, v in held:
            pieces.extend([((link, s, 0, lo, hi), v), ((link, s, 1, lo, hi), swap(v))])

    keep_pieces(1, 0, got)
    first, got = got, [[v[:, p * pw : (p + 1) * pw] for v in got] for p in range(PARTS)]

    masked = prepare(weight, keep)
    mine, theirs = [], []
    for p in range(PARTS):
        m, other, *more = forward(place, xs, masked, p, n, p == 0)
        whole = more[0] if more else whole
        mine.append(m)
        theirs.append(swap(other))

    def term(p, d):
        at = jnp.clip(d, 0, n - 1) * tr
        cut = lambda v: lax.dynamic_slice_in_dim(v, at, tr, 0).astype(f32)
        return cut(mine[p]) + cut(theirs[p])

    sent = [None] * PARTS
    for k in range(2, n + 1):
        for p in range(PARTS):
            if k > 2:
                keep_pieces(k - 1, p * pw, got[p])
            send = []
            if k == 2 and p:
                got[p] = [v[:, p * pw : (p + 1) * pw] for v in lax.optimization_barrier((*first, *got[p - 1]))[:2]]
            for link in range(2):
                upward = even if link == 0 else ~even
                d = jnp.where(upward, z + n - k + 1, z - n + k - 1)
                own = jnp.where((d >= 0) & (d < n), term(p, d), 0.0)
                came = jnp.where(has[1 - link], got[p][1 - link].astype(f32), 0.0)
                send.append((came + own).astype(bf16))
            got[p] = [exchange(v, link) for link, v in enumerate(send)]
            sent[p] = send
    outputs = jnp.zeros((tr, width), bf16)
    for p in range(PARTS):
        total = term(p, z)
        for link in range(2):
            total += jnp.where(has[link], got[p][link].astype(f32), 0.0)
        outputs = lax.dynamic_update_slice(outputs, total.astype(bf16), (0, p * pw))

    xt = whole.T
    acc = wg = None
    for p in range(PARTS):
        own = [(k, v) for k, v in pieces if k[3] < (p + 1) * pw and k[4] > p * pw]
        kinds, arrays = [k for k, _ in own], [v for _, v in own]
        last = p == PARTS - 1
        acc = input_grad_part(place, kinds, arrays, masked, acc, sent[p] if p == 0 else [wg], p, n, cols, tokens)
        if not last:
            acc = acc[0]
        wg = weight_grad_part(place, kinds, arrays, xt, keep, wg, [outputs] if last else sent[p + 1], p, n, width)
    total = acc[0].astype(f32)
    for k in range(1, cols):
        total = total + across(acc[k], k).astype(f32)
    return outputs, total.astype(bf16), wg


def solution(mesh):
    n, cols = mesh.shape["row"] // 2, mesh.shape["col"]
    return jax.shard_map(
        functools.partial(local, n, cols),
        mesh=mesh,
        in_specs=(P("col", "row"), P("row", "col"), P("row", "col"), P("row", "col")),
        out_specs=(P("row", "col"), P("col", "row"), P("row", "col")),
        check_vma=False,
    )
```

time: 234 us -> 152 us (0.65)
  waiting for transfers between devices: 139 us -> 30.1 us
  Pallas kernels: 0 us -> 66.7 us
  matrix products: 58.4 us -> 0 us
  starting transfers between devices: 0.34 us -> 25.8 us
  other arithmetic: 0.69 us -> 20.7 us
  local copies, waits for them, and re-layouts: 18.7 us -> 5.82 us
  between operations: 13.8 us -> 0.99 us
    all_gather x2 -> x0, waiting for transfers between devices: 78.5 us -> none  [the longest x1 76.2 us: local(): shard_rows = lax.all_gather(cotangent, 'row', axis=0, tiled=True)]
    pallas_call x0 -> x7, Pallas kernels: none -> 66.7 us  [the longest x6 56 us: call(): pl.pallas_call(body, grid_spec=pltpu.PrefetchScalarGridSpec(num_scalar_pr...]
    unnamed x6 -> x0, waiting for transfers between devices: 60.1 us -> none
    dot_general x3 -> x0, matrix products: 58.4 us -> none  [the longest x1 23.5 us: local(): jnp.dot(chosen, masked, preferred_element_type=jnp.float32)]
    ppermute x0 -> x29, waiting for transfers between devices: none -> 30.1 us  [the longest x14 30 us: local(): exchange = lambda v, link: lax.ppermute(v, 'row', links[link])]
    ppermute x0 -> x29, starting transfers between devices: none -> 25.8 us  [the longest x14 13.8 us: local(): exchange = lambda v, link: lax.ppermute(v, 'row', links[link])]
    convert_element_type x1 -> x10, other arithmetic: 0.69 us -> 18.2 us  [the longest x6 13.2 us: local(): send.append((came + own).astype(bf16))]
    unnamed x4 -> x38, local copies, waits for them, and re-layouts: 11.5 us -> 2.64 us
  transfers between devices with their start and end apart: 4 -> 29, of which waited for: 3 -> 4; matrix products, arithmetic and copies ran while one was open for 34% -> 15% of each run, Pallas kernels for 0% -> 44%
where the time goes in v2:
time: 152 us; the launch traced here: 150 us
  Pallas kernels  66.7 us (44%)
  waiting for transfers between devices  30.1 us (20%)
  starting transfers between devices  25.8 us (17%)
  other arithmetic  20.7 us (14%)
  local copies, waits for them, and re-layouts  5.82 us (4%)
    pallas_call x6, Pallas kernels, call(): pl.pallas_call(body, grid_spec=pltpu.PrefetchScalarGridSpec(num_scalar_pr...  56 us
    ppermute x14, waiting for transfers between devices, local(): exchange = lambda v, link: lax.ppermute(v, 'row', links[link])  30 us
    ppermute x14, starting transfers between devices, local(): exchange = lambda v, link: lax.ppermute(v, 'row', links[link])  13.8 us
    convert_element_type x6, other arithmetic, local(): send.append((came + own).astype(bf16))  13.2 us
    pallas_call x1, Pallas kernels, prepare(): pl.pallas_call(prepare_kernel, in_specs=[ANY, ANY], out_specs=ANY, out_sh...  10.8 us
    ppermute x6, starting transfers between devices, local(): lax.ppermute(v, 'col', [(i, i ^ k) for i in range(cols)])  6.14 us
    ppermute x9, starting transfers between devices, local(): swap = lambda v: lax.ppermute(v, 'row', [(i, i ^ 1) for i in range(2 * n)])  5.91 us
    convert_element_type x2, other arithmetic, local(): outputs = lax.dynamic_update_slice(outputs, total.astype(bf16), (0, p * pw))  3.44 us
  transfers between devices with their start and end apart: 29, of which 4 were waited for; matrix products, arithmetic and copies ran while one was open for 15% of the time, Pallas kernels for 44%

profile of v2, /device:TPU:1, one launch (start us, length us, event | category | flops | bytes accessed | tf_op | source)
XLA Modules:
  0.0 150.2 jit_solution(16083910869813725301)
XLA Ops:
  0.6 3.1 %collective-permute-start.2 = (bf16[128,1024]{1,0:T(8,128)(2,1)}, bf16[128,1024]{1,0:T(8,128)(2,1)S(1)}, u32[]{:S(2)}, u32[]{:S(2)}) collective-permute-start(bf16[128,1024]{1,0:T(8,128)(2,1)} %refs_0_.7), channel_id=1, source_target_pairs={{0,3},{1,2},{2,1},{3,0},{4,7},{5,6},{6,5},{7,4},{8,11},{9,10},{10,... | collective-permute-start | bytes 786440 | tf_op jit(solution)/shard_map/ppermute | solution.py:319
  4.1 1.4 collective-permute-start.8
  5.5 1.8 %collective-permute-start.4 = (bf16[64,7168]{1,0:T(8,128)(2,1)}, bf16[64,7168]{1,0:T(8,128)(2,1)}, u32[]{:S(2)}, u32[]{:S(2)}) collective-permute-start(bf16[64,7168]{1,0:T(8,128)(2,1)} %refs_0_.11), channel_id=1, source_target_pairs={{8,16},{16,8},{12,20},{20,12},{0,4},{4,0},{24,28},{28,24},{9,17},{... | collective-permute-start | bytes 2752520 | tf_op jit(solution)/shard_map/ppermute | solution.py:317
  7.3 0.7 convert_element_type.192
  8.0 0.8 broadcast_bitcast_fusion.keep_ref.refs_11_
  8.9 10.8 %prepare.1.refs_4_.refs_10_ = bf16[14,1024,512]{2,1,0:T(8,128)(2,1)} custom-call(bf16[1024,7168]{1,0:T(8,128)(2,1)} %w_ref.1, f32[8,7168]{1,0:T(8,128)} %broadcast_bitcast_fusion.keep_ref.refs_11_), custom_call_target="tpu_custom_call" | custom-call | flops 99999997952 | bytes 99999997952 | tf_op jit(solution)/shard_map/prepare/pallas_call | solution.py:57
  19.7 0.6 pad_add_fusion.place_ref
  20.3 0.7 copy-done.16
  21.0 0.7 copy-done.18
  21.7 9.0 %forward.2 = (bf16[256,3584]{1,0:T(8,128)(2,1)}, bf16[256,3584]{1,0:T(8,128)(2,1)}, bf16[512,1024]{1,0:T(8,128)(2,1)}) custom-call(s32[3]{0:T(128)} %pad_add_fusion.place_ref, bf16[128,1024]{1,0:T(8,128)(2,1)} %refs_0_.7, bf16[128,1024]{1,0:T(8,128)(2,1)} %copy-done.18, bf16[128,1024]{1,0:T(8,128)(2,1)} %copy-done.17, bf16[128,1024]{1,0:T(8,128)(2,1)} %copy-done.16, ...), custom_call_target="tpu_custom_call" | custom-call | flops 99999997952 | bytes 99999997952 | tf_op jit(solution)/shard_map/forward/pallas_call | solution.py:114
  30.8 9.0 %forward.3 = (bf16[256,3584]{1,0:T(8,128)(2,1)}, bf16[256,3584]{1,0:T(8,128)(2,1)}) custom-call(s32[3]{0:T(128)} %pad_add_fusion.place_ref, bf16[128,1024]{1,0:T(8,128)(2,1)} %refs_0_.7, bf16[128,1024]{1,0:T(8,128)(2,1)} %copy-done.18, bf16[128,1024]{1,0:T(8,128)(2,1)} %copy-done.17, bf16[128,1024]{1,0:T(8,128)(2,1)} %copy-done.16, ...), custom_call_target="tpu_custom_call" | custom-call | flops 99999997952 | bytes 99999997952 | tf_op jit(solution)/shard_map/forward/pallas_call | solution.py:114
  39.9 0.4 collective-permute-start.12
  40.3 2.7 %add_convert_fusion.10 = (bf16[64,3584]{1,0:T(8,128)(2,1)}, bf16[64,3584]{1,0:T(8,128)(2,1)S(1)}) fusion(bf16[64,7168]{1,0:T(8,128)(2,1)} %collective-permute-done.8.refs_2_, bf16[256,3584]{1,0:T(8,128)(2,1)} %collective-permute-done.3, s32[]{:T(128)S(6)} %select_n.259, bf16[256,3584]{1,0:T(8,128)(2,1)S(1)} %copy-done.1, pred[]{:T(512)S(6)} %and.52, ...), kind=kLoop, calls=%fused_computation.11 | loop fusion | flops 3670016 | bytes 3670028 | tf_op jit(solution)/shard_map/convert_element_type | solution.py:367
  43.1 2.4 %collective-permute-start.5 = (bf16[64,3584]{1,0:T(8,128)(2,1)S(1)}, bf16[64,3584]{1,0:T(8,128)(2,1)S(1)}, u32[]{:S(2)}, u32[]{:S(2)}) collective-permute-start(bf16[64,3584]{1,0:T(8,128)(2,1)S(1)} %get-tuple-element.36), channel_id=1, source_target_pairs={{0,8},{8,0},{4,12},{12,4},{16,24},{24,16},{20,28},{28,20},{1,9},{9... | collective-permute-start | bytes 1376264 | tf_op jit(solution)/shard_map/ppermute | solution.py:317
  45.5 0.6 collective-permute-start.19
  46.1 2.3 %copy.9 = bf16[512,1024]{0,1:T(8,128)(2,1)} copy(bf16[512,1024]{1,0:T(8,128)(2,1)} %get-tuple-element.20) | data formatting | bytes 2097152 | tf_op jit(solution)/shard_map/forward/pallas_call | solution.py:114
  48.4 0.5 collective-permute-start.21
  48.9 7.2 %collective-permute-done.5 = bf16[64,3584]{1,0:T(8,128)(2,1)S(1)} collective-permute-done((bf16[64,3584]{1,0:T(8,128)(2,1)S(1)}, bf16[64,3584]{1,0:T(8,128)(2,1)S(1)}, u32[]{:S(2)}, u32[]{:S(2)}) %collective-permute-start.5) | collective-permute-done | bytes 458784 | tf_op jit(solution)/shard_map/ppermute | solution.py:317
  56.1 2.0 %add_convert_fusion.6 = (bf16[64,3584]{1,0:T(8,128)(2,1)S(1)}, bf16[64,3584]{1,0:T(8,128)(2,1)S(1)}) fusion(bf16[256,3584]{1,0:T(8,128)(2,1)} %collective-permute-done.12, s32[]{:T(128)S(6)} %select_n.244, bf16[256,3584]{1,0:T(8,128)(2,1)S(1)} %copy-done, bf16[64,7168]{1,0:T(8,128)(2,1)} %collective-permute-done.4.refs_4_, pred[]{:T(512)S(6)} %and.49, ...), kind=kLoop, calls=%fused_computation.7 | loop fusion | flops 3670016 | bytes 3670028 | tf_op jit(solution)/shard_map/convert_element_type | solution.py:367
  58.1 2.6 %collective-permute-start.13 = (bf16[64,3584]{1,0:T(8,128)(2,1)S(1)}, bf16[64,3584]{1,0:T(8,128)(2,1)S(1)}, u32[]{:S(2)}, u32[]{:S(2)}) collective-permute-start(bf16[64,3584]{1,0:T(8,128)(2,1)S(1)} %get-tuple-element.33), channel_id=1, source_target_pairs={{0,8},{8,0},{4,12},{12,4},{16,24},{24,16},{20,28},{28,20},{1,9},{9... | collective-permute-start | bytes 1376264 | tf_op jit(solution)/shard_map/ppermute | solution.py:317
  61.0 1.6 %add_convert_fusion.12 = (bf16[64,3584]{1,0:T(8,128)(2,1)S(1)}, bf16[64,3584]{1,0:T(8,128)(2,1)S(1)}) fusion(bf16[64,3584]{1,0:T(8,128)(2,1)S(1)} %collective-permute-done.5, bf16[256,3584]{1,0:T(8,128)(2,1)} %collective-permute-done.3, s32[]{:T(128)S(6)} %select_n.249, bf16[256,3584]{1,0:T(8,128)(2,1)S(1)} %copy-done.2, pred[]{:T(512)S(6)} %and.50, ...), kind=kLoop, calls=%fused_computation.13 | loop fusion | flops 3670016 | bytes 3670028 | tf_op jit(solution)/shard_map/convert_element_type | solution.py:367
  62.7 8.9 %collective-permute-done.13 = bf16[64,3584]{1,0:T(8,128)(2,1)S(1)} collective-permute-done((bf16[64,3584]{1,0:T(8,128)(2,1)S(1)}, bf16[64,3584]{1,0:T(8,128)(2,1)S(1)}, u32[]{:S(2)}, u32[]{:S(2)}) %collective-permute-start.13) | collective-permute-done | bytes 458784 | tf_op jit(solution)/shard_map/ppermute | solution.py:317
  71.6 0.6 collective-permute-start.6
  72.2 0.7 collective-permute-start.10
  73.0 1.6 %add_convert_fusion.5 = (bf16[64,3584]{1,0:T(8,128)(2,1)S(1)}, bf16[64,3584]{1,0:T(8,128)(2,1)S(1)}) fusion(bf16[64,3584]{1,0:T(8,128)(2,1)S(1)} %collective-permute-done.13, bf16[256,3584]{1,0:T(8,128)(2,1)} %collective-permute-done.12, s32[]{:T(128)S(6)} %select_n.249, bf16[256,3584]{1,0:T(8,128)(2,1)S(1)} %copy-done, pred[]{:T(512)S(6)} %and.50, ...), kind=kLoop, calls=%fused_computation.6 | loop fusion | flops 3670016 | bytes 3670028 | tf_op jit(solution)/shard_map/convert_element_type | solution.py:367
  74.6 1.3 collective-permute-start.14
  75.9 8.4 %collective-permute-done.10 = bf16[64,3584]{1,0:T(8,128)(2,1)S(1)} collective-permute-done((bf16[64,3584]{1,0:T(8,128)(2,1)S(1)}, bf16[64,3584]{1,0:T(8,128)(2,1)S(1)}, u32[]{:S(2)}, u32[]{:S(2)}) %collective-permute-start.10) | collective-permute-done | bytes 458784 | tf_op jit(solution)/shard_map/ppermute | solution.py:317
  84.4 2.7 %add_convert_fusion.11 = (bf16[64,3584]{1,0:T(8,128)(2,1)}, bf16[64,3584]{1,0:T(8,128)(2,1)}) fusion(bf16[64,3584]{1,0:T(8,128)(2,1)S(1)} %collective-permute-done.6, bf16[256,3584]{1,0:T(8,128)(2,1)} %collective-permute-done.3, s32[]{:T(128)S(6)} %select_n.253, bf16[256,3584]{1,0:T(8,128)(2,1)S(1)} %copy-done.2, pred[]{:T(512)S(6)} %and.51, pred[]{:T(512)S(6)} %and.48, ...), kind=kLoop, calls=%fused_computation.12 | loop fusion | flops 3670016 | bytes 3670027 | tf_op jit(solution)/shard_map/convert_element_type | solution.py:367
  87.2 0.8 broadcast_select_fusion.1.refs_6_
  88.0 2.1 %collective-permute-start.24 = (bf16[64,3584]{1,0:T(8,128)(2,1)S(1)}, bf16[64,3584]{1,0:T(8,128)(2,1)S(1)}, u32[]{:S(2)}, u32[]{:S(2)}) collective-permute-start(bf16[64,3584]{1,0:T(8,128)(2,1)S(1)} %broadcast_select_fusion.refs_6_), channel_id=1, source_target_pairs={{0,4},{4,0},{8,12},{12,8},{16,20},{20,16},{24,28},{28,24},{1,5},{5... | collective-permute-start | bytes 1376264 | tf_op jit(solution)/shard_map/ppermute | solution.py:318
  90.1 5.6 %collective-permute-done.17 = bf16[64,3584]{1,0:T(8,128)(2,1)S(1)} collective-permute-done((bf16[64,3584]{1,0:T(8,128)(2,1)S(1)}, bf16[64,3584]{1,0:T(8,128)(2,1)S(1)}, u32[]{:S(2)}, u32[]{:S(2)}) %collective-permute-start.17) | collective-permute-done | bytes 458784 | tf_op jit(solution)/shard_map/ppermute | solution.py:317
  95.6 1.7 %collective-permute-start.25 = (bf16[64,3584]{1,0:T(8,128)(2,1)S(1)}, bf16[64,3584]{1,0:T(8,128)(2,1)S(1)}, u32[]{:S(2)}, u32[]{:S(2)}) collective-permute-start(bf16[64,3584]{1,0:T(8,128)(2,1)S(1)} %broadcast_select_fusion.2.refs_8_), channel_id=1, source_target_pairs={{0,4},{4,0},{8,12},{12,8},{16,20},{20,16},{24,28},{28,24},{1,5},{5... | collective-permute-start | bytes 1376264 | tf_op jit(solution)/shard_map/ppermute | solution.py:318
  97.3 2.6 %add_convert_fusion.4 = (bf16[64,3584]{1,0:T(8,128)(2,1)}, bf16[64,3584]{1,0:T(8,128)(2,1)}) fusion(bf16[64,3584]{1,0:T(8,128)(2,1)S(1)} %collective-permute-done.14, bf16[256,3584]{1,0:T(8,128)(2,1)} %collective-permute-done.12, s32[]{:T(128)S(6)} %select_n.253, bf16[256,3584]{1,0:T(8,128)(2,1)S(1)} %copy-done, pred[]{:T(512)S(6)} %and.51, pred[]{:T(512)S(6)} %and.48, ...), kind=kLoop, calls=%fused_computation.5 | loop fusion | flops 3670016 | bytes 3670027 | tf_op jit(solution)/shard_map/convert_element_type | solution.py:367
  100.0 0.6 collective-permute-start.11
  100.7 1.3 collective-permute-start.15
  102.0 0.4 collective-permute-start.18
  102.8 9.0 %input_grad.2.refs_11_ = f32[512,1024]{1,0:T(8,128)} custom-call(s32[3]{0:T(128)} %pad_add_fusion.place_ref, bf16[64,7168]{1,0:T(8,128)(2,1)} %refs_0_.11, bf16[64,7168]{1,0:T(8,128)(2,1)} %collective-permute-done.19.refs_1_, bf16[64,7168]{1,0:T(8,128)(2,1)} %collective-permute-done.8.refs_2_, bf16[64,7168]{1,0:T(8,128)(2,1)} %copy-done.11, ...), custom_call_target="tpu_custom_call" | custom-call | flops 99999997952 | bytes 99999997952 | tf_op jit(solution)/shard_map/input_grad/pallas_call | solution.py:114
  111.8 9.3 %weight_grad.2.refs_12_ = bf16[1024,7168]{1,0:T(8,128)(2,1)} custom-call(s32[3]{0:T(128)} %pad_add_fusion.place_ref, bf16[64,7168]{1,0:T(8,128)(2,1)} %refs_0_.11, bf16[64,7168]{1,0:T(8,128)(2,1)} %collective-permute-done.19.refs_1_, bf16[64,7168]{1,0:T(8,128)(2,1)} %collective-permute-done.8.refs_2_, bf16[64,7168]{1,0:T(8,128)(2,1)} %copy-done.11, ...), custom_call_target="tpu_custom_call" | custom-call | flops 99999997952 | bytes 99999997952 | tf_op jit(solution)/shard_map/weight_grad/pallas_call | solution.py:114
  121.3 0.4 collective-permute-start.23
  121.7 1.7 %add_convert_fusion.7 = bf16[64,3584]{1,0:T(8,128)(2,1)S(1)} fusion(bf16[64,3584]{1,0:T(8,128)(2,1)} %collective-permute-done.11, bf16[64,3584]{1,0:T(8,128)(2,1)} %collective-permute-done.7, bf16[256,3584]{1,0:T(8,128)(2,1)} %collective-permute-done.3, s32[]{:T(128)S(6)} %select_n.235, bf16[256,3584]{1,0:T(8,128)(2,1)} %get-tuple-element.14, pred[]{:T(512)S(6)} %and.48, ...), kind=kLoop, calls=%fused_computation.8 | loop fusion | flops 2293760 | bytes 2293766 | tf_op jit(solution)/shard_map/convert_element_type | solution.py:375
  123.5 0.8 copy-done.13
  124.3 10.2 %input_grad.3 = (bf16[128,1024]{1,0:T(8,128)(2,1)}, bf16[128,1024]{1,0:T(8,128)(2,1)}, bf16[128,1024]{1,0:T(8,128)(2,1)}, bf16[128,1024]{1,0:T(8,128)(2,1)}) custom-call(s32[3]{0:T(128)} %pad_add_fusion.place_ref, bf16[64,7168]{1,0:T(8,128)(2,1)} %refs_0_.11, bf16[64,7168]{1,0:T(8,128)(2,1)} %collective-permute-done.19.refs_1_, ...), custom_call_target="tpu_custom_call" | custom-call | flops 99999997952 | bytes 99999997952 | tf_op jit(solution)/shard_map/input_grad/pallas_call | solution.py:114
  134.5 1.3 collective-permute-start.26
  135.8 1.2 collective-permute-start.27
  137.2 1.7 %add_convert_fusion = bf16[64,3584]{1,0:T(8,128)(2,1)S(1)} fusion(bf16[64,3584]{1,0:T(8,128)(2,1)} %collective-permute-done.18, bf16[64,3584]{1,0:T(8,128)(2,1)} %collective-permute-done.15, bf16[256,3584]{1,0:T(8,128)(2,1)} %collective-permute-done.12, s32[]{:T(128)S(6)} %select_n.235, bf16[256,3584]{1,0:T(8,128)(2,1)} %get-tuple-element.16, pred[]{:T(512)S(6)} %and.48, ...), kind=kLoop, calls=%fused_computation.1 | loop fusion | flops 2293760 | bytes 2293766 | tf_op jit(solution)/shard_map/convert_element_type | solution.py:375
  139.0 1.0 pad_maximum_fusion.refs_13_
  139.9 9.3 %weight_grad.3 = bf16[1024,7168]{1,0:T(8,128)(2,1)} custom-call(s32[3]{0:T(128)} %pad_add_fusion.place_ref, bf16[64,7168]{1,0:T(8,128)(2,1)} %refs_0_.11, bf16[64,7168]{1,0:T(8,128)(2,1)} %collective-permute-done.19.refs_1_, bf16[64,7168]{1,0:T(8,128)(2,1)} %collective-permute-done.8.refs_2_, ...), custom_call_target="tpu_custom_call", output_to_operand_aliasing={{}: (13, {})} | custom-call | flops 99999997952 | bytes 99999997952 | tf_op jit(solution)/shard_map/weight_grad/pallas_call | solution.py:114
  149.3 0.9 add_convert_fusion.14
  (74 shorter events, 2.0 us)
Async XLA Ops:
  0.6 19.6 %collective-permute-start.2 = (bf16[128,1024]{1,0:T(8,128)(2,1)}, bf16[128,1024]{1,0:T(8,128)(2,1)S(1)}, u32[]{:S(2)}, u32[]{:S(2)}) collective-permute-start(bf16[128,1024]{1,0:T(8,128)(2,1)} %refs_0_.7), channel_id=1, source_target_pairs={{0,3},{1,2},{2,1},{3,0},{4,7},{5,6},{6,5},{7,4},{8,11},{9,10},{10,... | collective-permute-start | bytes 786440 | tf_op jit(solution)/shard_map/ppermute | solution.py:319
  3.7 16.6 %collective-permute-start.1 = (bf16[128,1024]{1,0:T(8,128)(2,1)}, bf16[128,1024]{1,0:T(8,128)(2,1)S(1)}, u32[]{:S(2)}, u32[]{:S(2)}) collective-permute-start(bf16[128,1024]{1,0:T(8,128)(2,1)} %refs_0_.7), channel_id=1, source_target_pairs={{0,2},{1,3},{2,0},{3,1},{4,6},{5,7},{6,4},{7,5},{8,10},{9,11},{10,... | collective-permute-start | bytes 786440 | tf_op jit(solution)/shard_map/ppermute | solution.py:319
  3.9 16.4 %collective-permute-start = (bf16[128,1024]{1,0:T(8,128)(2,1)}, bf16[128,1024]{1,0:T(8,128)(2,1)S(1)}, u32[]{:S(2)}, u32[]{:S(2)}) collective-permute-start(bf16[128,1024]{1,0:T(8,128)(2,1)} %refs_0_.7), channel_id=1, source_target_pairs={{0,1},{1,0},{2,3},{3,2},{4,5},{5,4},{6,7},{7,6},{8,9},{9,8},{10,11... | collective-permute-start | bytes 786440 | tf_op jit(solution)/shard_map/ppermute | solution.py:319
  4.1 36.2 %collective-permute-start.8 = (bf16[64,7168]{1,0:T(8,128)(2,1)}, bf16[64,7168]{1,0:T(8,128)(2,1)}, u32[]{:S(2)}, u32[]{:S(2)}) collective-permute-start(bf16[64,7168]{1,0:T(8,128)(2,1)} %refs_0_.11), channel_id=1, source_target_pairs={{0,8},{8,0},{4,12},{12,4},{16,24},{24,16},{20,28},{28,20},{1,9},{9... | collective-permute-start | bytes 2752520 | tf_op jit(solution)/shard_map/ppermute | solution.py:317
  5.5 34.8 %collective-permute-start.4 = (bf16[64,7168]{1,0:T(8,128)(2,1)}, bf16[64,7168]{1,0:T(8,128)(2,1)}, u32[]{:S(2)}, u32[]{:S(2)}) collective-permute-start(bf16[64,7168]{1,0:T(8,128)(2,1)} %refs_0_.11), channel_id=1, source_target_pairs={{8,16},{16,8},{12,20},{20,12},{0,4},{4,0},{24,28},{28,24},{9,17},{... | collective-permute-start | bytes 2752520 | tf_op jit(solution)/shard_map/ppermute | solution.py:317
  20.3 0.7 copy-start.16
  20.3 0.8 copy-start.17
  21.0 0.7 copy-start.18
  30.7 9.6 %copy-start.1 = (bf16[256,3584]{1,0:T(8,128)(2,1)S(1)}, bf16[256,3584]{1,0:T(8,128)(2,1)}, u32[]{:S(2)}) copy-start(bf16[256,3584]{1,0:T(8,128)(2,1)} %get-tuple-element.14) | copy-start | bytes 5505028
  30.7 9.6 %collective-permute-start.3 = (bf16[256,3584]{1,0:T(8,128)(2,1)}, bf16[256,3584]{1,0:T(8,128)(2,1)}, u32[]{:S(2)}, u32[]{:S(2)}) collective-permute-start(bf16[256,3584]{1,0:T(8,128)(2,1)} %get-tuple-element.15), channel_id=1, source_target_pairs={{0,4},{4,0},{8,12},{12,8},{16,20},{20,16},{24,28},{28,24},{1,5},{5... | collective-permute-start | bytes 5505032 | tf_op jit(solution)/shard_map/ppermute | solution.py:318
  39.9 16.2 %collective-permute-start.12 = (bf16[256,3584]{1,0:T(8,128)(2,1)}, bf16[256,3584]{1,0:T(8,128)(2,1)}, u32[]{:S(2)}, u32[]{:S(2)}) collective-permute-start(bf16[256,3584]{1,0:T(8,128)(2,1)} %get-tuple-element.17), channel_id=1, source_target_pairs={{0,4},{4,0},{8,12},{12,8},{16,20},{20,16},{24,28},{28,24},{1,5},{5... | collective-permute-start | bytes 5505032 | tf_op jit(solution)/shard_map/ppermute | solution.py:318
  43.0 13.1 %copy-start = (bf16[256,3584]{1,0:T(8,128)(2,1)S(1)}, bf16[256,3584]{1,0:T(8,128)(2,1)}, u32[]{:S(2)}) copy-start(bf16[256,3584]{1,0:T(8,128)(2,1)} %get-tuple-element.16) | copy-start | bytes 5505028
  43.0 5.5 %collective-permute-start.9 = (bf16[64,3584]{1,0:T(8,128)(2,1)}, bf16[64,3584]{1,0:T(8,128)(2,1)S(1)}, u32[]{:S(2)}, u32[]{:S(2)}) collective-permute-start(bf16[64,3584]{1,0:T(8,128)(2,1)} %get-tuple-element.35), channel_id=1, source_target_pairs={{8,16},{16,8},{12,20},{20,12},{0,4},{4,0},{24,28},{28,24},{9,17},{... | collective-permute-start | bytes 1376264 | tf_op jit(solution)/shard_map/ppermute | solution.py:317
  43.1 13.0 %collective-permute-start.5 = (bf16[64,3584]{1,0:T(8,128)(2,1)S(1)}, bf16[64,3584]{1,0:T(8,128)(2,1)S(1)}, u32[]{:S(2)}, u32[]{:S(2)}) collective-permute-start(bf16[64,3584]{1,0:T(8,128)(2,1)S(1)} %get-tuple-element.36), channel_id=1, source_target_pairs={{0,8},{8,0},{4,12},{12,4},{16,24},{24,16},{20,28},{28,20},{1,9},{9... | collective-permute-start | bytes 1376264 | tf_op jit(solution)/shard_map/ppermute | solution.py:317
  45.5 54.4 %collective-permute-start.19 = (bf16[64,7168]{1,0:T(8,128)(2,1)}, bf16[64,7168]{1,0:T(8,128)(2,1)}, u32[]{:S(2)}, u32[]{:S(2)}) collective-permute-start(bf16[64,7168]{1,0:T(8,128)(2,1)} %refs_0_.11), channel_id=1, source_target_pairs={{0,4},{4,0},{8,12},{12,8},{16,20},{20,16},{24,28},{28,24},{1,5},{5... | collective-permute-start | bytes 2752520 | tf_op jit(solution)/shard_map/ppermute | solution.py:318
  48.4 51.6 %collective-permute-start.20 = (bf16[64,7168]{1,0:T(8,128)(2,1)}, bf16[64,7168]{1,0:T(8,128)(2,1)S(1)}, u32[]{:S(2)}, u32[]{:S(2)}) collective-permute-start(bf16[64,7168]{1,0:T(8,128)(2,1)} %collective-permute-done.8.refs_2_), channel_id=1, source_target_pairs={{0,4},{4,0},{8,12},{12,8},{16,20},{20,16},{24,28},{28,24},{1,5},{5... | collective-permute-start | bytes 2752520 | tf_op jit(solution)/shard_map/ppermute | solution.py:318
  48.4 52.2 %collective-permute-start.21 = (bf16[64,7168]{1,0:T(8,128)(2,1)}, bf16[64,7168]{1,0:T(8,128)(2,1)S(1)}, u32[]{:S(2)}, u32[]{:S(2)}) collective-permute-start(bf16[64,7168]{1,0:T(8,128)(2,1)} %collective-permute-done.4.refs_4_), channel_id=1, source_target_pairs={{0,4},{4,0},{8,12},{12,8},{16,20},{20,16},{24,28},{28,24},{1,5},{5... | collective-permute-start | bytes 2752520 | tf_op jit(solution)/shard_map/ppermute | solution.py:318
  56.1 4.9 %copy-start.2 = (bf16[256,3584]{1,0:T(8,128)(2,1)S(1)}, bf16[256,3584]{1,0:T(8,128)(2,1)}, u32[]{:S(2)}) copy-start(bf16[256,3584]{1,0:T(8,128)(2,1)} %get-tuple-element.14) | copy-start | bytes 5505028
  58.1 13.5 %collective-permute-start.13 = (bf16[64,3584]{1,0:T(8,128)(2,1)S(1)}, bf16[64,3584]{1,0:T(8,128)(2,1)S(1)}, u32[]{:S(2)}, u32[]{:S(2)}) collective-permute-start(bf16[64,3584]{1,0:T(8,128)(2,1)S(1)} %get-tuple-element.33), channel_id=1, source_target_pairs={{0,8},{8,0},{4,12},{12,4},{16,24},{24,16},{20,28},{28,20},{1,9},{9... | collective-permute-start | bytes 1376264 | tf_op jit(solution)/shard_map/ppermute | solution.py:317
  60.7 11.5 %collective-permute-start.16 = (bf16[64,3584]{1,0:T(8,128)(2,1)S(1)}, bf16[64,3584]{1,0:T(8,128)(2,1)S(1)}, u32[]{:S(2)}, u32[]{:S(2)}) collective-permute-start(bf16[64,3584]{1,0:T(8,128)(2,1)S(1)} %get-tuple-element.34), channel_id=1, source_target_pairs={{8,16},{16,8},{12,20},{20,12},{0,4},{4,0},{24,28},{28,24},{9,17},{... | collective-permute-start | bytes 1376264 | tf_op jit(solution)/shard_map/ppermute | solution.py:317
  62.7 25.3 %copy-start.7 = (bf16[64,3584]{1,0:T(8,128)(2,1)}, bf16[64,3584]{1,0:T(8,128)(2,1)S(1)}, u32[]{:S(2)}) copy-start(bf16[64,3584]{1,0:T(8,128)(2,1)S(1)} %broadcast_select_fusion.refs_6_) | copy-start | bytes 1376260
  71.6 3.0 %collective-permute-start.6 = (bf16[64,3584]{1,0:T(8,128)(2,1)S(1)}, bf16[64,3584]{1,0:T(8,128)(2,1)S(1)}, u32[]{:S(2)}, u32[]{:S(2)}) collective-permute-start(bf16[64,3584]{1,0:T(8,128)(2,1)S(1)} %get-tuple-element.27), channel_id=1, source_target_pairs={{8,16},{16,8},{12,20},{20,12},{0,4},{4,0},{24,28},{28,24},{9,17},{... | collective-permute-start | bytes 1376264 | tf_op jit(solution)/shard_map/ppermute | solution.py:317
  72.2 12.2 %collective-permute-start.10 = (bf16[64,3584]{1,0:T(8,128)(2,1)S(1)}, bf16[64,3584]{1,0:T(8,128)(2,1)S(1)}, u32[]{:S(2)}, u32[]{:S(2)}) collective-permute-start(bf16[64,3584]{1,0:T(8,128)(2,1)S(1)} %get-tuple-element.28), channel_id=1, source_target_pairs={{0,8},{8,0},{4,12},{12,4},{16,24},{24,16},{20,28},{28,20},{1,9},{9... | collective-permute-start | bytes 1376264 | tf_op jit(solution)/shard_map/ppermute | solution.py:317
  74.6 13.4 %collective-permute-start.14 = (bf16[64,3584]{1,0:T(8,128)(2,1)S(1)}, bf16[64,3584]{1,0:T(8,128)(2,1)S(1)}, u32[]{:S(2)}, u32[]{:S(2)}) collective-permute-start(bf16[64,3584]{1,0:T(8,128)(2,1)S(1)} %get-tuple-element.31), channel_id=1, source_target_pairs={{8,16},{16,8},{12,20},{20,12},{0,4},{4,0},{24,28},{28,24},{9,17},{... | collective-permute-start | bytes 1376264 | tf_op jit(solution)/shard_map/ppermute | solution.py:317
  84.4 11.3 %collective-permute-start.17 = (bf16[64,3584]{1,0:T(8,128)(2,1)S(1)}, bf16[64,3584]{1,0:T(8,128)(2,1)S(1)}, u32[]{:S(2)}, u32[]{:S(2)}) collective-permute-start(bf16[64,3584]{1,0:T(8,128)(2,1)S(1)} %get-tuple-element.32), channel_id=1, source_target_pairs={{0,8},{8,0},{4,12},{12,4},{16,24},{24,16},{20,28},{28,20},{1,9},{9... | collective-permute-start | bytes 1376264 | tf_op jit(solution)/shard_map/ppermute | solution.py:317
  84.4 11.2 %copy-start.9 = (bf16[64,3584]{1,0:T(8,128)(2,1)}, bf16[64,3584]{1,0:T(8,128)(2,1)S(1)}, u32[]{:S(2)}) copy-start(bf16[64,3584]{1,0:T(8,128)(2,1)S(1)} %broadcast_select_fusion.2.refs_8_) | copy-start | bytes 1376260
  88.0 11.9 %copy-start.3 = (bf16[64,3584]{1,0:T(8,128)(2,1)}, bf16[64,3584]{1,0:T(8,128)(2,1)S(1)}, u32[]{:S(2)}) copy-start(bf16[64,3584]{1,0:T(8,128)(2,1)S(1)} %collective-permute-done.14) | copy-start | bytes 1376260
  88.0 12.7 %collective-permute-start.24 = (bf16[64,3584]{1,0:T(8,128)(2,1)S(1)}, bf16[64,3584]{1,0:T(8,128)(2,1)S(1)}, u32[]{:S(2)}, u32[]{:S(2)}) collective-permute-start(bf16[64,3584]{1,0:T(8,128)(2,1)S(1)} %broadcast_select_fusion.refs_6_), channel_id=1, source_target_pairs={{0,4},{4,0},{8,12},{12,8},{16,20},{20,16},{24,28},{28,24},{1,5},{5... | collective-permute-start | bytes 1376264 | tf_op jit(solution)/shard_map/ppermute | solution.py:318
  95.6 4.2 %copy-start.5 = (bf16[64,3584]{1,0:T(8,128)(2,1)}, bf16[64,3584]{1,0:T(8,128)(2,1)S(1)}, u32[]{:S(2)}) copy-start(bf16[64,3584]{1,0:T(8,128)(2,1)S(1)} %collective-permute-done.17) | copy-start | bytes 1376260
  95.6 6.4 %collective-permute-start.25 = (bf16[64,3584]{1,0:T(8,128)(2,1)S(1)}, bf16[64,3584]{1,0:T(8,128)(2,1)S(1)}, u32[]{:S(2)}, u32[]{:S(2)}) collective-permute-start(bf16[64,3584]{1,0:T(8,128)(2,1)S(1)} %broadcast_select_fusion.2.refs_8_), channel_id=1, source_target_pairs={{0,4},{4,0},{8,12},{12,8},{16,20},{20,16},{24,28},{28,24},{1,5},{5... | collective-permute-start | bytes 1376264 | tf_op jit(solution)/shard_map/ppermute | solution.py:318
  99.9 21.4 %collective-permute-start.7 = (bf16[64,3584]{1,0:T(8,128)(2,1)}, bf16[64,3584]{1,0:T(8,128)(2,1)}, u32[]{:S(2)}, u32[]{:S(2)}) collective-permute-start(bf16[64,3584]{1,0:T(8,128)(2,1)} %get-tuple-element.25.refs_11_), channel_id=1, source_target_pairs={{0,8},{8,0},{4,12},{12,4},{16,24},{24,16},{20,28},{28,20},{1,9},{9... | collective-permute-start | bytes 1376264 | tf_op jit(solution)/shard_map/ppermute | solution.py:317
  100.0 2.0 %copy-start.11 = (bf16[64,7168]{1,0:T(8,128)(2,1)}, bf16[64,7168]{1,0:T(8,128)(2,1)S(1)}, u32[]{:S(2)}) copy-start(bf16[64,7168]{1,0:T(8,128)(2,1)S(1)} %collective-permute-done.20.refs_3_) | copy-start | bytes 2752516
  100.0 21.7 %collective-permute-start.11 = (bf16[64,3584]{1,0:T(8,128)(2,1)}, bf16[64,3584]{1,0:T(8,128)(2,1)}, u32[]{:S(2)}, u32[]{:S(2)}) collective-permute-start(bf16[64,3584]{1,0:T(8,128)(2,1)} %get-tuple-element.26.refs_12_), channel_id=1, source_target_pairs={{8,16},{16,8},{12,20},{20,12},{0,4},{4,0},{24,28},{28,24},{9,17},{... | collective-permute-start | bytes 1376264 | tf_op jit(solution)/shard_map/ppermute | solution.py:317
  100.6 1.4 copy-start.12
  100.6 22.8 %collective-permute-start.22 = (bf16[64,3584]{1,0:T(8,128)(2,1)}, bf16[64,3584]{1,0:T(8,128)(2,1)}, u32[]{:S(2)}, u32[]{:S(2)}) collective-permute-start(bf16[64,3584]{1,0:T(8,128)(2,1)} %broadcast_select_fusion.1.refs_6_), channel_id=1, source_target_pairs={{0,4},{4,0},{8,12},{12,8},{16,20},{20,16},{24,28},{28,24},{1,5},{5... | collective-permute-start | bytes 1376264 | tf_op jit(solution)/shard_map/ppermute | solution.py:318
  100.7 1.8 %copy-start.14 = (bf16[64,3584]{1,0:T(8,128)(2,1)}, bf16[64,3584]{1,0:T(8,128)(2,1)S(1)}, u32[]{:S(2)}) copy-start(bf16[64,3584]{1,0:T(8,128)(2,1)S(1)} %collective-permute-done.24.refs_7_) | copy-start | bytes 1376260
  100.7 36.5 %collective-permute-start.15 = (bf16[64,3584]{1,0:T(8,128)(2,1)}, bf16[64,3584]{1,0:T(8,128)(2,1)}, u32[]{:S(2)}, u32[]{:S(2)}) collective-permute-start(bf16[64,3584]{1,0:T(8,128)(2,1)} %get-tuple-element.29.refs_12_), channel_id=1, source_target_pairs={{0,8},{8,0},{4,12},{12,4},{16,24},{24,16},{20,28},{28,20},{1,9},{9... | collective-permute-start | bytes 1376264 | tf_op jit(solution)/shard_map/ppermute | solution.py:317
  102.0 0.8 copy-start.15
  102.0 35.2 %collective-permute-start.18 = (bf16[64,3584]{1,0:T(8,128)(2,1)}, bf16[64,3584]{1,0:T(8,128)(2,1)}, u32[]{:S(2)}, u32[]{:S(2)}) collective-permute-start(bf16[64,3584]{1,0:T(8,128)(2,1)} %get-tuple-element.30.refs_13_), channel_id=1, source_target_pairs={{8,16},{16,8},{12,20},{20,12},{0,4},{4,0},{24,28},{28,24},{9,17},{... | collective-permute-start | bytes 1376264 | tf_op jit(solution)/shard_map/ppermute | solution.py:317
  111.8 9.4 %copy-start.4 = (bf16[64,3584]{1,0:T(8,128)(2,1)S(1)}, bf16[64,3584]{1,0:T(8,128)(2,1)}, u32[]{:S(2)}) copy-start(bf16[64,3584]{1,0:T(8,128)(2,1)} %copy-done.3) | copy-start | bytes 1376260
  111.8 9.4 %copy-start.6 = (bf16[64,3584]{1,0:T(8,128)(2,1)S(1)}, bf16[64,3584]{1,0:T(8,128)(2,1)}, u32[]{:S(2)}) copy-start(bf16[64,3584]{1,0:T(8,128)(2,1)} %copy-done.5) | copy-start | bytes 1376260
  121.3 2.2 %copy-start.8 = (bf16[64,3584]{1,0:T(8,128)(2,1)}, bf16[64,3584]{1,0:T(8,128)(2,1)S(1)}, u32[]{:S(2)}) copy-start(bf16[64,3584]{1,0:T(8,128)(2,1)S(1)} %broadcast_select_fusion.3.refs_8_) | copy-start | bytes 1376260
  121.3 2.2 %collective-permute-start.23 = (bf16[64,3584]{1,0:T(8,128)(2,1)S(1)}, bf16[64,3584]{1,0:T(8,128)(2,1)S(1)}, u32[]{:S(2)}, u32[]{:S(2)}) collective-permute-start(bf16[64,3584]{1,0:T(8,128)(2,1)S(1)} %broadcast_select_fusion.3.refs_8_), channel_id=1, source_target_pairs={{0,4},{4,0},{8,12},{12,8},{16,20},{20,16},{24,28},{28,24},{1,5},{5... | collective-permute-start | bytes 1376264 | tf_op jit(solution)/shard_map/ppermute | solution.py:318
  123.5 0.8 copy-start.13
  134.5 14.8 %collective-permute-start.26 = (bf16[128,1024]{1,0:T(8,128)(2,1)}, bf16[128,1024]{1,0:T(8,128)(2,1)S(1)}, u32[]{:S(2)}, u32[]{:S(2)}) collective-permute-start(bf16[128,1024]{1,0:T(8,128)(2,1)} %get-tuple-element.22), channel_id=1, source_target_pairs={{0,1},{1,0},{2,3},{3,2},{4,5},{5,4},{6,7},{7,6},{8,9},{9,8},{10,11... | collective-permute-start | bytes 786440 | tf_op jit(solution)/shard_map/ppermute | solution.py:319
  135.8 13.5 %collective-permute-start.27 = (bf16[128,1024]{1,0:T(8,128)(2,1)}, bf16[128,1024]{1,0:T(8,128)(2,1)S(1)}, u32[]{:S(2)}, u32[]{:S(2)}) collective-permute-start(bf16[128,1024]{1,0:T(8,128)(2,1)} %get-tuple-element.23), channel_id=1, source_target_pairs={{0,2},{1,3},{2,0},{3,1},{4,6},{5,7},{6,4},{7,5},{8,10},{9,11},{10,... | collective-permute-start | bytes 786440 | tf_op jit(solution)/shard_map/ppermute | solution.py:319
  137.0 12.3 %collective-permute-start.28 = (bf16[128,1024]{1,0:T(8,128)(2,1)}, bf16[128,1024]{1,0:T(8,128)(2,1)S(1)}, u32[]{:S(2)}, u32[]{:S(2)}) collective-permute-start(bf16[128,1024]{1,0:T(8,128)(2,1)} %get-tuple-element.24), channel_id=1, source_target_pairs={{0,3},{1,2},{2,1},{3,0},{4,7},{5,6},{6,5},{7,4},{8,11},{9,10},{10,... | collective-permute-start | bytes 786440 | tf_op jit(solution)/shard_map/ppermute | solution.py:319
  139.9 9.4 %copy-start.10 = (bf16[128,1024]{1,0:T(8,128)(2,1)S(1)}, bf16[128,1024]{1,0:T(8,128)(2,1)}, u32[]{:S(2)}) copy-start(bf16[128,1024]{1,0:T(8,128)(2,1)} %get-tuple-element.21) | copy-start | bytes 786436

commit v3 on v0

v3 whole, which is shorter than its diff:
```python
import functools

import jax
import jax.numpy as jnp
from jax import lax
from jax.experimental import pallas as pl
from jax.experimental.pallas import tpu as pltpu
from jax.sharding import PartitionSpec as P

BLOCK = 128
PARTS = 2
AHEAD = 2
ROWS_AHEAD = 4
COST = 10 ** 11
VMEM_LIMIT = 60 * 1024 * 1024


def tile_of(width):
    return next(t for t in (512, 256, 128) if width % t == 0)


def at_tile(ref, j, t):
    return ref.at[:, pl.ds(j * t, t)]


def token_places(n, cols, tokens, place_ref):
    own, tr = tokens // cols, tokens // (2 * n)
    size = min(own, tr)
    for k in range(cols):
        for i in range(own // size):
            row = (place_ref[2] ^ k) * own + i * size
            r = row // tr
            held = ((r + place_ref[1]) % 2) * (tokens // 2) + (r // 2) * tr + row % tr
            yield k, i * size, pl.multiple_of(held, size), size


def mask_tile(tile_ref, keep):
    for a in range(tile_ref.shape[0] // BLOCK):
        rows = slice(a * BLOCK, (a + 1) * BLOCK)
        tile_ref[rows, :] = tile_ref[rows, :] * keep[a : a + 1, :].astype(tile_ref.dtype)


def load_weight(w_ref, keep_ref, wv, kv, sems, part):
    steps, _, t = wv.shape
    copies = [pltpu.make_async_copy(keep_ref.at[:, pl.ds(part * steps * t, steps * t)], kv, sems.at[steps])]
    return copies + [pltpu.make_async_copy(at_tile(w_ref, part * steps + j, t), wv.at[j], sems.at[j]) for j in range(steps)]


def forward_kernel(n, cols, part, emit, place_ref, *refs):
    x_refs, (w_ref, keep_ref) = refs[:cols], refs[cols : cols + 2]
    outs, (xs, wv, kv, ov, w_sems, o_sems, x_sem) = refs[cols + 2 : -7], refs[-7:]
    steps, _, t = wv.shape
    tokens = xs.shape[0]
    half = tokens // 2
    for k, at, held, size in token_places(n, cols, tokens, place_ref):
        pltpu.make_async_copy(x_refs[k].at[pl.ds(at, size), :], xs.at[pl.ds(held, size), :], x_sem).start()
    loads = load_weight(w_ref, keep_ref, wv, kv, w_sems, part)
    for copy in loads[: 1 + AHEAD]:
        copy.start()
    pltpu.make_async_copy(xs, xs, x_sem).wait()
    stores = []
    if emit:
        stores.append(pltpu.make_async_copy(xs, outs[2], x_sem))
        stores[0].start()
    loads[0].wait()
    for j in range(steps):
        loads[1 + j].wait()
        if j + AHEAD < steps:
            loads[1 + j + AHEAD].start()
        mask_tile(wv.at[j], kv[:, j * t : (j + 1) * t])
        acc = jnp.dot(xs[...], wv[j], preferred_element_type=jnp.float32)
        ov[j] = acc.astype(jnp.bfloat16)
        for i in range(2):
            rows = pl.ds(i * half, half)
            stores.append(pltpu.make_async_copy(ov.at[j, rows, :], at_tile(outs[i], j, t), o_sems.at[i, j]))
            stores[-1].start()
    for copy in stores:
        copy.wait()


ANY = pl.BlockSpec(memory_space=pl.ANY)


def call(kernel, name, place, args, out_shape, scratch, aliases=None, after=(), cost=COST):
    held = len(args)
    body = lambda place_ref, *refs: kernel(place_ref, *refs[:held], *refs[held + len(after) :])
    return pl.pallas_call(
        body,
        grid_spec=pltpu.PrefetchScalarGridSpec(
            num_scalar_prefetch=1,
            grid=(),
            in_specs=[ANY] * (held + len(after)),
            out_specs=jax.tree.map(lambda _: ANY, out_shape),
            scratch_shapes=scratch,
        ),
        out_shape=out_shape,
        input_output_aliases=aliases or {},
        compiler_params=pltpu.CompilerParams(vmem_limit_bytes=VMEM_LIMIT),
        cost_estimate=pl.CostEstimate(flops=cost, bytes_accessed=cost, transcendentals=0),
        name=name,
    )(place, *args, *after)


def pause_kernel(place_ref, out_ref, held, sem):
    held[...] = jnp.zeros_like(held)
    store = pltpu.make_async_copy(held, out_ref, sem)
    store.start()
    store.wait()


def pause(place, after):
    shape = (8, 128)
    return call(
        pause_kernel,
        "pause",
        place,
        [],
        jax.ShapeDtypeStruct(shape, jnp.float32),
        [pltpu.VMEM(shape, jnp.float32), pltpu.SemaphoreType.DMA],
        after=after,
    )


def forward(place, xs, weight, keep, after, part, n, emit):
    depth, width = weight.shape
    t = tile_of(width // PARTS)
    steps = width // PARTS // t
    tokens = xs[0].shape[0] * len(xs)
    bf16 = jnp.bfloat16
    outs = [jax.ShapeDtypeStruct((tokens // 2, steps * t), bf16)] * 2
    return call(
        functools.partial(forward_kernel, n, len(xs), part, emit),
        "forward",
        place,
        [*xs, weight, keep],
        outs + ([jax.ShapeDtypeStruct((tokens, depth), bf16)] if emit else []),
        [
            pltpu.VMEM((tokens, depth), bf16),
            pltpu.VMEM((steps, depth, t), bf16),
            pltpu.VMEM((depth // BLOCK, steps * t), jnp.float32),
            pltpu.VMEM((steps, tokens, t), bf16),
            pltpu.SemaphoreType.DMA((steps + 1,)),
            pltpu.SemaphoreType.DMA((2, steps)),
            pltpu.SemaphoreType.DMA,
        ],
        after=after,
    )


def origin_of(n, z, piece):
    link, s, _ = piece
    sign = jnp.where(z % 2 == 0, s, -s)
    if link == 2:
        return jnp.where((z + sign >= 0) & (z + sign < n), z + sign, z - sign)
    return z - sign if link == 1 else z + sign


def groups_of(steps):
    ends = sorted({min(e, steps) for e in (1, 4, steps)})
    return list(zip([0, *ends], ends))


def start_pieces(n, place_ref, pieces, refs, held, sems, t):
    tokens, width = held.shape
    tr = tokens // (2 * n)
    for g, (lo, hi) in enumerate(groups_of(width // t)):
        for piece, ref in zip(pieces, refs):
            origin = origin_of(n, place_ref[0], piece)

            @pl.when((origin >= 0) & (origin < n))
            def _():
                at = pl.multiple_of(piece[2] * (tokens // 2) + origin * tr, tr)
                columns = pl.ds(lo * t, (hi - lo) * t)
                pltpu.make_async_copy(ref.at[:, columns], held.at[pl.ds(at, tr), columns], sems.at[g]).start()


def each_piece(n, place_ref, pieces, body):
    for i, piece in enumerate(pieces):
        origin = origin_of(n, place_ref[0], piece)
        pl.when((origin >= 0) & (origin < n))(functools.partial(body, i, origin))


def product_rows(n, place_ref, pieces, piece_refs, w_ref, keep_ref, held, wv, kv, acc, sems, w_sems):
    steps, _, t = wv.shape
    tr = held.shape[0] // len(pieces)
    loads = load_weight(w_ref, keep_ref, wv, kv, w_sems, 0)
    for copy in loads[:2]:
        copy.start()

    def rows_of(i):
        return pltpu.make_async_copy(piece_refs[i], held.at[pl.ds(i * tr, tr), :], sems.at[i])

    each_piece(n, place_ref, pieces, lambda i, _: rows_of(i).start())
    for copy in loads[2 : 1 + ROWS_AHEAD]:
        copy.start()
    each_piece(n, place_ref, pieces, lambda i, _: rows_of(i).wait())
    loads[0].wait()
    for j in range(steps):
        loads[1 + j].wait()
        if j + ROWS_AHEAD < steps:
            loads[1 + j + ROWS_AHEAD].start()
        columns = slice(j * t, (j + 1) * t)
        mask_tile(wv.at[j], kv[:, columns])
        product = lax.dot_general(held[:, columns], wv[j], (((1,), (1,)), ((), ())), preferred_element_type=jnp.float32)
        if j == 0:
            acc[...] = product
        else:
            acc[...] += product


def early_kernel(n, pieces, place_ref, *refs):
    piece_refs, (w_ref, keep_ref, out_ref, held, wv, kv, acc, ob, sems, w_sems, o_sem) = refs[: len(pieces)], refs[len(pieces) :]
    product_rows(n, place_ref, pieces, piece_refs, w_ref, keep_ref, held, wv, kv, acc, sems, w_sems)
    ob[...] = acc[...].astype(jnp.bfloat16)
    store = pltpu.make_async_copy(ob, out_ref, o_sem)
    store.start()
    store.wait()


def early_rows(place, n, pieces, arrays, weight, keep, after):
    depth, width = weight.shape
    t = tile_of(width // PARTS)
    steps = width // t
    rows = len(pieces) * arrays[0].shape[0]
    f32, bf16 = jnp.float32, jnp.bfloat16
    return call(
        functools.partial(early_kernel, n, pieces),
        "early_rows",
        place,
        [*arrays, weight, keep],
        jax.ShapeDtypeStruct((rows, depth), bf16),
        [
            pltpu.VMEM((rows, width), bf16),
            pltpu.VMEM((steps, depth, t), bf16),
            pltpu.VMEM((depth // BLOCK, width), f32),
            pltpu.VMEM((rows, depth), f32),
            pltpu.VMEM((rows, depth), bf16),
            pltpu.SemaphoreType.DMA((len(pieces),)),
            pltpu.SemaphoreType.DMA((steps + 1,)),
            pltpu.SemaphoreType.DMA,
        ],
        after=after,
    )


def late_kernel(n, cols, early, late, place_ref, *refs):
    piece_refs, (w_ref, keep_ref, early_ref), refs = refs[: len(late)], refs[len(late) : len(late) + 3], refs[len(late) + 3 :]
    out_refs, (held, wv, kv, acc, ob, sems, w_sems, e_sems, o_sem) = refs[:cols], refs[cols:]
    tokens = ob.shape[0]
    tr = tokens // (2 * n)
    rows = lambda piece, origin: pl.ds(pl.multiple_of(piece[2] * (tokens // 2) + origin * tr, tr), tr)

    def early_of(i, origin):
        return pltpu.make_async_copy(early_ref.at[pl.ds(i * tr, tr), :], ob.at[rows(early[i], origin), :], e_sems.at[i])

    each_piece(n, place_ref, early, lambda i, origin: early_of(i, origin).start())
    product_rows(n, place_ref, late, piece_refs, w_ref, keep_ref, held, wv, kv, acc, sems, w_sems)
    each_piece(n, place_ref, early, lambda i, origin: early_of(i, origin).wait())

    def store(i, origin):
        ob[rows(late[i], origin), :] = acc[i * tr : (i + 1) * tr, :].astype(jnp.bfloat16)

    each_piece(n, place_ref, late, store)
    for k, at, row, size in token_places(n, cols, tokens, place_ref):
        pltpu.make_async_copy(ob.at[pl.ds(row, size), :], out_refs[k].at[pl.ds(at, size), :], o_sem).start()
    pltpu.make_async_copy(ob, ob, o_sem).wait()


def late_rows(place, early, late, arrays, weight, keep, done, after, n, cols):
    depth, width = weight.shape
    tr = arrays[0].shape[0]
    tokens = 2 * n * tr
    t = tile_of(width // PARTS)
    steps = width // t
    f32, bf16 = jnp.float32, jnp.bfloat16
    rows = len(late) * tr
    return call(
        functools.partial(late_kernel, n, cols, early, late),
        "late_rows",
        place,
        [*arrays, weight, keep, done],
        [jax.ShapeDtypeStruct((tokens // cols, depth), bf16)] * cols,
        [
            pltpu.VMEM((rows, width), bf16),
            pltpu.VMEM((steps, depth, t), bf16),
            pltpu.VMEM((depth // BLOCK, width), f32),
            pltpu.VMEM((rows, depth), f32),
            pltpu.VMEM((tokens, depth), bf16),
            pltpu.SemaphoreType.DMA((len(late),)),
            pltpu.SemaphoreType.DMA((steps + 1,)),
            pltpu.SemaphoreType.DMA((len(early),)),
            pltpu.SemaphoreType.DMA,
        ],
        after=after,
    )


def send_kernel(n, k, links, behind, place_ref, *refs):
    mine_ref, theirs_ref, refs = refs[0], refs[1], refs[2:]
    came_refs, refs = refs[: len(behind)], refs[len(behind) :]
    out_refs, (terms, cv, ov, sems, o_sems) = refs[: len(links)], refs[len(links) :]
    tr = ov.shape[1]
    z = place_ref[0]
    odd = lax.rem(z, 2)

    def each_link(body):
        for i, link in enumerate(links):
            upward = odd == link
            d = jnp.where(upward, z + n - k + 1, z - n + k - 1)
            pl.when((d >= 0) & (d < n))(functools.partial(body, i, link, d))

    def load(i, link, d):
        for h, ref in enumerate((mine_ref, theirs_ref)):
            source = ref.at[pl.ds(pl.multiple_of(d * tr, tr), tr), :]
            pltpu.make_async_copy(source, terms.at[i, h], sems.at[i]).start()
        if 1 - link in behind:
            pltpu.make_async_copy(came_refs[behind.index(1 - link)], cv.at[i], sems.at[len(links) + i]).start()

    def add(i, link, d):
        pltpu.make_async_copy(terms.at[i], terms.at[i], sems.at[i]).wait()
        total = terms[i, 0].astype(jnp.float32) + terms[i, 1].astype(jnp.float32)
        if 1 - link in behind:
            pltpu.make_async_copy(cv.at[i], cv.at[i], sems.at[len(links) + i]).wait()
            other = z + 1 - 2 * odd if link == 1 else z - 1 + 2 * odd
            total += jnp.where((other >= 0) & (other < n), cv[i].astype(jnp.float32), 0.0)
        ov[i] = total.astype(jnp.bfloat16)
        pltpu.make_async_copy(ov.at[i], out_refs[i], o_sems.at[i]).start()

    each_link(load)
    each_link(add)
    each_link(lambda i, link, d: pltpu.make_async_copy(ov.at[i], out_refs[i], o_sems.at[i]).wait())


def send_sums(place, mine, theirs, came, links, after, k, n):
    behind = tuple(link for link in range(2) if came[link] is not None)
    pw = mine.shape[1]
    tr = mine.shape[0] // n
    bf16 = jnp.bfloat16
    return call(
        functools.partial(send_kernel, n, k, links, behind),
        "send_sums",
        place,
        [mine, theirs, *(came[link] for link in behind)],
        [jax.ShapeDtypeStruct((tr, pw), bf16)] * len(links),
        [
            pltpu.VMEM((len(links), 2, tr, pw), bf16),
            pltpu.VMEM((len(links), tr, pw), bf16),
            pltpu.VMEM((len(links), tr, pw), bf16),
            pltpu.SemaphoreType.DMA((2 * len(links),)),
            pltpu.SemaphoreType.DMA((len(links),)),
        ],
        after=after,
        cost=1 if k < n else COST,
    )


def weight_grad_kernel(n, pieces, scale, place_ref, *refs):
    piece_refs, (xt_ref, keep_ref, out_ref, held, xt, kv, ov, sems, x_sems, o_sems) = refs[: len(pieces)], refs[len(pieces) :]
    steps, _, t = ov.shape
    loads = [pltpu.make_async_copy(xt_ref, xt, x_sems.at[0]), pltpu.make_async_copy(keep_ref, kv, x_sems.at[1])]
    for copy in loads:
        copy.start()
    start_pieces(n, place_ref, pieces, piece_refs, held, sems, t)
    groups = groups_of(steps)
    for copy in loads:
        copy.wait()
    stores = []
    for j in range(steps):
        for g, (lo, hi) in enumerate(groups):
            if lo == j:
                part = held.at[:, pl.ds(lo * t, (hi - lo) * t)]
                pltpu.make_async_copy(part, part, sems.at[g]).wait()
        acc = jnp.dot(xt[...], held[:, j * t : (j + 1) * t], preferred_element_type=jnp.float32)
        for a in range(xt.shape[0] // BLOCK):
            rows = slice(a * BLOCK, (a + 1) * BLOCK)
            keep = kv[a : a + 1, j * t : (j + 1) * t] * scale
            ov[j, rows, :] = (acc[rows, :] * keep).astype(jnp.bfloat16)
        stores.append(pltpu.make_async_copy(ov.at[j], at_tile(out_ref, j, t), o_sems.at[j]))
        stores[-1].start()
    for copy in stores:
        copy.wait()


def weight_grad(place, pieces, arrays, xt, keep, n, width):
    depth, tokens = xt.shape
    t = tile_of(width // PARTS)
    steps = width // t
    bf16 = jnp.bfloat16
    return call(
        functools.partial(weight_grad_kernel, n, pieces, tokens ** (-0.5)),
        "weight_grad",
        place,
        [*arrays, xt, keep],
        jax.ShapeDtypeStruct((depth, width), bf16),
        [
            pltpu.VMEM((tokens, width), bf16),
            pltpu.VMEM((depth, tokens), bf16),
            pltpu.VMEM((depth // BLOCK, width), jnp.float32),
            pltpu.VMEM((steps, depth, t), bf16),
            pltpu.SemaphoreType.DMA((len(groups_of(steps)),)),
            pltpu.SemaphoreType.DMA((2,)),
            pltpu.SemaphoreType.DMA((steps,)),
        ],
    )


def finish_kernel(n, cols, links, place_ref, *refs):
    z = place_ref[0]
    each = 2 + len(links)
    sum_refs, grad_refs, (out_ref, grad_ref, sv, gv, ov, ob, sems, o_sems) = (
        refs[: each * PARTS],
        refs[each * PARTS : each * PARTS + cols],
        refs[each * PARTS + cols :],
    )
    tr, pw = sv.shape[-2:]
    for p in range(PARTS):
        for i in range(each):
            ref = sum_refs[each * p + i]
            if i < 2:
                ref = ref.at[pl.ds(pl.multiple_of(z * tr, tr), tr), :]
            pltpu.make_async_copy(ref, sv.at[p, i], sems.at[p]).start()
    for k in range(cols):
        pltpu.make_async_copy(grad_refs[k], gv.at[k], sems.at[PARTS]).start()
    odd = lax.rem(z, 2)
    stores = []
    for p in range(PARTS):
        pltpu.make_async_copy(sv.at[p], sv.at[p], sems.at[p]).wait()
        total = sv[p, 0].astype(jnp.float32) + sv[p, 1].astype(jnp.float32)
        for i, link in enumerate(links):
            other = z + 1 - 2 * odd if link == 0 else z - 1 + 2 * odd
            came = sv[p, 2 + i].astype(jnp.float32)
            total += jnp.where((other >= 0) & (other < n), came, 0.0)
        ov[p] = total.astype(jnp.bfloat16)
        stores.append(pltpu.make_async_copy(ov.at[p], out_ref.at[:, pl.ds(p * pw, pw)], o_sems.at[p]))
        stores[-1].start()
    pltpu.make_async_copy(gv, gv, sems.at[PARTS]).wait()
    total = gv[0].astype(jnp.float32)
    for k in range(1, cols):
        total += gv[k].astype(jnp.float32)
    ob[...] = total.astype(jnp.bfloat16)
    stores.append(pltpu.make_async_copy(ob, grad_ref, o_sems.at[PARTS]))
    stores[-1].start()
    for copy in stores:
        copy.wait()


def finish(place, sums, grads, links, n):
    tr, pw = sums[0][-1].shape
    rows, depth = grads[0].shape
    cols = len(grads)
    bf16 = jnp.bfloat16
    return call(
        functools.partial(finish_kernel, n, cols, links),
        "finish",
        place,
        [v for part in sums for v in part] + grads,
        [jax.ShapeDtypeStruct((tr, pw * PARTS), bf16), jax.ShapeDtypeStruct((rows, depth), bf16)],
        [
            pltpu.VMEM((PARTS, 2 + len(links), tr, pw), bf16),
            pltpu.VMEM((cols, rows, depth), bf16),
            pltpu.VMEM((PARTS, tr, pw), bf16),
            pltpu.VMEM((rows, depth), bf16),
            pltpu.SemaphoreType.DMA((PARTS + 1,)),
            pltpu.SemaphoreType.DMA((PARTS + 1,)),
        ],
    )


def local(n, cols, inputs, weight, mask, cotangent):
    row, col = lax.axis_index("row"), lax.axis_index("col")
    z, core = row // 2, row % 2
    place = jnp.stack([z, core, col]).astype(jnp.int32)
    width = weight.shape[1]
    pw = width // PARTS
    tr = cotangent.shape[0]
    tokens = tr * 2 * n

    f32, bf16 = jnp.float32, jnp.bfloat16
    swap = lambda v: lax.ppermute(v, "row", [(i, i ^ 1) for i in range(2 * n)])
    across = lambda v, k: lax.ppermute(v, "col", [(i, i ^ k) for i in range(cols)])

    def pairs_of(link, ups, downs):
        pairs = [(i, i + 1) for i in ups if i % 2 == link and i + 1 < n]
        return pairs + [(i, i - 1) for i in downs if i % 2 != link and i > 0]

    def over(v, link, ups, downs):
        pairs = pairs_of(link, ups, downs)
        if not pairs:
            return None
        pairs = [(2 * i + c, 2 * j + c) for i, j in pairs for c in range(2)]
        if {i for i, _ in pairs} == {j for _, j in pairs}:
            pairs += [(i, i ^ 1) for i in sorted(set(range(2 * n)) - {i for i, _ in pairs})]
        return lax.ppermute(v, "row", pairs)

    even = z % 2 == 0

    xs = [inputs] + [across(inputs, k) for k in range(1, cols)]
    keep = jnp.repeat(mask.astype(f32), BLOCK, axis=1)
    came = [over(cotangent, link, range(n), range(n)) for link in range(2)]
    first = came
    pieces = [((0, 0, 0), cotangent), ((0, 0, 1), swap(cotangent))]

    def keep_pieces(s):
        have = [(link, v) for link, v in enumerate(came) if v is not None]
        if len(have) == 2 and 2 * s >= n:
            origin = jnp.where(even, z + s, z - s)
            have = [(2, jnp.where((origin >= 0) & (origin < n), *came))]
        for link, v in have:
            pieces.extend([((link, s, 0), v), ((link, s, 1), swap(v))])

    keep_pieces(1)

    mine, theirs = [], []
    for p in range(PARTS):
        m, other, *more = forward(place, xs, weight, keep, first if p else (), p, n, p == 0)
        whole = more[0] if more else whole
        mine.append(m)
        theirs.append(swap(other))
    xt = whole.T

    sums = [[None, None] for _ in range(PARTS)]
    sent = {}

    def slot(k, p, after):
        ups, downs = range(k - 1), range(n - k + 1, n)
        links = tuple(link for link in range(2) if pairs_of(link, ups, downs))
        sent[k, p] = send_sums(place, mine[p], theirs[p], sums[p], links, after, k, n)
        sums[p] = [None, None]
        for link, v in zip(links, sent[k, p]):
            sums[p][link] = over(v, link, ups, downs)

    after = ()
    for k in range(2, n + 1):
        if k < n:
            came = [
                None if came[1 - link] is None else over(came[1 - link], link, range(k - 1, n), range(n - k + 1))
                for link in range(2)
            ]
        slot(k, 0, after)
        after = sent[k, 0]
        if k == 2:
            came, after = lax.optimization_barrier((came, after))
            after = [*after, *(v for v in came if v is not None)]
        if k == n:
            late = [(i, v) for i, v in pieces if 2 * i[1] >= n]
            parts = late_rows(
                place, kinds, [i for i, _ in late], [v for _, v in late], weight, keep, early, after, n, cols
            )
            after = parts
        for p in range(1, PARTS):
            slot(k, p, after)
            after = sent[k, p]
        if k == 2:
            held = [(i, v) for i, v in pieces if 2 * i[1] < n]
            kinds = [i for i, _ in held]
            early = early_rows(place, n, kinds, [v for _, v in held], weight, keep, after)
            after = [early]
        elif k < n:
            after = [pause(place, after)]
            came, after = lax.optimization_barrier((came, after))
        if k < n:
            keep_pieces(k)
    grads = [parts[0]] + [across(parts[k], k) for k in range(1, cols)]
    wg = weight_grad(place, [k for k, _ in pieces], [v for _, v in pieces], xt, keep, n, width)
    links = [link for link in range(2) if sums[0][link] is not None]
    ends = [[mine[p], theirs[p], *(sums[p][link] for link in links)] for p in range(PARTS)]
    outputs, input_grad = finish(place, ends, grads, links, n)
    return outputs, input_grad, wg


def solution(mesh):
    n, cols = mesh.shape["row"] // 2, mesh.shape["col"]
    return jax.shard_map(
        functools.partial(local, n, cols),
        mesh=mesh,
        in_specs=(P("col", "row"), P("row", "col"), P("row", "col"), P("row", "col")),
        out_specs=(P("row", "col"), P("col", "row"), P("row", "col")),
        check_vma=False,
    )
```

time: 234 us -> 143 us (0.61); the launches traced: 230 us -> 142 us
  waiting for transfers between devices: 139 us -> 15 us
  Pallas kernels: 0 us -> 76 us
  matrix products: 58.4 us -> 0 us
  starting transfers between devices: 0.34 us -> 36.2 us
  between operations: 13.8 us -> 1.12 us
  local copies, waits for them, and re-layouts: 18.7 us -> 11.3 us
    all_gather x2 -> x0, waiting for transfers between devices: 78.5 us -> none  [the longest x1 76.2 us: local(): shard_rows = lax.all_gather(cotangent, 'row', axis=0, tiled=True)]
    pallas_call x0 -> x13, Pallas kernels: none -> 76 us  [call(): pl.pallas_call(body, grid_spec=pltpu.PrefetchScalarGridSpec(num_scalar_pr...]
    unnamed x6 -> x0, waiting for transfers between devices: 60.1 us -> none
    dot_general x3 -> x0, matrix products: 58.4 us -> none  [the longest x1 23.5 us: local(): jnp.dot(chosen, masked, preferred_element_type=jnp.float32)]
    ppermute x0 -> x28, starting transfers between devices: none -> 36.2 us  [the longest x15 25.1 us: over(): return lax.ppermute(v, 'row', pairs)]
    ppermute x0 -> x28, waiting for transfers between devices: none -> 15 us  [the longest x15 7.62 us: over(): return lax.ppermute(v, 'row', pairs)]
    broadcast_in_dim x1 -> x0, local copies, waits for them, and re-layouts: 7.15 us -> none  [expand_mask(): jnp.broadcast_to(mask_bf16[:, None, :, None], (tile_rows, BLOCK, tile_col...]
    unnamed x4 -> x26, local copies, waits for them, and re-layouts: 11.5 us -> 8.05 us
  transfers between devices with their start and end apart: 4 -> 28, of which waited for: 3 -> 4; matrix products, arithmetic and copies ran while one was open for 34% -> 4% of each run, Pallas kernels for 0% -> 51%
where the time goes in v3:
time: 143 us; the launch traced here: 142 us
  Pallas kernels  76 us (53%)
  starting transfers between devices  36.2 us (25%)
  waiting for transfers between devices  15 us (10%)
  local copies, waits for them, and re-layouts  11.3 us (8%)
  other arithmetic  2.36 us (2%)
    pallas_call x13, Pallas kernels, call(): pl.pallas_call(body, grid_spec=pltpu.PrefetchScalarGridSpec(num_scalar_pr...  76 us
    ppermute x15, starting transfers between devices, over(): return lax.ppermute(v, 'row', pairs)  25.1 us
    unnamed x26, local copies, waits for them, and re-layouts  8.05 us
    ppermute x15, waiting for transfers between devices, over(): return lax.ppermute(v, 'row', pairs)  7.62 us
    ppermute x6, waiting for transfers between devices, local(): lax.ppermute(v, 'col', [(i, i ^ k) for i in range(cols)])  7.39 us
    ppermute x6, starting transfers between devices, local(): lax.ppermute(v, 'col', [(i, i ^ k) for i in range(cols)])  6.14 us
    ppermute x7, starting transfers between devices, local(): swap = lambda v: lax.ppermute(v, 'row', [(i, i ^ 1) for i in range(2 * n)])  4.9 us
  transfers between devices with their start and end apart: 28, of which 4 were waited for; matrix products, arithmetic and copies ran while one was open for 4% of the time, Pallas kernels for 51%

profile of v3, /device:TPU:1, one launch (start us, length us, event | category | flops | bytes accessed | tf_op | source)
XLA Modules:
  0.0 142.0 jit_solution(15595072309715707804)
XLA Ops:
  0.6 3.1 %collective-permute-start.2 = (bf16[128,1024]{1,0:T(8,128)(2,1)}, bf16[128,1024]{1,0:T(8,128)(2,1)S(1)}, u32[]{:S(2)}, u32[]{:S(2)}) collective-permute-start(bf16[128,1024]{1,0:T(8,128)(2,1)} %refs_0_.5), channel_id=1, source_target_pairs={{0,3},{1,2},{2,1},{3,0},{4,7},{5,6},{6,5},{7,4},{8,11},{9,10},{10,... | collective-permute-start | bytes 786440 | tf_op jit(solution)/shard_map/ppermute | solution.py:480
  4.1 1.2 collective-permute-start.8
  5.3 1.5 %collective-permute-start.6 = (bf16[64,7168]{1,0:T(8,128)(2,1)}, bf16[64,7168]{1,0:T(8,128)(2,1)}, u32[]{:S(2)}, u32[]{:S(2)}) collective-permute-start(bf16[64,7168]{1,0:T(8,128)(2,1)} %refs_0_.7), channel_id=1, source_target_pairs={{0,8},{4,12},{16,24},{20,28},{8,0},{12,4},{24,16},{28,20},{1,9},{5... | collective-permute-start | bytes 2752520 | tf_op jit(solution)/shard_map/ppermute | solution.py:493
  6.8 0.7 convert_element_type.3
  7.5 0.8 broadcast_bitcast_fusion.refs_5_.refs_7_.refs_11_
  9.0 1.0 collective-permute-done.2.refs_3_
  10.0 6.4 %collective-permute-done.1.refs_2_ = bf16[128,1024]{1,0:T(8,128)(2,1)S(1)} collective-permute-done((bf16[128,1024]{1,0:T(8,128)(2,1)}, bf16[128,1024]{1,0:T(8,128)(2,1)S(1)}, u32[]{:S(2)}, u32[]{:S(2)}) %collective-permute-start.1) | collective-permute-done | bytes 262176 | tf_op jit(solution)/shard_map/ppermute | solution.py:480
  16.4 0.7 copy-done.11
  17.1 0.7 copy-done.12
  17.8 8.9 %forward.2 = (bf16[256,3584]{1,0:T(8,128)(2,1)}, bf16[256,3584]{1,0:T(8,128)(2,1)}, bf16[512,1024]{1,0:T(8,128)(2,1)}) custom-call(s32[3]{0:T(128)} %pad_add_fusion.place_ref, bf16[128,1024]{1,0:T(8,128)(2,1)} %refs_0_.5, bf16[128,1024]{1,0:T(8,128)(2,1)} %copy-done.12, bf16[128,1024]{1,0:T(8,128)(2,1)} %copy-done.11, bf16[128,1024]{1,0:T(8,128)(2,1)} %copy-done.10, ...), custom_call_target="tpu_custom_call" | custom-call | flops 99999997952 | bytes 99999997952 | tf_op jit(solution)/shard_map/forward/pallas_call | solution.py:87
  27.2 1.3 collective-permute-start.11
  28.7 8.9 %forward.3 = (bf16[256,3584]{1,0:T(8,128)(2,1)}, bf16[256,3584]{1,0:T(8,128)(2,1)}) custom-call(s32[3]{0:T(128)} %pad_add_fusion.place_ref, bf16[128,1024]{1,0:T(8,128)(2,1)} %refs_0_.5, bf16[128,1024]{1,0:T(8,128)(2,1)} %copy-done.12, bf16[128,1024]{1,0:T(8,128)(2,1)} %copy-done.11, bf16[128,1024]{1,0:T(8,128)(2,1)} %copy-done.10, ...), custom_call_target="tpu_custom_call" | custom-call | flops 99999997952 | bytes 99999997952 | tf_op jit(solution)/shard_map/forward/pallas_call | solution.py:87
  38.1 2.3 %copy.8 = bf16[512,1024]{0,1:T(8,128)(2,1)} copy(bf16[512,1024]{1,0:T(8,128)(2,1)} %get-tuple-element.50) | data formatting | bytes 2097152 | tf_op jit(solution)/shard_map/forward/pallas_call | solution.py:87
  40.8 0.8 copy-done
  41.7 2.8 %send_sums.6.refs_2_ = bf16[64,3584]{1,0:T(8,128)(2,1)} custom-call(s32[3]{0:T(128)} %pad_add_fusion.place_ref, bf16[256,3584]{1,0:T(8,128)(2,1)} %get-tuple-element.27.refs_0_, bf16[256,3584]{1,0:T(8,128)(2,1)} %copy-done), custom_call_target="tpu_custom_call" | custom-call | flops 1 | bytes 1 | tf_op jit(solution)/shard_map/send_sums/pallas_call | solution.py:87
  44.4 6.7 %collective-permute-done.11.refs_3_ = bf16[64,7168]{1,0:T(8,128)(2,1)S(1)} collective-permute-done((bf16[64,7168]{1,0:T(8,128)(2,1)}, bf16[64,7168]{1,0:T(8,128)(2,1)S(1)}, u32[]{:S(2)}, u32[]{:S(2)}) %collective-permute-start.11) | collective-permute-done | bytes 917536 | tf_op jit(solution)/shard_map/ppermute | solution.py:493
  51.1 0.9 collective-permute-start.7
  52.0 3.8 %collective-permute-start.4 = (bf16[64,3584]{1,0:T(8,128)(2,1)}, bf16[64,3584]{1,0:T(8,128)(2,1)S(1)}, u32[]{:S(2)}, u32[]{:S(2)}) collective-permute-start(bf16[64,3584]{1,0:T(8,128)(2,1)} %send_sums.6.refs_2_), channel_id=1, source_target_pairs={{0,8},{4,12},{24,16},{28,20},{1,9},{5,13},{25,17},{29,21},{2,10},{... | collective-permute-start | bytes 1376264 | tf_op jit(solution)/shard_map/ppermute | solution.py:493
  55.9 1.0 broadcast_select_fusion.refs_0_.refs_6_
  56.9 1.3 collective-permute-start.15
  58.2 2.7 %send_sums.7.refs_8_ = bf16[64,3584]{1,0:T(8,128)(2,1)} custom-call(s32[3]{0:T(128)} %pad_add_fusion.place_ref, bf16[256,3584]{1,0:T(8,128)(2,1)} %get-tuple-element.29.refs_0_.refs_4_, bf16[256,3584]{1,0:T(8,128)(2,1)} %collective-permute-done.10.refs_1_.refs_5_, bf16[64,3584]{1,0:T(8,128)(2,1)} %send_sums.6.refs_2_, bf16[64,7168]{1,0:T(8,128)(2,1)} %copy-done.1, ...), custom_call_target="tpu_custom_call" | custom-call | flops 1 | bytes 1 | tf_op jit(solution)/shard_map/send_sums/pallas_call | solution.py:87
  61.0 1.3 collective-permute-start.21
  62.3 3.4 %collective-permute-start.16 = (bf16[64,3584]{1,0:T(8,128)(2,1)}, bf16[64,3584]{1,0:T(8,128)(2,1)S(1)}, u32[]{:S(2)}, u32[]{:S(2)}) collective-permute-start(bf16[64,3584]{1,0:T(8,128)(2,1)} %send_sums.7.refs_8_), channel_id=1, source_target_pairs={{0,8},{4,12},{24,16},{28,20},{1,9},{5,13},{25,17},{29,21},{2,10},{... | collective-permute-start | bytes 1376264 | tf_op jit(solution)/shard_map/ppermute | solution.py:493
  65.7 0.9 copy-done.4
  66.6 11.7 %early_rows.1.refs_3_.refs_6_ = bf16[384,1024]{1,0:T(8,128)(2,1)} custom-call(s32[3]{0:T(128)} %pad_add_fusion.place_ref, bf16[64,7168]{1,0:T(8,128)(2,1)} %refs_0_.7, bf16[64,7168]{1,0:T(8,128)(2,1)} %collective-permute-done.5.refs_1_, bf16[64,7168]{1,0:T(8,128)(2,1)} %collective-permute-done.6.refs_6_.refs_2_, bf16[64,7168]{1,0:T(8,128)(2,1)} %copy-done.4, ...), custom_call_target="tpu_custom_call" | custom-call | flops 99999997952 | bytes 99999997952 | tf_op jit(solution)/shard_map/early_rows/pallas_call | solution.py:87
  78.4 0.8 copy-done.2
  79.2 2.8 %send_sums.8 = (bf16[64,3584]{1,0:T(8,128)(2,1)}, bf16[64,3584]{1,0:T(8,128)(2,1)}) custom-call(s32[3]{0:T(128)} %pad_add_fusion.place_ref, bf16[256,3584]{1,0:T(8,128)(2,1)} %get-tuple-element.27.refs_0_, bf16[256,3584]{1,0:T(8,128)(2,1)} %copy-done, bf16[64,3584]{1,0:T(8,128)(2,1)} %copy-done.2, bf16[384,1024]{1,0:T(8,128)(2,1)} %early_rows.1.refs_3_.refs_6_), custom_call_target="tpu_custom_call" | custom-call | flops 1 | bytes 1 | tf_op jit(solution)/shard_map/send_sums/pallas_call | solution.py:87
  82.0 2.3 %collective-permute-start.13 = (bf16[64,3584]{1,0:T(8,128)(2,1)}, bf16[64,3584]{1,0:T(8,128)(2,1)S(1)}, u32[]{:S(2)}, u32[]{:S(2)}) collective-permute-start(bf16[64,3584]{1,0:T(8,128)(2,1)} %get-tuple-element.34.refs_3_), channel_id=1, source_target_pairs={{0,8},{4,12},{24,16},{28,20},{1,9},{5,13},{25,17},{29,21},{2,10},{... | collective-permute-start | bytes 1376264 | tf_op jit(solution)/shard_map/ppermute | solution.py:493
  84.7 0.8 copy-done.3
  85.5 2.8 %send_sums.9 = (bf16[64,3584]{1,0:T(8,128)(2,1)}, bf16[64,3584]{1,0:T(8,128)(2,1)}) custom-call(s32[3]{0:T(128)} %pad_add_fusion.place_ref, bf16[256,3584]{1,0:T(8,128)(2,1)} %get-tuple-element.29.refs_0_.refs_4_, bf16[256,3584]{1,0:T(8,128)(2,1)} %collective-permute-done.10.refs_1_.refs_5_, bf16[64,3584]{1,0:T(8,128)(2,1)} %copy-done.3, ...), custom_call_target="tpu_custom_call" | custom-call | flops 1 | bytes 1 | tf_op jit(solution)/shard_map/send_sums/pallas_call | solution.py:87
  88.2 3.4 %collective-permute-start.19 = (bf16[64,3584]{1,0:T(8,128)(2,1)}, bf16[64,3584]{1,0:T(8,128)(2,1)}, u32[]{:S(2)}, u32[]{:S(2)}) collective-permute-start(bf16[64,3584]{1,0:T(8,128)(2,1)} %get-tuple-element.36.refs_0_), channel_id=1, source_target_pairs={{0,8},{4,12},{24,16},{28,20},{1,9},{5,13},{25,17},{29,21},{2,10},{... | collective-permute-start | bytes 1376264 | tf_op jit(solution)/shard_map/ppermute | solution.py:493
  91.6 1.3 pause.1.refs_4_
  93.6 0.9 collective-permute-done.13.refs_2_
  94.5 1.2 collective-permute-start.22
  95.7 0.8 copy-done.9
  96.5 2.9 %send_sums.10 = (bf16[64,3584]{1,0:T(8,128)(2,1)}, bf16[64,3584]{1,0:T(8,128)(2,1)}) custom-call(s32[3]{0:T(128)} %pad_add_fusion.place_ref, bf16[256,3584]{1,0:T(8,128)(2,1)} %get-tuple-element.27.refs_0_, bf16[256,3584]{1,0:T(8,128)(2,1)} %copy-done, bf16[64,3584]{1,0:T(8,128)(2,1)} %copy-done.8, bf16[64,3584]{1,0:T(8,128)(2,1)} %copy-done.9, ...), custom_call_target="tpu_custom_call" | custom-call | flops 99999997952 | bytes 99999997952 | tf_op jit(solution)/shard_map/send_sums/pallas_call | solution.py:87
  99.5 2.6 %collective-permute-start.17 = (bf16[64,3584]{1,0:T(8,128)(2,1)}, bf16[64,3584]{1,0:T(8,128)(2,1)}, u32[]{:S(2)}, u32[]{:S(2)}) collective-permute-start(bf16[64,3584]{1,0:T(8,128)(2,1)} %get-tuple-element.39.refs_7_), channel_id=1, source_target_pairs={{0,8},{4,12},{16,24},{20,28},{8,0},{12,4},{24,16},{28,20},{1,9},{5... | collective-permute-start | bytes 1376264 | tf_op jit(solution)/shard_map/ppermute | solution.py:493
  102.1 1.1 collective-permute-start.18
  103.1 1.0 copy-done.5
  104.1 11.2 %late_rows.1 = (bf16[128,1024]{1,0:T(8,128)(2,1)}, bf16[128,1024]{1,0:T(8,128)(2,1)}, bf16[128,1024]{1,0:T(8,128)(2,1)}, bf16[128,1024]{1,0:T(8,128)(2,1)}) custom-call(s32[3]{0:T(128)} %pad_add_fusion.place_ref, bf16[64,7168]{1,0:T(8,128)(2,1)} %broadcast_select_fusion.refs_0_.refs_6_, bf16[64,7168]{1,0:T(8,128)(2,1)} %collective-permute-done.21.refs_1_.refs_7_, ...), custom_call_target="tpu_custom_call" | custom-call | flops 99999997952 | bytes 99999997952 | tf_op jit(solution)/shard_map/late_rows/pallas_call | solution.py:87
  115.3 1.3 collective-permute-start.25
  117.2 0.9 collective-permute-start.27
  118.1 2.9 %send_sums.11 = (bf16[64,3584]{1,0:T(8,128)(2,1)}, bf16[64,3584]{1,0:T(8,128)(2,1)}) custom-call(s32[3]{0:T(128)} %pad_add_fusion.place_ref, bf16[256,3584]{1,0:T(8,128)(2,1)} %get-tuple-element.29.refs_0_.refs_4_, bf16[256,3584]{1,0:T(8,128)(2,1)} %collective-permute-done.10.refs_1_.refs_5_, bf16[64,3584]{1,0:T(8,128)(2,1)} %collective-permute-done.19.refs_2_, ...), custom_call_target="tpu_custom_call" | custom-call | flops 99999997952 | bytes 99999997952 | tf_op jit(solution)/shard_map/send_sums/pallas_call | solution.py:87
  121.1 1.9 %collective-permute-start.24 = (bf16[64,3584]{1,0:T(8,128)(2,1)}, bf16[64,3584]{1,0:T(8,128)(2,1)S(1)}, u32[]{:S(2)}, u32[]{:S(2)}) collective-permute-start(bf16[64,3584]{1,0:T(8,128)(2,1)} %get-tuple-element.47), channel_id=1, source_target_pairs={{8,16},{12,20},{16,8},{20,12},{0,4},{4,0},{24,28},{28,24},{9,17},{... | collective-permute-start | bytes 1376264 | tf_op jit(solution)/shard_map/ppermute | solution.py:493
  123.0 13.3 %weight_grad.1 = bf16[1024,7168]{1,0:T(8,128)(2,1)} custom-call(s32[3]{0:T(128)} %pad_add_fusion.place_ref, bf16[64,7168]{1,0:T(8,128)(2,1)} %refs_0_.7, bf16[64,7168]{1,0:T(8,128)(2,1)} %collective-permute-done.5.refs_1_, bf16[64,7168]{1,0:T(8,128)(2,1)} %collective-permute-done.6.refs_6_.refs_2_, bf16[64,7168]{1,0:T(8,128)(2,1)} %copy-done.4, ...), custom_call_target="tpu_custom_call" | custom-call | flops 99999997952 | bytes 99999997952 | tf_op jit(solution)/shard_map/weight_grad/pallas_call | solution.py:87
  136.4 0.8 copy-done.6
  137.1 0.8 copy-done.7
  138.0 3.8 %finish.1 = (bf16[64,7168]{1,0:T(8,128)(2,1)}, bf16[128,1024]{1,0:T(8,128)(2,1)}) custom-call(s32[3]{0:T(128)} %pad_add_fusion.place_ref, bf16[256,3584]{1,0:T(8,128)(2,1)} %get-tuple-element.27.refs_0_, bf16[256,3584]{1,0:T(8,128)(2,1)} %copy-done, bf16[64,3584]{1,0:T(8,128)(2,1)} %collective-permute-done.17.refs_2_, ...), custom_call_target="tpu_custom_call" | custom-call | flops 99999997952 | bytes 99999997952 | tf_op jit(solution)/shard_map/finish/pallas_call | solution.py:87
  (53 shorter events, 4.4 us)
Async XLA Ops:
  0.6 9.3 %collective-permute-start.2 = (bf16[128,1024]{1,0:T(8,128)(2,1)}, bf16[128,1024]{1,0:T(8,128)(2,1)S(1)}, u32[]{:S(2)}, u32[]{:S(2)}) collective-permute-start(bf16[128,1024]{1,0:T(8,128)(2,1)} %refs_0_.5), channel_id=1, source_target_pairs={{0,3},{1,2},{2,1},{3,0},{4,7},{5,6},{6,5},{7,4},{8,11},{9,10},{10,... | collective-permute-start | bytes 786440 | tf_op jit(solution)/shard_map/ppermute | solution.py:480
  3.7 12.7 %collective-permute-start.1 = (bf16[128,1024]{1,0:T(8,128)(2,1)}, bf16[128,1024]{1,0:T(8,128)(2,1)S(1)}, u32[]{:S(2)}, u32[]{:S(2)}) collective-permute-start(bf16[128,1024]{1,0:T(8,128)(2,1)} %refs_0_.5), channel_id=1, source_target_pairs={{0,2},{1,3},{2,0},{3,1},{4,6},{5,7},{6,4},{7,5},{8,10},{9,11},{10,... | collective-permute-start | bytes 786440 | tf_op jit(solution)/shard_map/ppermute | solution.py:480
  3.9 12.5 %collective-permute-start = (bf16[128,1024]{1,0:T(8,128)(2,1)}, bf16[128,1024]{1,0:T(8,128)(2,1)S(1)}, u32[]{:S(2)}, u32[]{:S(2)}) collective-permute-start(bf16[128,1024]{1,0:T(8,128)(2,1)} %refs_0_.5), channel_id=1, source_target_pairs={{0,1},{1,0},{2,3},{3,2},{4,5},{5,4},{6,7},{7,6},{8,9},{9,8},{10,11... | collective-permute-start | bytes 786440 | tf_op jit(solution)/shard_map/ppermute | solution.py:480
  4.1 23.1 %collective-permute-start.8 = (bf16[64,7168]{1,0:T(8,128)(2,1)}, bf16[64,7168]{1,0:T(8,128)(2,1)}, u32[]{:S(2)}, u32[]{:S(2)}) collective-permute-start(bf16[64,7168]{1,0:T(8,128)(2,1)} %refs_0_.7), channel_id=1, source_target_pairs={{8,16},{12,20},{16,8},{20,12},{0,4},{4,0},{24,28},{28,24},{9,17},{... | collective-permute-start | bytes 2752520 | tf_op jit(solution)/shard_map/ppermute | solution.py:493
  5.3 23.2 %collective-permute-start.6 = (bf16[64,7168]{1,0:T(8,128)(2,1)}, bf16[64,7168]{1,0:T(8,128)(2,1)}, u32[]{:S(2)}, u32[]{:S(2)}) collective-permute-start(bf16[64,7168]{1,0:T(8,128)(2,1)} %refs_0_.7), channel_id=1, source_target_pairs={{0,8},{4,12},{16,24},{20,28},{8,0},{12,4},{24,16},{28,20},{1,9},{5... | collective-permute-start | bytes 2752520 | tf_op jit(solution)/shard_map/ppermute | solution.py:493
  10.0 6.4 %copy-start.10 = (bf16[128,1024]{1,0:T(8,128)(2,1)}, bf16[128,1024]{1,0:T(8,128)(2,1)S(1)}, u32[]{:S(2)}) copy-start(bf16[128,1024]{1,0:T(8,128)(2,1)S(1)} %collective-permute-done.2.refs_3_) | copy-start | bytes 786436
  16.4 0.7 copy-start.11
  17.1 0.7 copy-start.12
  26.7 13.7 %collective-permute-start.3 = (bf16[256,3584]{1,0:T(8,128)(2,1)}, bf16[256,3584]{1,0:T(8,128)(2,1)S(1)}, u32[]{:S(2)}, u32[]{:S(2)}) collective-permute-start(bf16[256,3584]{1,0:T(8,128)(2,1)} %get-tuple-element.28), channel_id=1, source_target_pairs={{0,4},{4,0},{8,12},{12,8},{16,20},{20,16},{24,28},{28,24},{1,5},{5... | collective-permute-start | bytes 5505032 | tf_op jit(solution)/shard_map/ppermute | solution.py:479
  27.2 23.9 %collective-permute-start.11 = (bf16[64,7168]{1,0:T(8,128)(2,1)}, bf16[64,7168]{1,0:T(8,128)(2,1)S(1)}, u32[]{:S(2)}, u32[]{:S(2)}) collective-permute-start(bf16[64,7168]{1,0:T(8,128)(2,1)} %collective-permute-done.8.refs_7_.refs_4_), channel_id=1, source_target_pairs={{16,24},{20,28},{8,0},{12,4},{17,25},{21,29},{9,1},{13,5},{18,26},... | collective-permute-start | bytes 2752520 | tf_op jit(solution)/shard_map/ppermute | solution.py:493
  28.5 23.6 %collective-permute-start.12 = (bf16[64,7168]{1,0:T(8,128)(2,1)}, bf16[64,7168]{1,0:T(8,128)(2,1)}, u32[]{:S(2)}, u32[]{:S(2)}) collective-permute-start(bf16[64,7168]{1,0:T(8,128)(2,1)} %collective-permute-done.6.refs_6_.refs_2_), channel_id=1, source_target_pairs={{8,16},{12,20},{16,8},{20,12},{0,4},{4,0},{24,28},{28,24},{9,17},{... | collective-permute-start | bytes 2752520 | tf_op jit(solution)/shard_map/ppermute | solution.py:493
  37.5 19.4 %collective-permute-start.10 = (bf16[256,3584]{1,0:T(8,128)(2,1)}, bf16[256,3584]{1,0:T(8,128)(2,1)}, u32[]{:S(2)}, u32[]{:S(2)}) collective-permute-start(bf16[256,3584]{1,0:T(8,128)(2,1)} %get-tuple-element.30), channel_id=1, source_target_pairs={{0,4},{4,0},{8,12},{12,8},{16,20},{20,16},{24,28},{28,24},{1,5},{5... | collective-permute-start | bytes 5505032 | tf_op jit(solution)/shard_map/ppermute | solution.py:479
  38.0 23.0 %collective-permute-start.5 = (bf16[64,7168]{1,0:T(8,128)(2,1)}, bf16[64,7168]{1,0:T(8,128)(2,1)}, u32[]{:S(2)}, u32[]{:S(2)}) collective-permute-start(bf16[64,7168]{1,0:T(8,128)(2,1)} %refs_0_.7), channel_id=1, source_target_pairs={{0,4},{4,0},{8,12},{12,8},{16,20},{20,16},{24,28},{28,24},{1,5},{5... | collective-permute-start | bytes 2752520 | tf_op jit(solution)/shard_map/ppermute | solution.py:479
  40.4 1.2 copy-start
  40.4 21.8 %collective-permute-start.9 = (bf16[64,7168]{1,0:T(8,128)(2,1)}, bf16[64,7168]{1,0:T(8,128)(2,1)}, u32[]{:S(2)}, u32[]{:S(2)}) collective-permute-start(bf16[64,7168]{1,0:T(8,128)(2,1)} %collective-permute-done.8.refs_7_.refs_4_), channel_id=1, source_target_pairs={{0,4},{4,0},{8,12},{12,8},{16,20},{20,16},{24,28},{28,24},{1,5},{5... | collective-permute-start | bytes 2752520 | tf_op jit(solution)/shard_map/ppermute | solution.py:479
  51.1 7.1 %copy-start.1 = (bf16[64,7168]{1,0:T(8,128)(2,1)}, bf16[64,7168]{1,0:T(8,128)(2,1)S(1)}, u32[]{:S(2)}) copy-start(bf16[64,7168]{1,0:T(8,128)(2,1)S(1)} %collective-permute-done.11.refs_3_) | copy-start | bytes 2752516
  51.1 14.6 %collective-permute-start.7 = (bf16[64,7168]{1,0:T(8,128)(2,1)}, bf16[64,7168]{1,0:T(8,128)(2,1)S(1)}, u32[]{:S(2)}, u32[]{:S(2)}) collective-permute-start(bf16[64,7168]{1,0:T(8,128)(2,1)} %collective-permute-done.6.refs_6_.refs_2_), channel_id=1, source_target_pairs={{0,4},{4,0},{8,12},{12,8},{16,20},{20,16},{24,28},{28,24},{1,5},{5... | collective-permute-start | bytes 2752520 | tf_op jit(solution)/shard_map/ppermute | solution.py:479
  52.0 26.4 %collective-permute-start.4 = (bf16[64,3584]{1,0:T(8,128)(2,1)}, bf16[64,3584]{1,0:T(8,128)(2,1)S(1)}, u32[]{:S(2)}, u32[]{:S(2)}) collective-permute-start(bf16[64,3584]{1,0:T(8,128)(2,1)} %send_sums.6.refs_2_), channel_id=1, source_target_pairs={{0,8},{4,12},{24,16},{28,20},{1,9},{5,13},{25,17},{29,21},{2,10},{... | collective-permute-start | bytes 1376264 | tf_op jit(solution)/shard_map/ppermute | solution.py:493
  56.9 36.0 %collective-permute-start.15 = (bf16[64,7168]{1,0:T(8,128)(2,1)}, bf16[64,7168]{1,0:T(8,128)(2,1)}, u32[]{:S(2)}, u32[]{:S(2)}) collective-permute-start(bf16[64,7168]{1,0:T(8,128)(2,1)} %collective-permute-done.12.refs_4_), channel_id=1, source_target_pairs={{16,24},{20,28},{8,0},{12,4},{17,25},{21,29},{9,1},{13,5},{18,26},... | collective-permute-start | bytes 2752520 | tf_op jit(solution)/shard_map/ppermute | solution.py:493
  61.0 41.1 %collective-permute-start.21 = (bf16[64,7168]{1,0:T(8,128)(2,1)}, bf16[64,7168]{1,0:T(8,128)(2,1)}, u32[]{:S(2)}, u32[]{:S(2)}) collective-permute-start(bf16[64,7168]{1,0:T(8,128)(2,1)} %broadcast_select_fusion.refs_0_.refs_6_), channel_id=1, source_target_pairs={{0,4},{4,0},{8,12},{12,8},{16,20},{20,16},{24,28},{28,24},{1,5},{5... | collective-permute-start | bytes 2752520 | tf_op jit(solution)/shard_map/ppermute | solution.py:479
  62.3 22.4 %collective-permute-start.16 = (bf16[64,3584]{1,0:T(8,128)(2,1)}, bf16[64,3584]{1,0:T(8,128)(2,1)S(1)}, u32[]{:S(2)}, u32[]{:S(2)}) collective-permute-start(bf16[64,3584]{1,0:T(8,128)(2,1)} %send_sums.7.refs_8_), channel_id=1, source_target_pairs={{0,8},{4,12},{24,16},{28,20},{1,9},{5,13},{25,17},{29,21},{2,10},{... | collective-permute-start | bytes 1376264 | tf_op jit(solution)/shard_map/ppermute | solution.py:493
  65.7 0.9 copy-start.4
  78.4 0.8 copy-start.2
  82.0 12.5 %collective-permute-start.13 = (bf16[64,3584]{1,0:T(8,128)(2,1)}, bf16[64,3584]{1,0:T(8,128)(2,1)S(1)}, u32[]{:S(2)}, u32[]{:S(2)}) collective-permute-start(bf16[64,3584]{1,0:T(8,128)(2,1)} %get-tuple-element.34.refs_3_), channel_id=1, source_target_pairs={{0,8},{4,12},{24,16},{28,20},{1,9},{5,13},{25,17},{29,21},{2,10},{... | collective-permute-start | bytes 1376264 | tf_op jit(solution)/shard_map/ppermute | solution.py:493
  84.3 11.4 %collective-permute-start.14 = (bf16[64,3584]{1,0:T(8,128)(2,1)}, bf16[64,3584]{1,0:T(8,128)(2,1)S(1)}, u32[]{:S(2)}, u32[]{:S(2)}) collective-permute-start(bf16[64,3584]{1,0:T(8,128)(2,1)} %get-tuple-element.35.refs_4_), channel_id=1, source_target_pairs={{8,16},{12,20},{16,8},{20,12},{0,4},{4,0},{24,28},{28,24},{9,17},{... | collective-permute-start | bytes 1376264 | tf_op jit(solution)/shard_map/ppermute | solution.py:493
  84.7 0.8 copy-start.3
  88.2 28.4 %collective-permute-start.19 = (bf16[64,3584]{1,0:T(8,128)(2,1)}, bf16[64,3584]{1,0:T(8,128)(2,1)}, u32[]{:S(2)}, u32[]{:S(2)}) collective-permute-start(bf16[64,3584]{1,0:T(8,128)(2,1)} %get-tuple-element.36.refs_0_), channel_id=1, source_target_pairs={{0,8},{4,12},{24,16},{28,20},{1,9},{5,13},{25,17},{29,21},{2,10},{... | collective-permute-start | bytes 1376264 | tf_op jit(solution)/shard_map/ppermute | solution.py:493
  92.9 24.3 %collective-permute-start.20 = (bf16[64,3584]{1,0:T(8,128)(2,1)}, bf16[64,3584]{1,0:T(8,128)(2,1)}, u32[]{:S(2)}, u32[]{:S(2)}) collective-permute-start(bf16[64,3584]{1,0:T(8,128)(2,1)} %get-tuple-element.37.refs_1_), channel_id=1, source_target_pairs={{8,16},{12,20},{16,8},{20,12},{0,4},{4,0},{24,28},{28,24},{9,17},{... | collective-permute-start | bytes 1376264 | tf_op jit(solution)/shard_map/ppermute | solution.py:493
  94.5 1.2 copy-start.8
  94.5 8.7 %collective-permute-start.22 = (bf16[64,7168]{1,0:T(8,128)(2,1)}, bf16[64,7168]{1,0:T(8,128)(2,1)S(1)}, u32[]{:S(2)}, u32[]{:S(2)}) collective-permute-start(bf16[64,7168]{1,0:T(8,128)(2,1)} %collective-permute-done.15.refs_2_.refs_8_), channel_id=1, source_target_pairs={{0,4},{4,0},{8,12},{12,8},{16,20},{20,16},{24,28},{28,24},{1,5},{5... | collective-permute-start | bytes 2752520 | tf_op jit(solution)/shard_map/ppermute | solution.py:479
  95.7 0.8 copy-start.9
  99.5 21.5 %collective-permute-start.17 = (bf16[64,3584]{1,0:T(8,128)(2,1)}, bf16[64,3584]{1,0:T(8,128)(2,1)}, u32[]{:S(2)}, u32[]{:S(2)}) collective-permute-start(bf16[64,3584]{1,0:T(8,128)(2,1)} %get-tuple-element.39.refs_7_), channel_id=1, source_target_pairs={{0,8},{4,12},{16,24},{20,28},{8,0},{12,4},{24,16},{28,20},{1,9},{5... | collective-permute-start | bytes 1376264 | tf_op jit(solution)/shard_map/ppermute | solution.py:493
  102.1 19.0 %collective-permute-start.18 = (bf16[64,3584]{1,0:T(8,128)(2,1)}, bf16[64,3584]{1,0:T(8,128)(2,1)}, u32[]{:S(2)}, u32[]{:S(2)}) collective-permute-start(bf16[64,3584]{1,0:T(8,128)(2,1)} %get-tuple-element.40.refs_8_), channel_id=1, source_target_pairs={{8,16},{12,20},{16,8},{20,12},{0,4},{4,0},{24,28},{28,24},{9,17},{... | collective-permute-start | bytes 1376264 | tf_op jit(solution)/shard_map/ppermute | solution.py:493
  103.1 1.0 copy-start.5
  115.3 21.0 %collective-permute-start.25 = (bf16[128,1024]{1,0:T(8,128)(2,1)}, bf16[128,1024]{1,0:T(8,128)(2,1)}, u32[]{:S(2)}, u32[]{:S(2)}) collective-permute-start(bf16[128,1024]{1,0:T(8,128)(2,1)} %get-tuple-element.43.refs_5_), channel_id=1, source_target_pairs={{0,1},{1,0},{2,3},{3,2},{4,5},{5,4},{6,7},{7,6},{8,9},{9,8},{10,11... | collective-permute-start | bytes 786440 | tf_op jit(solution)/shard_map/ppermute | solution.py:480
  116.6 19.7 %collective-permute-start.26 = (bf16[128,1024]{1,0:T(8,128)(2,1)}, bf16[128,1024]{1,0:T(8,128)(2,1)}, u32[]{:S(2)}, u32[]{:S(2)}) collective-permute-start(bf16[128,1024]{1,0:T(8,128)(2,1)} %get-tuple-element.44.refs_6_), channel_id=1, source_target_pairs={{0,2},{1,3},{2,0},{3,1},{4,6},{5,7},{6,4},{7,5},{8,10},{9,11},{10,... | collective-permute-start | bytes 786440 | tf_op jit(solution)/shard_map/ppermute | solution.py:480
  117.2 19.2 %collective-permute-start.27 = (bf16[128,1024]{1,0:T(8,128)(2,1)}, bf16[128,1024]{1,0:T(8,128)(2,1)}, u32[]{:S(2)}, u32[]{:S(2)}) collective-permute-start(bf16[128,1024]{1,0:T(8,128)(2,1)} %get-tuple-element.45.refs_7_), channel_id=1, source_target_pairs={{0,3},{1,2},{2,1},{3,0},{4,7},{5,6},{6,5},{7,4},{8,11},{9,10},{10,... | collective-permute-start | bytes 786440 | tf_op jit(solution)/shard_map/ppermute | solution.py:480
  121.0 15.3 %collective-permute-start.23 = (bf16[64,3584]{1,0:T(8,128)(2,1)}, bf16[64,3584]{1,0:T(8,128)(2,1)S(1)}, u32[]{:S(2)}, u32[]{:S(2)}) collective-permute-start(bf16[64,3584]{1,0:T(8,128)(2,1)} %get-tuple-element.46), channel_id=1, source_target_pairs={{0,8},{4,12},{16,24},{20,28},{8,0},{12,4},{24,16},{28,20},{1,9},{5... | collective-permute-start | bytes 1376264 | tf_op jit(solution)/shard_map/ppermute | solution.py:493
  121.1 15.3 %collective-permute-start.24 = (bf16[64,3584]{1,0:T(8,128)(2,1)}, bf16[64,3584]{1,0:T(8,128)(2,1)S(1)}, u32[]{:S(2)}, u32[]{:S(2)}) collective-permute-start(bf16[64,3584]{1,0:T(8,128)(2,1)} %get-tuple-element.47), channel_id=1, source_target_pairs={{8,16},{12,20},{16,8},{20,12},{0,4},{4,0},{24,28},{28,24},{9,17},{... | collective-permute-start | bytes 1376264 | tf_op jit(solution)/shard_map/ppermute | solution.py:493
  136.4 0.8 copy-start.6
  137.1 0.8 copy-start.7

commit v4 on v3

--- a/solution.py
+++ b/solution.py
@@ -12,7 +12,7 @@
 AHEAD = 2
 ROWS_AHEAD = 4
 COST = 10 ** 11
-VMEM_LIMIT = 60 * 1024 * 1024
+VMEM_LIMIT = 64 * 1024 * 1024
 
 
 def tile_of(width):
@@ -144,6 +144,7 @@
             pltpu.SemaphoreType.DMA,
         ],
         after=after,
+        cost=COST if part else 1,
     )
 
 
@@ -331,7 +332,7 @@
     each_link(lambda i, link, d: pltpu.make_async_copy(ov.at[i], out_refs[i], o_sems.at[i]).wait())
 
 
-def send_sums(place, mine, theirs, came, links, after, k, n):
+def send_sums(place, mine, theirs, came, links, after, k, n, first):
     behind = tuple(link for link in range(2) if came[link] is not None)
     pw = mine.shape[1]
     tr = mine.shape[0] // n
@@ -350,7 +351,7 @@
             pltpu.SemaphoreType.DMA((len(links),)),
         ],
         after=after,
-        cost=1 if k < n else COST,
+        cost=COST if k == n and first else 1,
     )
 
 
@@ -524,7 +525,7 @@
     def slot(k, p, after):
         ups, downs = range(k - 1), range(n - k + 1, n)
         links = tuple(link for link in range(2) if pairs_of(link, ups, downs))
-        sent[k, p] = send_sums(place, mine[p], theirs[p], sums[p], links, after, k, n)
+        sent[k, p] = send_sums(place, mine[p], theirs[p], sums[p], links, after, k, n, p == 0)
         sums[p] = [None, None]
         for link, v in zip(links, sent[k, p]):
             sums[p][link] = over(v, link, ups, downs)
@@ -539,7 +540,10 @@
         slot(k, 0, after)
         after = sent[k, 0]
         if k == 2:
-            came, after = lax.optimization_barrier((came, after))
+            held = [(i, v) for i, v in pieces if 2 * i[1] < n]
+            kinds = [i for i, _ in held]
+            early = early_rows(place, n, kinds, [v for _, v in held], weight, keep, after)
+            came, after = lax.optimization_barrier((came, [early]))
             after = [*after, *(v for v in came if v is not None)]
         if k == n:
             late = [(i, v) for i, v in pieces if 2 * i[1] >= n]
@@ -550,12 +554,7 @@
         for p in range(1, PARTS):
             slot(k, p, after)
             after = sent[k, p]
-        if k == 2:
-            held = [(i, v) for i, v in pieces if 2 * i[1] < n]
-            kinds = [i for i, _ in held]
-            early = early_rows(place, n, kinds, [v for _, v in held], weight, keep, after)
-            after = [early]
-        elif k < n:
+        if 2 < k < n:
             after = [pause(place, after)]
             came, after = lax.optimization_barrier((came, after))
         if k < n:

time: 143 us -> 135 us (0.944)
  local copies, waits for them, and re-layouts: 11.3 us -> 3.2 us
  waiting for transfers between devices: 15 us -> 7.18 us
  starting transfers between devices: 36.2 us -> 43.2 us
    unnamed x26 -> x0, local copies, waits for them, and re-layouts: 8.05 us -> none
    ppermute x15, starting transfers between devices: 25.1 us -> 31.7 us  [over(): return lax.ppermute(v, 'row', pairs)]
    ppermute x15, waiting for transfers between devices: 7.62 us -> 1.75 us  [over(): return lax.ppermute(v, 'row', pairs)]
    ppermute x6, waiting for transfers between devices: 7.39 us -> 5.41 us  [local(): lax.ppermute(v, 'col', [(i, i ^ k) for i in range(cols)])]
  transfers between devices with their start and end apart: 28 -> 28, of which waited for: 4 -> 3; matrix products, arithmetic and copies ran while one was open for 4% -> 5% of each run, Pallas kernels for 51% -> 54%
where the time goes in v4:
time: 135 us; the launch traced here: 134 us
  Pallas kernels  75.8 us (56%)
  starting transfers between devices  43.2 us (32%)
  waiting for transfers between devices  7.18 us (5%)
  other arithmetic  3.47 us (3%)
  local copies, waits for them, and re-layouts  3.2 us (2%)
    pallas_call x13, Pallas kernels, call(): pl.pallas_call(body, grid_spec=pltpu.PrefetchScalarGridSpec(num_scalar_pr...  75.8 us
    ppermute x15, starting transfers between devices, over(): return lax.ppermute(v, 'row', pairs)  31.7 us
    ppermute x6, starting transfers between devices, local(): lax.ppermute(v, 'col', [(i, i ^ k) for i in range(cols)])  6.14 us
    ppermute x6, waiting for transfers between devices, local(): lax.ppermute(v, 'col', [(i, i ^ k) for i in range(cols)])  5.41 us
    ppermute x7, starting transfers between devices, local(): swap = lambda v: lax.ppermute(v, 'row', [(i, i ^ 1) for i in range(2 * n)])  5.37 us
  transfers between devices with their start and end apart: 28, of which 3 were waited for; matrix products, arithmetic and copies ran while one was open for 5% of the time, Pallas kernels for 54%

profile of v4, /device:TPU:1, one launch (start us, length us, event | category | flops | bytes accessed | tf_op | source)
XLA Modules:
  0.0 133.9 jit_solution(8758865439722379197)
XLA Ops:
  0.6 3.1 %collective-permute-start.2 = (bf16[128,1024]{1,0:T(8,128)(2,1)}, bf16[128,1024]{1,0:T(8,128)(2,1)}, u32[]{:S(2)}, u32[]{:S(2)}) collective-permute-start(bf16[128,1024]{1,0:T(8,128)(2,1)} %refs_0_.5), channel_id=1, source_target_pairs={{0,3},{1,2},{2,1},{3,0},{4,7},{5,6},{6,5},{7,4},{8,11},{9,10},{10,... | collective-permute-start | bytes 786440 | tf_op jit(solution)/shard_map/ppermute | solution.py:481
  3.7 0.2 collective-permute-start.1
  3.9 0.1 collective-permute-start
  4.1 1.2 collective-permute-start.6
  5.3 1.5 %collective-permute-start.5 = (bf16[64,7168]{1,0:T(8,128)(2,1)}, bf16[64,7168]{1,0:T(8,128)(2,1)}, u32[]{:S(2)}, u32[]{:S(2)}) collective-permute-start(bf16[64,7168]{1,0:T(8,128)(2,1)} %refs_0_.7), channel_id=1, source_target_pairs={{0,8},{4,12},{16,24},{20,28},{8,0},{12,4},{24,16},{28,20},{1,9},{5... | collective-permute-start | bytes 2752520 | tf_op jit(solution)/shard_map/ppermute | solution.py:494
  6.8 0.7 convert_element_type.3
  7.5 0.1 copy.7
  7.5 0.8 broadcast_bitcast_fusion.refs_5_.refs_7_.refs_11_
  8.4 0.6 pad_add_fusion.place_ref
  8.9 1.1 collective-permute-done.2.refs_3_
  10.1 2.1 %collective-permute-start.10 = (bf16[64,7168]{1,0:T(8,128)(2,1)}, bf16[64,7168]{1,0:T(8,128)(2,1)}, u32[]{:S(2)}, u32[]{:S(2)}) collective-permute-start(bf16[64,7168]{1,0:T(8,128)(2,1)} %refs_0_.7), channel_id=1, source_target_pairs={{0,4},{4,0},{8,12},{12,8},{16,20},{20,16},{24,28},{28,24},{1,5},{5... | collective-permute-start | bytes 2752520 | tf_op jit(solution)/shard_map/ppermute | solution.py:480
  12.1 4.3 %collective-permute-done.1.refs_2_ = bf16[128,1024]{1,0:T(8,128)(2,1)} collective-permute-done((bf16[128,1024]{1,0:T(8,128)(2,1)}, bf16[128,1024]{1,0:T(8,128)(2,1)}, u32[]{:S(2)}, u32[]{:S(2)}) %collective-permute-start.1) | collective-permute-done | bytes 262176 | tf_op jit(solution)/shard_map/ppermute | solution.py:481
  16.4 8.9 %forward.2 = (bf16[256,3584]{1,0:T(8,128)(2,1)}, bf16[256,3584]{1,0:T(8,128)(2,1)}, bf16[512,1024]{1,0:T(8,128)(2,1)}) custom-call(s32[3]{0:T(128)} %pad_add_fusion.place_ref, bf16[128,1024]{1,0:T(8,128)(2,1)} %refs_0_.5, bf16[128,1024]{1,0:T(8,128)(2,1)} %collective-permute-done.refs_1_, bf16[128,1024]{1,0:T(8,128)(2,1)} %collective-permute-done.1.refs_2_, ...), custom_call_target="tpu_custom_call" | custom-call | flops 1 | bytes 1 | tf_op jit(solution)/shard_map/forward/pallas_call | solution.py:87
  25.3 2.3 %copy.8 = bf16[512,1024]{0,1:T(8,128)(2,1)} copy(bf16[512,1024]{1,0:T(8,128)(2,1)} %get-tuple-element.50) | data formatting | bytes 2097152 | tf_op jit(solution)/shard_map/forward/pallas_call | solution.py:87
  27.6 0.8 collective-permute-start.3
  28.5 0.4 collective-permute-start.11
  28.9 8.8 %forward.3 = (bf16[256,3584]{1,0:T(8,128)(2,1)}, bf16[256,3584]{1,0:T(8,128)(2,1)}) custom-call(s32[3]{0:T(128)} %pad_add_fusion.place_ref, bf16[128,1024]{1,0:T(8,128)(2,1)} %refs_0_.5, bf16[128,1024]{1,0:T(8,128)(2,1)} %collective-permute-done.refs_1_, bf16[128,1024]{1,0:T(8,128)(2,1)} %collective-permute-done.1.refs_2_, ...), custom_call_target="tpu_custom_call" | custom-call | flops 99999997952 | bytes 99999997952 | tf_op jit(solution)/shard_map/forward/pallas_call | solution.py:87
  37.8 0.1 collective-permute-start.7
  37.9 1.3 collective-permute-start.8
  39.2 2.7 %send_sums.6.refs_8_ = bf16[64,3584]{1,0:T(8,128)(2,1)} custom-call(s32[3]{0:T(128)} %pad_add_fusion.place_ref, bf16[256,3584]{1,0:T(8,128)(2,1)} %get-tuple-element.27.refs_0_, bf16[256,3584]{1,0:T(8,128)(2,1)} %collective-permute-done.3.refs_1_), custom_call_target="tpu_custom_call" | custom-call | flops 1 | bytes 1 | tf_op jit(solution)/shard_map/send_sums/pallas_call | solution.py:87
  41.9 0.5 collective-permute-start.9
  42.4 5.7 %collective-permute-start.4 = (bf16[64,3584]{1,0:T(8,128)(2,1)}, bf16[64,3584]{1,0:T(8,128)(2,1)}, u32[]{:S(2)}, u32[]{:S(2)}) collective-permute-start(bf16[64,3584]{1,0:T(8,128)(2,1)} %send_sums.6.refs_8_), channel_id=1, source_target_pairs={{0,8},{4,12},{24,16},{28,20},{1,9},{5,13},{25,17},{29,21},{2,10},{... | collective-permute-start | bytes 1376264 | tf_op jit(solution)/shard_map/ppermute | solution.py:494
  48.1 11.7 %early_rows.1.refs_2_.refs_6_ = bf16[384,1024]{1,0:T(8,128)(2,1)} custom-call(s32[3]{0:T(128)} %pad_add_fusion.place_ref, bf16[64,7168]{1,0:T(8,128)(2,1)} %refs_0_.7, bf16[64,7168]{1,0:T(8,128)(2,1)} %collective-permute-done.10.refs_1_, bf16[64,7168]{1,0:T(8,128)(2,1)} %collective-permute-done.5.refs_6_.refs_2_, ...), custom_call_target="tpu_custom_call" | custom-call | flops 99999997952 | bytes 99999997952 | tf_op jit(solution)/shard_map/early_rows/pallas_call | solution.py:87
  59.9 1.7 %collective-permute-done.8.refs_3_ = bf16[64,7168]{1,0:T(8,128)(2,1)} collective-permute-done((bf16[64,7168]{1,0:T(8,128)(2,1)}, bf16[64,7168]{1,0:T(8,128)(2,1)}, u32[]{:S(2)}, u32[]{:S(2)}) %collective-permute-start.8) | collective-permute-done | bytes 917536 | tf_op jit(solution)/shard_map/ppermute | solution.py:494
  61.6 1.3 collective-permute-start.15
  62.9 2.7 %send_sums.7.refs_3_ = bf16[64,3584]{1,0:T(8,128)(2,1)} custom-call(s32[3]{0:T(128)} %pad_add_fusion.place_ref, bf16[256,3584]{1,0:T(8,128)(2,1)} %get-tuple-element.29.refs_0_.refs_4_, bf16[256,3584]{1,0:T(8,128)(2,1)} %collective-permute-done.7.refs_1_.refs_5_, bf16[384,1024]{1,0:T(8,128)(2,1)} %early_rows.1.refs_2_.refs_6_, ...), custom_call_target="tpu_custom_call" | custom-call | flops 1 | bytes 1 | tf_op jit(solution)/shard_map/send_sums/pallas_call | solution.py:87
  65.6 5.8 %collective-permute-start.16 = (bf16[64,3584]{1,0:T(8,128)(2,1)}, bf16[64,3584]{1,0:T(8,128)(2,1)}, u32[]{:S(2)}, u32[]{:S(2)}) collective-permute-start(bf16[64,3584]{1,0:T(8,128)(2,1)} %send_sums.7.refs_3_), channel_id=1, source_target_pairs={{0,8},{4,12},{24,16},{28,20},{1,9},{5,13},{25,17},{29,21},{2,10},{... | collective-permute-start | bytes 1376264 | tf_op jit(solution)/shard_map/ppermute | solution.py:494
  71.4 2.2 %broadcast_select_fusion.refs_0_.refs_6_ = bf16[64,7168]{1,0:T(8,128)(2,1)} fusion(bf16[64,7168]{1,0:T(8,128)(2,1)} %collective-permute-done.8.refs_3_, bf16[64,7168]{1,0:T(8,128)(2,1)} %collective-permute-done.9.refs_4_, pred[]{:T(512)S(6)} %and.22), kind=kLoop, calls=%fused_computation | loop fusion | flops 458752 | bytes 2752513 | tf_op jit(solution)/shard_map/jit(_where)/select_n | solution.py:508
  73.6 1.6 %collective-permute-start.21 = (bf16[64,7168]{1,0:T(8,128)(2,1)}, bf16[64,7168]{1,0:T(8,128)(2,1)}, u32[]{:S(2)}, u32[]{:S(2)}) collective-permute-start(bf16[64,7168]{1,0:T(8,128)(2,1)} %broadcast_select_fusion.refs_0_.refs_6_), channel_id=1, source_target_pairs={{0,4},{4,0},{8,12},{12,8},{16,20},{20,16},{24,28},{28,24},{1,5},{5... | collective-permute-start | bytes 2752520 | tf_op jit(solution)/shard_map/ppermute | solution.py:480
  75.2 2.8 %send_sums.8 = (bf16[64,3584]{1,0:T(8,128)(2,1)}, bf16[64,3584]{1,0:T(8,128)(2,1)}) custom-call(s32[3]{0:T(128)} %pad_add_fusion.place_ref, bf16[256,3584]{1,0:T(8,128)(2,1)} %get-tuple-element.27.refs_0_, bf16[256,3584]{1,0:T(8,128)(2,1)} %collective-permute-done.3.refs_1_, bf16[64,3584]{1,0:T(8,128)(2,1)} %collective-permute-done.4.refs_2_, ...), custom_call_target="tpu_custom_call" | custom-call | flops 1 | bytes 1 | tf_op jit(solution)/shard_map/send_sums/pallas_call | solution.py:87
  78.0 2.1 %collective-permute-start.13 = (bf16[64,3584]{1,0:T(8,128)(2,1)}, bf16[64,3584]{1,0:T(8,128)(2,1)}, u32[]{:S(2)}, u32[]{:S(2)}) collective-permute-start(bf16[64,3584]{1,0:T(8,128)(2,1)} %get-tuple-element.34.refs_3_), channel_id=1, source_target_pairs={{0,8},{4,12},{24,16},{28,20},{1,9},{5,13},{25,17},{29,21},{2,10},{... | collective-permute-start | bytes 1376264 | tf_op jit(solution)/shard_map/ppermute | solution.py:494
  80.1 2.7 %send_sums.9 = (bf16[64,3584]{1,0:T(8,128)(2,1)}, bf16[64,3584]{1,0:T(8,128)(2,1)}) custom-call(s32[3]{0:T(128)} %pad_add_fusion.place_ref, bf16[256,3584]{1,0:T(8,128)(2,1)} %get-tuple-element.29.refs_0_.refs_4_, bf16[256,3584]{1,0:T(8,128)(2,1)} %collective-permute-done.7.refs_1_.refs_5_, bf16[64,3584]{1,0:T(8,128)(2,1)} %collective-permute-done.16.refs_2_, ...), custom_call_target="tpu_custom_call" | custom-call | flops 1 | bytes 1 | tf_op jit(solution)/shard_map/send_sums/pallas_call | solution.py:87
  82.8 4.5 %collective-permute-start.19 = (bf16[64,3584]{1,0:T(8,128)(2,1)}, bf16[64,3584]{1,0:T(8,128)(2,1)}, u32[]{:S(2)}, u32[]{:S(2)}) collective-permute-start(bf16[64,3584]{1,0:T(8,128)(2,1)} %get-tuple-element.36.refs_0_), channel_id=1, source_target_pairs={{0,8},{4,12},{24,16},{28,20},{1,9},{5,13},{25,17},{29,21},{2,10},{... | collective-permute-start | bytes 1376264 | tf_op jit(solution)/shard_map/ppermute | solution.py:494
  87.3 1.3 pause.1.refs_4_
  88.6 3.6 %collective-permute-start.20 = (bf16[64,3584]{1,0:T(8,128)(2,1)}, bf16[64,3584]{1,0:T(8,128)(2,1)}, u32[]{:S(2)}, u32[]{:S(2)}) collective-permute-start(bf16[64,3584]{1,0:T(8,128)(2,1)} %get-tuple-element.37.refs_1_), channel_id=1, source_target_pairs={{8,16},{12,20},{16,8},{20,12},{0,4},{4,0},{24,28},{28,24},{9,17},{... | collective-permute-start | bytes 1376264 | tf_op jit(solution)/shard_map/ppermute | solution.py:494
  92.2 0.3 collective-permute-start.22
  92.5 3.0 %send_sums.10 = (bf16[64,3584]{1,0:T(8,128)(2,1)}, bf16[64,3584]{1,0:T(8,128)(2,1)}) custom-call(s32[3]{0:T(128)} %pad_add_fusion.place_ref, bf16[256,3584]{1,0:T(8,128)(2,1)} %get-tuple-element.27.refs_0_, bf16[256,3584]{1,0:T(8,128)(2,1)} %collective-permute-done.3.refs_1_, bf16[64,3584]{1,0:T(8,128)(2,1)} %collective-permute-done.13.refs_2_, ...), custom_call_target="tpu_custom_call" | custom-call | flops 99999997952 | bytes 99999997952 | tf_op jit(solution)/shard_map/send_sums/pallas_call | solution.py:87
  95.5 2.7 %collective-permute-start.17 = (bf16[64,3584]{1,0:T(8,128)(2,1)}, bf16[64,3584]{1,0:T(8,128)(2,1)}, u32[]{:S(2)}, u32[]{:S(2)}) collective-permute-start(bf16[64,3584]{1,0:T(8,128)(2,1)} %get-tuple-element.39.refs_7_), channel_id=1, source_target_pairs={{0,8},{4,12},{16,24},{20,28},{8,0},{12,4},{24,16},{28,20},{1,9},{5... | collective-permute-start | bytes 1376264 | tf_op jit(solution)/shard_map/ppermute | solution.py:494
  98.2 0.3 collective-permute-start.18
  98.5 11.0 %late_rows.1 = (bf16[128,1024]{1,0:T(8,128)(2,1)}, bf16[128,1024]{1,0:T(8,128)(2,1)}, bf16[128,1024]{1,0:T(8,128)(2,1)}, bf16[128,1024]{1,0:T(8,128)(2,1)}) custom-call(s32[3]{0:T(128)} %pad_add_fusion.place_ref, bf16[64,7168]{1,0:T(8,128)(2,1)} %broadcast_select_fusion.refs_0_.refs_6_, bf16[64,7168]{1,0:T(8,128)(2,1)} %collective-permute-done.21.refs_1_.refs_7_, ...), custom_call_target="tpu_custom_call" | custom-call | flops 99999997952 | bytes 99999997952 | tf_op jit(solution)/shard_map/late_rows/pallas_call | solution.py:87
  109.5 1.3 collective-permute-start.25
  110.7 1.0 collective-permute-start.26
  111.7 0.4 collective-permute-start.27
  112.2 3.0 %send_sums.11 = (bf16[64,3584]{1,0:T(8,128)(2,1)}, bf16[64,3584]{1,0:T(8,128)(2,1)}) custom-call(s32[3]{0:T(128)} %pad_add_fusion.place_ref, bf16[256,3584]{1,0:T(8,128)(2,1)} %get-tuple-element.29.refs_0_.refs_4_, bf16[256,3584]{1,0:T(8,128)(2,1)} %collective-permute-done.7.refs_1_.refs_5_, bf16[64,3584]{1,0:T(8,128)(2,1)} %collective-permute-done.19.refs_2_, ...), custom_call_target="tpu_custom_call" | custom-call | flops 1 | bytes 1 | tf_op jit(solution)/shard_map/send_sums/pallas_call | solution.py:87
  115.2 0.1 collective-permute-start.23
  115.3 1.3 collective-permute-start.24
  116.5 13.3 %weight_grad.1 = bf16[1024,7168]{1,0:T(8,128)(2,1)} custom-call(s32[3]{0:T(128)} %pad_add_fusion.place_ref, bf16[64,7168]{1,0:T(8,128)(2,1)} %refs_0_.7, bf16[64,7168]{1,0:T(8,128)(2,1)} %collective-permute-done.10.refs_1_, bf16[64,7168]{1,0:T(8,128)(2,1)} %collective-permute-done.5.refs_6_.refs_2_, bf16[64,7168]{1,0:T(8,128)(2,1)} %collective-permute-done.11.refs_3_, ...), custom_call_target="tpu_custom_call" | custom-call | flops 99999997952 | bytes 99999997952 | tf_op jit(solution)/shard_map/weight_grad/pallas_call | solution.py:87
  129.9 3.9 %finish.1 = (bf16[64,7168]{1,0:T(8,128)(2,1)}, bf16[128,1024]{1,0:T(8,128)(2,1)}) custom-call(s32[3]{0:T(128)} %pad_add_fusion.place_ref, bf16[256,3584]{1,0:T(8,128)(2,1)} %get-tuple-element.27.refs_0_, bf16[256,3584]{1,0:T(8,128)(2,1)} %collective-permute-done.3.refs_1_, bf16[64,3584]{1,0:T(8,128)(2,1)} %collective-permute-done.17.refs_2_, ...), custom_call_target="tpu_custom_call" | custom-call | flops 99999997952 | bytes 99999997952 | tf_op jit(solution)/shard_map/finish/pallas_call | solution.py:87
  (27 shorter events, 0.1 us)
Async XLA Ops:
  0.6 9.5 %collective-permute-start.2 = (bf16[128,1024]{1,0:T(8,128)(2,1)}, bf16[128,1024]{1,0:T(8,128)(2,1)}, u32[]{:S(2)}, u32[]{:S(2)}) collective-permute-start(bf16[128,1024]{1,0:T(8,128)(2,1)} %refs_0_.5), channel_id=1, source_target_pairs={{0,3},{1,2},{2,1},{3,0},{4,7},{5,6},{6,5},{7,4},{8,11},{9,10},{10,... | collective-permute-start | bytes 786440 | tf_op jit(solution)/shard_map/ppermute | solution.py:481
  3.7 12.7 %collective-permute-start.1 = (bf16[128,1024]{1,0:T(8,128)(2,1)}, bf16[128,1024]{1,0:T(8,128)(2,1)}, u32[]{:S(2)}, u32[]{:S(2)}) collective-permute-start(bf16[128,1024]{1,0:T(8,128)(2,1)} %refs_0_.5), channel_id=1, source_target_pairs={{0,2},{1,3},{2,0},{3,1},{4,6},{5,7},{6,4},{7,5},{8,10},{9,11},{10,... | collective-permute-start | bytes 786440 | tf_op jit(solution)/shard_map/ppermute | solution.py:481
  3.9 12.5 %collective-permute-start = (bf16[128,1024]{1,0:T(8,128)(2,1)}, bf16[128,1024]{1,0:T(8,128)(2,1)}, u32[]{:S(2)}, u32[]{:S(2)}) collective-permute-start(bf16[128,1024]{1,0:T(8,128)(2,1)} %refs_0_.5), channel_id=1, source_target_pairs={{0,1},{1,0},{2,3},{3,2},{4,5},{5,4},{6,7},{7,6},{8,9},{9,8},{10,11... | collective-permute-start | bytes 786440 | tf_op jit(solution)/shard_map/ppermute | solution.py:481
  4.1 24.3 %collective-permute-start.6 = (bf16[64,7168]{1,0:T(8,128)(2,1)}, bf16[64,7168]{1,0:T(8,128)(2,1)}, u32[]{:S(2)}, u32[]{:S(2)}) collective-permute-start(bf16[64,7168]{1,0:T(8,128)(2,1)} %refs_0_.7), channel_id=1, source_target_pairs={{8,16},{12,20},{16,8},{20,12},{0,4},{4,0},{24,28},{28,24},{9,17},{... | collective-permute-start | bytes 2752520 | tf_op jit(solution)/shard_map/ppermute | solution.py:494
  5.3 23.2 %collective-permute-start.5 = (bf16[64,7168]{1,0:T(8,128)(2,1)}, bf16[64,7168]{1,0:T(8,128)(2,1)}, u32[]{:S(2)}, u32[]{:S(2)}) collective-permute-start(bf16[64,7168]{1,0:T(8,128)(2,1)} %refs_0_.7), channel_id=1, source_target_pairs={{0,8},{4,12},{16,24},{20,28},{8,0},{12,4},{24,16},{28,20},{1,9},{5... | collective-permute-start | bytes 2752520 | tf_op jit(solution)/shard_map/ppermute | solution.py:494
  10.1 31.8 %collective-permute-start.10 = (bf16[64,7168]{1,0:T(8,128)(2,1)}, bf16[64,7168]{1,0:T(8,128)(2,1)}, u32[]{:S(2)}, u32[]{:S(2)}) collective-permute-start(bf16[64,7168]{1,0:T(8,128)(2,1)} %refs_0_.7), channel_id=1, source_target_pairs={{0,4},{4,0},{8,12},{12,8},{16,20},{20,16},{24,28},{28,24},{1,5},{5... | collective-permute-start | bytes 2752520 | tf_op jit(solution)/shard_map/ppermute | solution.py:480
  27.6 10.3 %collective-permute-start.3 = (bf16[256,3584]{1,0:T(8,128)(2,1)}, bf16[256,3584]{1,0:T(8,128)(2,1)}, u32[]{:S(2)}, u32[]{:S(2)}) collective-permute-start(bf16[256,3584]{1,0:T(8,128)(2,1)} %get-tuple-element.28), channel_id=1, source_target_pairs={{0,4},{4,0},{8,12},{12,8},{16,20},{20,16},{24,28},{28,24},{1,5},{5... | collective-permute-start | bytes 5505032 | tf_op jit(solution)/shard_map/ppermute | solution.py:480
  28.4 14.0 %collective-permute-start.12 = (bf16[64,7168]{1,0:T(8,128)(2,1)}, bf16[64,7168]{1,0:T(8,128)(2,1)}, u32[]{:S(2)}, u32[]{:S(2)}) collective-permute-start(bf16[64,7168]{1,0:T(8,128)(2,1)} %collective-permute-done.6.refs_7_.refs_4_), channel_id=1, source_target_pairs={{0,4},{4,0},{8,12},{12,8},{16,20},{20,16},{24,28},{28,24},{1,5},{5... | collective-permute-start | bytes 2752520 | tf_op jit(solution)/shard_map/ppermute | solution.py:480
  28.5 19.7 %collective-permute-start.11 = (bf16[64,7168]{1,0:T(8,128)(2,1)}, bf16[64,7168]{1,0:T(8,128)(2,1)}, u32[]{:S(2)}, u32[]{:S(2)}) collective-permute-start(bf16[64,7168]{1,0:T(8,128)(2,1)} %collective-permute-done.5.refs_6_.refs_2_), channel_id=1, source_target_pairs={{0,4},{4,0},{8,12},{12,8},{16,20},{20,16},{24,28},{28,24},{1,5},{5... | collective-permute-start | bytes 2752520 | tf_op jit(solution)/shard_map/ppermute | solution.py:480
  37.8 25.1 %collective-permute-start.7 = (bf16[256,3584]{1,0:T(8,128)(2,1)}, bf16[256,3584]{1,0:T(8,128)(2,1)}, u32[]{:S(2)}, u32[]{:S(2)}) collective-permute-start(bf16[256,3584]{1,0:T(8,128)(2,1)} %get-tuple-element.30), channel_id=1, source_target_pairs={{0,4},{4,0},{8,12},{12,8},{16,20},{20,16},{24,28},{28,24},{1,5},{5... | collective-permute-start | bytes 5505032 | tf_op jit(solution)/shard_map/ppermute | solution.py:480
  37.9 23.7 %collective-permute-start.8 = (bf16[64,7168]{1,0:T(8,128)(2,1)}, bf16[64,7168]{1,0:T(8,128)(2,1)}, u32[]{:S(2)}, u32[]{:S(2)}) collective-permute-start(bf16[64,7168]{1,0:T(8,128)(2,1)} %collective-permute-done.6.refs_7_.refs_4_), channel_id=1, source_target_pairs={{16,24},{20,28},{8,0},{12,4},{17,25},{21,29},{9,1},{13,5},{18,26},... | collective-permute-start | bytes 2752520 | tf_op jit(solution)/shard_map/ppermute | solution.py:494
  41.9 19.7 %collective-permute-start.9 = (bf16[64,7168]{1,0:T(8,128)(2,1)}, bf16[64,7168]{1,0:T(8,128)(2,1)}, u32[]{:S(2)}, u32[]{:S(2)}) collective-permute-start(bf16[64,7168]{1,0:T(8,128)(2,1)} %collective-permute-done.5.refs_6_.refs_2_), channel_id=1, source_target_pairs={{8,16},{12,20},{16,8},{20,12},{0,4},{4,0},{24,28},{28,24},{9,17},{... | collective-permute-start | bytes 2752520 | tf_op jit(solution)/shard_map/ppermute | solution.py:494
  42.4 32.8 %collective-permute-start.4 = (bf16[64,3584]{1,0:T(8,128)(2,1)}, bf16[64,3584]{1,0:T(8,128)(2,1)}, u32[]{:S(2)}, u32[]{:S(2)}) collective-permute-start(bf16[64,3584]{1,0:T(8,128)(2,1)} %send_sums.6.refs_8_), channel_id=1, source_target_pairs={{0,8},{4,12},{24,16},{28,20},{1,9},{5,13},{25,17},{29,21},{2,10},{... | collective-permute-start | bytes 1376264 | tf_op jit(solution)/shard_map/ppermute | solution.py:494
  61.6 27.0 %collective-permute-start.15 = (bf16[64,7168]{1,0:T(8,128)(2,1)}, bf16[64,7168]{1,0:T(8,128)(2,1)}, u32[]{:S(2)}, u32[]{:S(2)}) collective-permute-start(bf16[64,7168]{1,0:T(8,128)(2,1)} %collective-permute-done.9.refs_4_), channel_id=1, source_target_pairs={{16,24},{20,28},{8,0},{12,4},{17,25},{21,29},{9,1},{13,5},{18,26},... | collective-permute-start | bytes 2752520 | tf_op jit(solution)/shard_map/ppermute | solution.py:494
  65.6 14.4 %collective-permute-start.16 = (bf16[64,3584]{1,0:T(8,128)(2,1)}, bf16[64,3584]{1,0:T(8,128)(2,1)}, u32[]{:S(2)}, u32[]{:S(2)}) collective-permute-start(bf16[64,3584]{1,0:T(8,128)(2,1)} %send_sums.7.refs_3_), channel_id=1, source_target_pairs={{0,8},{4,12},{24,16},{28,20},{1,9},{5,13},{25,17},{29,21},{2,10},{... | collective-permute-start | bytes 1376264 | tf_op jit(solution)/shard_map/ppermute | solution.py:494
  73.6 24.5 %collective-permute-start.21 = (bf16[64,7168]{1,0:T(8,128)(2,1)}, bf16[64,7168]{1,0:T(8,128)(2,1)}, u32[]{:S(2)}, u32[]{:S(2)}) collective-permute-start(bf16[64,7168]{1,0:T(8,128)(2,1)} %broadcast_select_fusion.refs_0_.refs_6_), channel_id=1, source_target_pairs={{0,4},{4,0},{8,12},{12,8},{16,20},{20,16},{24,28},{28,24},{1,5},{5... | collective-permute-start | bytes 2752520 | tf_op jit(solution)/shard_map/ppermute | solution.py:480
  78.0 14.2 %collective-permute-start.13 = (bf16[64,3584]{1,0:T(8,128)(2,1)}, bf16[64,3584]{1,0:T(8,128)(2,1)}, u32[]{:S(2)}, u32[]{:S(2)}) collective-permute-start(bf16[64,3584]{1,0:T(8,128)(2,1)} %get-tuple-element.34.refs_3_), channel_id=1, source_target_pairs={{0,8},{4,12},{24,16},{28,20},{1,9},{5,13},{25,17},{29,21},{2,10},{... | collective-permute-start | bytes 1376264 | tf_op jit(solution)/shard_map/ppermute | solution.py:494
  80.1 12.5 %collective-permute-start.14 = (bf16[64,3584]{1,0:T(8,128)(2,1)}, bf16[64,3584]{1,0:T(8,128)(2,1)}, u32[]{:S(2)}, u32[]{:S(2)}) collective-permute-start(bf16[64,3584]{1,0:T(8,128)(2,1)} %get-tuple-element.35.refs_4_), channel_id=1, source_target_pairs={{8,16},{12,20},{16,8},{20,12},{0,4},{4,0},{24,28},{28,24},{9,17},{... | collective-permute-start | bytes 1376264 | tf_op jit(solution)/shard_map/ppermute | solution.py:494
  82.8 27.9 %collective-permute-start.19 = (bf16[64,3584]{1,0:T(8,128)(2,1)}, bf16[64,3584]{1,0:T(8,128)(2,1)}, u32[]{:S(2)}, u32[]{:S(2)}) collective-permute-start(bf16[64,3584]{1,0:T(8,128)(2,1)} %get-tuple-element.36.refs_0_), channel_id=1, source_target_pairs={{0,8},{4,12},{24,16},{28,20},{1,9},{5,13},{25,17},{29,21},{2,10},{... | collective-permute-start | bytes 1376264 | tf_op jit(solution)/shard_map/ppermute | solution.py:494
  88.6 23.2 %collective-permute-start.20 = (bf16[64,3584]{1,0:T(8,128)(2,1)}, bf16[64,3584]{1,0:T(8,128)(2,1)}, u32[]{:S(2)}, u32[]{:S(2)}) collective-permute-start(bf16[64,3584]{1,0:T(8,128)(2,1)} %get-tuple-element.37.refs_1_), channel_id=1, source_target_pairs={{8,16},{12,20},{16,8},{20,12},{0,4},{4,0},{24,28},{28,24},{9,17},{... | collective-permute-start | bytes 1376264 | tf_op jit(solution)/shard_map/ppermute | solution.py:494
  92.2 6.2 %collective-permute-start.22 = (bf16[64,7168]{1,0:T(8,128)(2,1)}, bf16[64,7168]{1,0:T(8,128)(2,1)}, u32[]{:S(2)}, u32[]{:S(2)}) collective-permute-start(bf16[64,7168]{1,0:T(8,128)(2,1)} %collective-permute-done.15.refs_2_.refs_8_), channel_id=1, source_target_pairs={{0,4},{4,0},{8,12},{12,8},{16,20},{20,16},{24,28},{28,24},{1,5},{5... | collective-permute-start | bytes 2752520 | tf_op jit(solution)/shard_map/ppermute | solution.py:480
  95.5 19.6 %collective-permute-start.17 = (bf16[64,3584]{1,0:T(8,128)(2,1)}, bf16[64,3584]{1,0:T(8,128)(2,1)}, u32[]{:S(2)}, u32[]{:S(2)}) collective-permute-start(bf16[64,3584]{1,0:T(8,128)(2,1)} %get-tuple-element.39.refs_7_), channel_id=1, source_target_pairs={{0,8},{4,12},{16,24},{20,28},{8,0},{12,4},{24,16},{28,20},{1,9},{5... | collective-permute-start | bytes 1376264 | tf_op jit(solution)/shard_map/ppermute | solution.py:494
  98.2 17.1 %collective-permute-start.18 = (bf16[64,3584]{1,0:T(8,128)(2,1)}, bf16[64,3584]{1,0:T(8,128)(2,1)}, u32[]{:S(2)}, u32[]{:S(2)}) collective-permute-start(bf16[64,3584]{1,0:T(8,128)(2,1)} %get-tuple-element.40.refs_8_), channel_id=1, source_target_pairs={{8,16},{12,20},{16,8},{20,12},{0,4},{4,0},{24,28},{28,24},{9,17},{... | collective-permute-start | bytes 1376264 | tf_op jit(solution)/shard_map/ppermute | solution.py:494
  109.5 20.4 %collective-permute-start.25 = (bf16[128,1024]{1,0:T(8,128)(2,1)}, bf16[128,1024]{1,0:T(8,128)(2,1)}, u32[]{:S(2)}, u32[]{:S(2)}) collective-permute-start(bf16[128,1024]{1,0:T(8,128)(2,1)} %get-tuple-element.43.refs_5_), channel_id=1, source_target_pairs={{0,1},{1,0},{2,3},{3,2},{4,5},{5,4},{6,7},{7,6},{8,9},{9,8},{10,11... | collective-permute-start | bytes 786440 | tf_op jit(solution)/shard_map/ppermute | solution.py:481
  110.7 19.1 %collective-permute-start.26 = (bf16[128,1024]{1,0:T(8,128)(2,1)}, bf16[128,1024]{1,0:T(8,128)(2,1)}, u32[]{:S(2)}, u32[]{:S(2)}) collective-permute-start(bf16[128,1024]{1,0:T(8,128)(2,1)} %get-tuple-element.44.refs_6_), channel_id=1, source_target_pairs={{0,2},{1,3},{2,0},{3,1},{4,6},{5,7},{6,4},{7,5},{8,10},{9,11},{10,... | collective-permute-start | bytes 786440 | tf_op jit(solution)/shard_map/ppermute | solution.py:481
  111.7 18.1 %collective-permute-start.27 = (bf16[128,1024]{1,0:T(8,128)(2,1)}, bf16[128,1024]{1,0:T(8,128)(2,1)}, u32[]{:S(2)}, u32[]{:S(2)}) collective-permute-start(bf16[128,1024]{1,0:T(8,128)(2,1)} %get-tuple-element.45.refs_7_), channel_id=1, source_target_pairs={{0,3},{1,2},{2,1},{3,0},{4,7},{5,6},{6,5},{7,4},{8,11},{9,10},{10,... | collective-permute-start | bytes 786440 | tf_op jit(solution)/shard_map/ppermute | solution.py:481
  115.2 14.7 %collective-permute-start.23 = (bf16[64,3584]{1,0:T(8,128)(2,1)}, bf16[64,3584]{1,0:T(8,128)(2,1)}, u32[]{:S(2)}, u32[]{:S(2)}) collective-permute-start(bf16[64,3584]{1,0:T(8,128)(2,1)} %get-tuple-element.46), channel_id=1, source_target_pairs={{0,8},{4,12},{16,24},{20,28},{8,0},{12,4},{24,16},{28,20},{1,9},{5... | collective-permute-start | bytes 1376264 | tf_op jit(solution)/shard_map/ppermute | solution.py:494
  115.3 14.6 %collective-permute-start.24 = (bf16[64,3584]{1,0:T(8,128)(2,1)}, bf16[64,3584]{1,0:T(8,128)(2,1)}, u32[]{:S(2)}, u32[]{:S(2)}) collective-permute-start(bf16[64,3584]{1,0:T(8,128)(2,1)} %get-tuple-element.47), channel_id=1, source_target_pairs={{8,16},{12,20},{16,8},{20,12},{0,4},{4,0},{24,28},{28,24},{9,17},{... | collective-permute-start | bytes 1376264 | tf_op jit(solution)/shard_map/ppermute | solution.py:494

commit v5 on v4

--- a/solution.py
+++ b/solution.py
@@ -101,26 +101,6 @@
     )(place, *args, *after)
 
 
-def pause_kernel(place_ref, out_ref, held, sem):
-    held[...] = jnp.zeros_like(held)
-    store = pltpu.make_async_copy(held, out_ref, sem)
-    store.start()
-    store.wait()
-
-
-def pause(place, after):
-    shape = (8, 128)
-    return call(
-        pause_kernel,
-        "pause",
-        place,
-        [],
-        jax.ShapeDtypeStruct(shape, jnp.float32),
-        [pltpu.VMEM(shape, jnp.float32), pltpu.SemaphoreType.DMA],
-        after=after,
-    )
-
-
 def forward(place, xs, weight, keep, after, part, n, emit):
     depth, width = weight.shape
     t = tile_of(width // PARTS)
@@ -517,7 +497,6 @@
         whole = more[0] if more else whole
         mine.append(m)
         theirs.append(swap(other))
-    xt = whole.T
 
     sums = [[None, None] for _ in range(PARTS)]
     sent = {}
@@ -542,9 +521,6 @@
         if k == 2:
             held = [(i, v) for i, v in pieces if 2 * i[1] < n]
             kinds = [i for i, _ in held]
-            early = early_rows(place, n, kinds, [v for _, v in held], weight, keep, after)
-            came, after = lax.optimization_barrier((came, [early]))
-            after = [*after, *(v for v in came if v is not None)]
         if k == n:
             late = [(i, v) for i, v in pieces if 2 * i[1] >= n]
             parts = late_rows(
@@ -554,11 +530,16 @@
         for p in range(1, PARTS):
             slot(k, p, after)
             after = sent[k, p]
-        if 2 < k < n:
-            after = [pause(place, after)]
+        if k == 2:
+            early = early_rows(place, n, kinds, [v for _, v in held], weight, keep, after)
+            after = [early]
+            came, after = lax.optimization_barrier((came, after))
+            after = [*after, *(v for v in came if v is not None)]
+        elif k < n:
             came, after = lax.optimization_barrier((came, after))
         if k < n:
             keep_pieces(k)
+    xt = lax.optimization_barrier((whole, sent[3, 0]))[0].T
     grads = [parts[0]] + [across(parts[k], k) for k in range(1, cols)]
     wg = weight_grad(place, [k for k, _ in pieces], [v for _, v in pieces], xt, keep, n, width)
     links = [link for link in range(2) if sums[0][link] is not None]

time: 135 us -> 132 us (0.978)
  starting transfers between devices: 43.2 us -> 38.8 us
  waiting for transfers between devices: 7.18 us -> 11.2 us
    ppermute x7, starting transfers between devices: 5.37 us -> 2.48 us  [local(): swap = lambda v: lax.ppermute(v, 'row', [(i, i ^ 1) for i in range(2 * n)])]
    ppermute x15, waiting for transfers between devices: 1.75 us -> 4.3 us  [over(): return lax.ppermute(v, 'row', pairs)]
    pallas_call x1 -> x0, local copies, waits for them, and re-layouts: 2.3 us -> none  [call(): pl.pallas_call(body, grid_spec=pltpu.PrefetchScalarGridSpec(num_scalar_pr...]
    ppermute x15, starting transfers between devices: 31.7 us -> 30.1 us  [over(): return lax.ppermute(v, 'row', pairs)]
    ppermute x6, waiting for transfers between devices: 5.41 us -> 6.9 us  [local(): lax.ppermute(v, 'col', [(i, i ^ k) for i in range(cols)])]
    pallas_call x13 -> x12, Pallas kernels: 75.8 us -> 74.5 us  [call(): pl.pallas_call(body, grid_spec=pltpu.PrefetchScalarGridSpec(num_scalar_pr...]
  transfers between devices with their start and end apart: 28 -> 28, of which waited for: 3 -> 4; matrix products, arithmetic and copies ran while one was open for 5% -> 4% of each run, Pallas kernels for 54% -> 54%
where the time goes in v5:
time: 132 us; the launch traced here: 131 us
  Pallas kernels  74.5 us (56%)
  starting transfers between devices  38.8 us (29%)
  waiting for transfers between devices  11.2 us (8%)
  other arithmetic  3.54 us (3%)
  local copies, waits for them, and re-layouts  2.2 us (2%)
    pallas_call x12, Pallas kernels, call(): pl.pallas_call(body, grid_spec=pltpu.PrefetchScalarGridSpec(num_scalar_pr...  74.5 us
    ppermute x15, starting transfers between devices, over(): return lax.ppermute(v, 'row', pairs)  30.1 us
    ppermute x6, waiting for transfers between devices, local(): lax.ppermute(v, 'col', [(i, i ^ k) for i in range(cols)])  6.9 us
    ppermute x6, starting transfers between devices, local(): lax.ppermute(v, 'col', [(i, i ^ k) for i in range(cols)])  6.14 us
    ppermute x15, waiting for transfers between devices, over(): return lax.ppermute(v, 'row', pairs)  4.3 us
  transfers between devices with their start and end apart: 28, of which 4 were waited for; matrix products, arithmetic and copies ran while one was open for 4% of the time, Pallas kernels for 54%

profile of v5, /device:TPU:1, one launch (start us, length us, event | category | flops | bytes accessed | tf_op | source)
XLA Modules:
  0.0 131.2 jit_solution(13477821227725077027)
XLA Ops:
  0.6 3.1 %collective-permute-start.2 = (bf16[128,1024]{1,0:T(8,128)(2,1)}, bf16[128,1024]{1,0:T(8,128)(2,1)}, u32[]{:S(2)}, u32[]{:S(2)}) collective-permute-start(bf16[128,1024]{1,0:T(8,128)(2,1)} %refs_0_.5), channel_id=1, source_target_pairs={{0,3},{1,2},{2,1},{3,0},{4,7},{5,6},{6,5},{7,4},{8,11},{9,10},{10,... | collective-permute-start | bytes 786440 | tf_op jit(solution)/shard_map/ppermute | solution.py:461
  3.7 0.2 collective-permute-start.1
  3.9 0.1 collective-permute-start
  4.1 1.4 %collective-permute-start.7 = (bf16[64,7168]{1,0:T(8,128)(2,1)}, bf16[64,7168]{1,0:T(8,128)(2,1)}, u32[]{:S(2)}, u32[]{:S(2)}) collective-permute-start(bf16[64,7168]{1,0:T(8,128)(2,1)} %refs_0_.7), channel_id=1, source_target_pairs={{0,8},{4,12},{16,24},{20,28},{8,0},{12,4},{24,16},{28,20},{1,9},{5... | collective-permute-start | bytes 2752520 | tf_op jit(solution)/shard_map/ppermute | solution.py:474
  5.5 1.8 %collective-permute-start.5 = (bf16[64,7168]{1,0:T(8,128)(2,1)}, bf16[64,7168]{1,0:T(8,128)(2,1)}, u32[]{:S(2)}, u32[]{:S(2)}) collective-permute-start(bf16[64,7168]{1,0:T(8,128)(2,1)} %refs_0_.7), channel_id=1, source_target_pairs={{8,16},{12,20},{16,8},{20,12},{0,4},{4,0},{24,28},{28,24},{9,17},{... | collective-permute-start | bytes 2752520 | tf_op jit(solution)/shard_map/ppermute | solution.py:474
  7.3 0.7 convert_element_type.3
  8.0 0.1 copy.7
  8.0 0.8 broadcast_bitcast_fusion.refs_5_.refs_7_.refs_11_
  8.9 0.7 pad_add_fusion.place_ref
  9.5 0.6 collective-permute-done.2.refs_3_
  10.1 6.3 %collective-permute-done.1.refs_2_ = bf16[128,1024]{1,0:T(8,128)(2,1)} collective-permute-done((bf16[128,1024]{1,0:T(8,128)(2,1)}, bf16[128,1024]{1,0:T(8,128)(2,1)}, u32[]{:S(2)}, u32[]{:S(2)}) %collective-permute-start.1) | collective-permute-done | bytes 262176 | tf_op jit(solution)/shard_map/ppermute | solution.py:461
  16.4 8.9 %forward.2 = (bf16[256,3584]{1,0:T(8,128)(2,1)}, bf16[256,3584]{1,0:T(8,128)(2,1)}, bf16[512,1024]{1,0:T(8,128)(2,1)}) custom-call(s32[3]{0:T(128)} %pad_add_fusion.place_ref, bf16[128,1024]{1,0:T(8,128)(2,1)} %refs_0_.5, bf16[128,1024]{1,0:T(8,128)(2,1)} %collective-permute-done.refs_1_, bf16[128,1024]{1,0:T(8,128)(2,1)} %collective-permute-done.1.refs_2_, ...), custom_call_target="tpu_custom_call" | custom-call | flops 1 | bytes 1 | tf_op jit(solution)/shard_map/forward/pallas_call | solution.py:87
  25.3 0.8 collective-permute-start.3
  26.2 8.8 %forward.3 = (bf16[256,3584]{1,0:T(8,128)(2,1)}, bf16[256,3584]{1,0:T(8,128)(2,1)}) custom-call(s32[3]{0:T(128)} %pad_add_fusion.place_ref, bf16[128,1024]{1,0:T(8,128)(2,1)} %refs_0_.5, bf16[128,1024]{1,0:T(8,128)(2,1)} %collective-permute-done.refs_1_, bf16[128,1024]{1,0:T(8,128)(2,1)} %collective-permute-done.1.refs_2_, ...), custom_call_target="tpu_custom_call" | custom-call | flops 99999997952 | bytes 99999997952 | tf_op jit(solution)/shard_map/forward/pallas_call | solution.py:87
  35.0 1.0 collective-permute-start.12
  36.1 0.1 collective-permute-start.9
  36.1 0.4 collective-permute-start.10
  36.6 0.1 collective-permute-start.11
  36.7 0.4 collective-permute-start.8
  37.1 2.7 %send_sums.6.refs_2_ = bf16[64,3584]{1,0:T(8,128)(2,1)} custom-call(s32[3]{0:T(128)} %pad_add_fusion.place_ref, bf16[256,3584]{1,0:T(8,128)(2,1)} %get-tuple-element.29.refs_0_, bf16[256,3584]{1,0:T(8,128)(2,1)} %collective-permute-done.3.refs_1_), custom_call_target="tpu_custom_call" | custom-call | flops 1 | bytes 1 | tf_op jit(solution)/shard_map/send_sums/pallas_call | solution.py:87
  39.8 1.3 collective-permute-start.6
  41.1 2.7 %send_sums.7.refs_8_ = bf16[64,3584]{1,0:T(8,128)(2,1)} custom-call(s32[3]{0:T(128)} %pad_add_fusion.place_ref, bf16[256,3584]{1,0:T(8,128)(2,1)} %get-tuple-element.31.refs_0_.refs_4_, bf16[256,3584]{1,0:T(8,128)(2,1)} %collective-permute-done.12.refs_1_.refs_5_, bf16[64,3584]{1,0:T(8,128)(2,1)} %send_sums.6.refs_2_), custom_call_target="tpu_custom_call" | custom-call | flops 1 | bytes 1 | tf_op jit(solution)/shard_map/send_sums/pallas_call | solution.py:87
  43.9 4.1 %collective-permute-start.4 = (bf16[64,3584]{1,0:T(8,128)(2,1)}, bf16[64,3584]{1,0:T(8,128)(2,1)}, u32[]{:S(2)}, u32[]{:S(2)}) collective-permute-start(bf16[64,3584]{1,0:T(8,128)(2,1)} %send_sums.6.refs_2_), channel_id=1, source_target_pairs={{0,8},{4,12},{24,16},{28,20},{1,9},{5,13},{25,17},{29,21},{2,10},{... | collective-permute-start | bytes 1376264 | tf_op jit(solution)/shard_map/ppermute | solution.py:474
  48.0 2.0 %collective-permute-start.16 = (bf16[64,3584]{1,0:T(8,128)(2,1)}, bf16[64,3584]{1,0:T(8,128)(2,1)}, u32[]{:S(2)}, u32[]{:S(2)}) collective-permute-start(bf16[64,3584]{1,0:T(8,128)(2,1)} %send_sums.7.refs_8_), channel_id=1, source_target_pairs={{0,8},{4,12},{24,16},{28,20},{1,9},{5,13},{25,17},{29,21},{2,10},{... | collective-permute-start | bytes 1376264 | tf_op jit(solution)/shard_map/ppermute | solution.py:474
  50.1 11.7 %early_rows.1.refs_3_.refs_6_ = bf16[384,1024]{1,0:T(8,128)(2,1)} custom-call(s32[3]{0:T(128)} %pad_add_fusion.place_ref, bf16[64,7168]{1,0:T(8,128)(2,1)} %refs_0_.7, bf16[64,7168]{1,0:T(8,128)(2,1)} %collective-permute-done.9.refs_1_, bf16[64,7168]{1,0:T(8,128)(2,1)} %collective-permute-done.7.refs_6_.refs_2_, ...), custom_call_target="tpu_custom_call" | custom-call | flops 99999997952 | bytes 99999997952 | tf_op jit(solution)/shard_map/early_rows/pallas_call | solution.py:87
  61.8 2.6 %collective-permute-done.6.refs_4_ = bf16[64,7168]{1,0:T(8,128)(2,1)} collective-permute-done((bf16[64,7168]{1,0:T(8,128)(2,1)}, bf16[64,7168]{1,0:T(8,128)(2,1)}, u32[]{:S(2)}, u32[]{:S(2)}) %collective-permute-start.6) | collective-permute-done | bytes 917536 | tf_op jit(solution)/shard_map/ppermute | solution.py:474
  64.4 1.3 collective-permute-start.15
  65.7 2.8 %send_sums.8 = (bf16[64,3584]{1,0:T(8,128)(2,1)}, bf16[64,3584]{1,0:T(8,128)(2,1)}) custom-call(s32[3]{0:T(128)} %pad_add_fusion.place_ref, bf16[256,3584]{1,0:T(8,128)(2,1)} %get-tuple-element.29.refs_0_, bf16[256,3584]{1,0:T(8,128)(2,1)} %collective-permute-done.3.refs_1_, bf16[64,3584]{1,0:T(8,128)(2,1)} %collective-permute-done.4.refs_2_, ...), custom_call_target="tpu_custom_call" | custom-call | flops 1 | bytes 1 | tf_op jit(solution)/shard_map/send_sums/pallas_call | solution.py:87
  68.5 6.1 %collective-permute-start.13 = (bf16[64,3584]{1,0:T(8,128)(2,1)}, bf16[64,3584]{1,0:T(8,128)(2,1)}, u32[]{:S(2)}, u32[]{:S(2)}) collective-permute-start(bf16[64,3584]{1,0:T(8,128)(2,1)} %get-tuple-element.36.refs_3_), channel_id=1, source_target_pairs={{0,8},{4,12},{24,16},{28,20},{1,9},{5,13},{25,17},{29,21},{2,10},{... | collective-permute-start | bytes 1376264 | tf_op jit(solution)/shard_map/ppermute | solution.py:474
  74.5 1.4 %collective-permute-start.14 = (bf16[64,3584]{1,0:T(8,128)(2,1)}, bf16[64,3584]{1,0:T(8,128)(2,1)}, u32[]{:S(2)}, u32[]{:S(2)}) collective-permute-start(bf16[64,3584]{1,0:T(8,128)(2,1)} %get-tuple-element.37.refs_4_), channel_id=1, source_target_pairs={{8,16},{12,20},{16,8},{20,12},{0,4},{4,0},{24,28},{28,24},{9,17},{... | collective-permute-start | bytes 1376264 | tf_op jit(solution)/shard_map/ppermute | solution.py:474
  76.0 2.2 %broadcast_select_fusion.refs_0_.refs_6_ = bf16[64,7168]{1,0:T(8,128)(2,1)} fusion(bf16[64,7168]{1,0:T(8,128)(2,1)} %collective-permute-done.6.refs_4_, bf16[64,7168]{1,0:T(8,128)(2,1)} %collective-permute-done.8.refs_5_, pred[]{:T(512)S(6)} %and.22), kind=kLoop, calls=%fused_computation | loop fusion | flops 458752 | bytes 2752513 | tf_op jit(solution)/shard_map/jit(_where)/select_n | solution.py:488
  78.2 1.3 copy.8
  79.5 2.8 %send_sums.9 = (bf16[64,3584]{1,0:T(8,128)(2,1)}, bf16[64,3584]{1,0:T(8,128)(2,1)}) custom-call(s32[3]{0:T(128)} %pad_add_fusion.place_ref, bf16[256,3584]{1,0:T(8,128)(2,1)} %get-tuple-element.31.refs_0_.refs_4_, bf16[256,3584]{1,0:T(8,128)(2,1)} %collective-permute-done.12.refs_1_.refs_5_, bf16[64,3584]{1,0:T(8,128)(2,1)} %collective-permute-done.16.refs_2_, ...), custom_call_target="tpu_custom_call" | custom-call | flops 1 | bytes 1 | tf_op jit(solution)/shard_map/send_sums/pallas_call | solution.py:87
  82.3 3.6 %collective-permute-start.19 = (bf16[64,3584]{1,0:T(8,128)(2,1)}, bf16[64,3584]{1,0:T(8,128)(2,1)}, u32[]{:S(2)}, u32[]{:S(2)}) collective-permute-start(bf16[64,3584]{1,0:T(8,128)(2,1)} %get-tuple-element.40.refs_4_), channel_id=1, source_target_pairs={{0,8},{4,12},{24,16},{28,20},{1,9},{5,13},{25,17},{29,21},{2,10},{... | collective-permute-start | bytes 1376264 | tf_op jit(solution)/shard_map/ppermute | solution.py:474
  85.9 1.7 %collective-permute-done.15.refs_2_.refs_8_ = bf16[64,7168]{1,0:T(8,128)(2,1)} collective-permute-done((bf16[64,7168]{1,0:T(8,128)(2,1)}, bf16[64,7168]{1,0:T(8,128)(2,1)}, u32[]{:S(2)}, u32[]{:S(2)}) %collective-permute-start.15) | collective-permute-done | bytes 917536 | tf_op jit(solution)/shard_map/ppermute | solution.py:474
  87.6 1.8 %collective-permute-start.20 = (bf16[64,3584]{1,0:T(8,128)(2,1)}, bf16[64,3584]{1,0:T(8,128)(2,1)}, u32[]{:S(2)}, u32[]{:S(2)}) collective-permute-start(bf16[64,3584]{1,0:T(8,128)(2,1)} %get-tuple-element.41.refs_5_), channel_id=1, source_target_pairs={{8,16},{12,20},{16,8},{20,12},{0,4},{4,0},{24,28},{28,24},{9,17},{... | collective-permute-start | bytes 1376264 | tf_op jit(solution)/shard_map/ppermute | solution.py:474
  89.4 2.9 %send_sums.10 = (bf16[64,3584]{1,0:T(8,128)(2,1)}, bf16[64,3584]{1,0:T(8,128)(2,1)}) custom-call(s32[3]{0:T(128)} %pad_add_fusion.place_ref, bf16[256,3584]{1,0:T(8,128)(2,1)} %get-tuple-element.29.refs_0_, bf16[256,3584]{1,0:T(8,128)(2,1)} %collective-permute-done.3.refs_1_, bf16[64,3584]{1,0:T(8,128)(2,1)} %collective-permute-done.13.refs_2_, ...), custom_call_target="tpu_custom_call" | custom-call | flops 99999997952 | bytes 99999997952 | tf_op jit(solution)/shard_map/send_sums/pallas_call | solution.py:87
  92.3 1.8 %collective-permute-start.17 = (bf16[64,3584]{1,0:T(8,128)(2,1)}, bf16[64,3584]{1,0:T(8,128)(2,1)}, u32[]{:S(2)}, u32[]{:S(2)}) collective-permute-start(bf16[64,3584]{1,0:T(8,128)(2,1)} %get-tuple-element.42.refs_7_), channel_id=1, source_target_pairs={{0,8},{4,12},{16,24},{20,28},{8,0},{12,4},{24,16},{28,20},{1,9},{5... | collective-permute-start | bytes 1376264 | tf_op jit(solution)/shard_map/ppermute | solution.py:474
  94.1 0.3 collective-permute-start.18
  94.4 11.0 %late_rows.1 = (bf16[128,1024]{1,0:T(8,128)(2,1)}, bf16[128,1024]{1,0:T(8,128)(2,1)}, bf16[128,1024]{1,0:T(8,128)(2,1)}, bf16[128,1024]{1,0:T(8,128)(2,1)}) custom-call(s32[3]{0:T(128)} %pad_add_fusion.place_ref, bf16[64,7168]{1,0:T(8,128)(2,1)} %broadcast_select_fusion.refs_0_.refs_6_, bf16[64,7168]{1,0:T(8,128)(2,1)} %collective-permute-done.21.refs_1_.refs_7_, ...), custom_call_target="tpu_custom_call" | custom-call | flops 99999997952 | bytes 99999997952 | tf_op jit(solution)/shard_map/late_rows/pallas_call | solution.py:87
  105.4 1.3 collective-permute-start.25
  106.7 1.2 collective-permute-start.26
  107.9 0.2 collective-permute-start.27
  108.1 2.9 %send_sums.11 = (bf16[64,3584]{1,0:T(8,128)(2,1)}, bf16[64,3584]{1,0:T(8,128)(2,1)}) custom-call(s32[3]{0:T(128)} %pad_add_fusion.place_ref, bf16[256,3584]{1,0:T(8,128)(2,1)} %get-tuple-element.31.refs_0_.refs_4_, bf16[256,3584]{1,0:T(8,128)(2,1)} %collective-permute-done.12.refs_1_.refs_5_, bf16[64,3584]{1,0:T(8,128)(2,1)} %collective-permute-done.19.refs_2_, ...), custom_call_target="tpu_custom_call" | custom-call | flops 1 | bytes 1 | tf_op jit(solution)/shard_map/send_sums/pallas_call | solution.py:87
  111.1 0.6 collective-permute-start.23
  111.7 2.2 %collective-permute-start.24 = (bf16[64,3584]{1,0:T(8,128)(2,1)}, bf16[64,3584]{1,0:T(8,128)(2,1)}, u32[]{:S(2)}, u32[]{:S(2)}) collective-permute-start(bf16[64,3584]{1,0:T(8,128)(2,1)} %get-tuple-element.50), channel_id=1, source_target_pairs={{8,16},{12,20},{16,8},{20,12},{0,4},{4,0},{24,28},{28,24},{9,17},{... | collective-permute-start | bytes 1376264 | tf_op jit(solution)/shard_map/ppermute | solution.py:474
  113.8 13.3 %weight_grad.1 = bf16[1024,7168]{1,0:T(8,128)(2,1)} custom-call(s32[3]{0:T(128)} %pad_add_fusion.place_ref, bf16[64,7168]{1,0:T(8,128)(2,1)} %refs_0_.7, bf16[64,7168]{1,0:T(8,128)(2,1)} %collective-permute-done.9.refs_1_, bf16[64,7168]{1,0:T(8,128)(2,1)} %collective-permute-done.7.refs_6_.refs_2_, bf16[64,7168]{1,0:T(8,128)(2,1)} %collective-permute-done.10.refs_3_, ...), custom_call_target="tpu_custom_call" | custom-call | flops 99999997952 | bytes 99999997952 | tf_op jit(solution)/shard_map/weight_grad/pallas_call | solution.py:87
  127.2 3.8 %finish.1 = (bf16[64,7168]{1,0:T(8,128)(2,1)}, bf16[128,1024]{1,0:T(8,128)(2,1)}) custom-call(s32[3]{0:T(128)} %pad_add_fusion.place_ref, bf16[256,3584]{1,0:T(8,128)(2,1)} %get-tuple-element.29.refs_0_, bf16[256,3584]{1,0:T(8,128)(2,1)} %collective-permute-done.3.refs_1_, bf16[64,3584]{1,0:T(8,128)(2,1)} %collective-permute-done.17.refs_2_, ...), custom_call_target="tpu_custom_call" | custom-call | flops 99999997952 | bytes 99999997952 | tf_op jit(solution)/shard_map/finish/pallas_call | solution.py:87
  (28 shorter events, 0.1 us)
Async XLA Ops:
  0.6 9.5 %collective-permute-start.2 = (bf16[128,1024]{1,0:T(8,128)(2,1)}, bf16[128,1024]{1,0:T(8,128)(2,1)}, u32[]{:S(2)}, u32[]{:S(2)}) collective-permute-start(bf16[128,1024]{1,0:T(8,128)(2,1)} %refs_0_.5), channel_id=1, source_target_pairs={{0,3},{1,2},{2,1},{3,0},{4,7},{5,6},{6,5},{7,4},{8,11},{9,10},{10,... | collective-permute-start | bytes 786440 | tf_op jit(solution)/shard_map/ppermute | solution.py:461
  3.7 12.7 %collective-permute-start.1 = (bf16[128,1024]{1,0:T(8,128)(2,1)}, bf16[128,1024]{1,0:T(8,128)(2,1)}, u32[]{:S(2)}, u32[]{:S(2)}) collective-permute-start(bf16[128,1024]{1,0:T(8,128)(2,1)} %refs_0_.5), channel_id=1, source_target_pairs={{0,2},{1,3},{2,0},{3,1},{4,6},{5,7},{6,4},{7,5},{8,10},{9,11},{10,... | collective-permute-start | bytes 786440 | tf_op jit(solution)/shard_map/ppermute | solution.py:461
  3.9 12.5 %collective-permute-start = (bf16[128,1024]{1,0:T(8,128)(2,1)}, bf16[128,1024]{1,0:T(8,128)(2,1)}, u32[]{:S(2)}, u32[]{:S(2)}) collective-permute-start(bf16[128,1024]{1,0:T(8,128)(2,1)} %refs_0_.5), channel_id=1, source_target_pairs={{0,1},{1,0},{2,3},{3,2},{4,5},{5,4},{6,7},{7,6},{8,9},{9,8},{10,11... | collective-permute-start | bytes 786440 | tf_op jit(solution)/shard_map/ppermute | solution.py:461
  4.1 22.1 %collective-permute-start.7 = (bf16[64,7168]{1,0:T(8,128)(2,1)}, bf16[64,7168]{1,0:T(8,128)(2,1)}, u32[]{:S(2)}, u32[]{:S(2)}) collective-permute-start(bf16[64,7168]{1,0:T(8,128)(2,1)} %refs_0_.7), channel_id=1, source_target_pairs={{0,8},{4,12},{16,24},{20,28},{8,0},{12,4},{24,16},{28,20},{1,9},{5... | collective-permute-start | bytes 2752520 | tf_op jit(solution)/shard_map/ppermute | solution.py:474
  5.5 20.7 %collective-permute-start.5 = (bf16[64,7168]{1,0:T(8,128)(2,1)}, bf16[64,7168]{1,0:T(8,128)(2,1)}, u32[]{:S(2)}, u32[]{:S(2)}) collective-permute-start(bf16[64,7168]{1,0:T(8,128)(2,1)} %refs_0_.7), channel_id=1, source_target_pairs={{8,16},{12,20},{16,8},{20,12},{0,4},{4,0},{24,28},{28,24},{9,17},{... | collective-permute-start | bytes 2752520 | tf_op jit(solution)/shard_map/ppermute | solution.py:474
  25.3 11.3 %collective-permute-start.3 = (bf16[256,3584]{1,0:T(8,128)(2,1)}, bf16[256,3584]{1,0:T(8,128)(2,1)}, u32[]{:S(2)}, u32[]{:S(2)}) collective-permute-start(bf16[256,3584]{1,0:T(8,128)(2,1)} %get-tuple-element.30), channel_id=1, source_target_pairs={{0,4},{4,0},{8,12},{12,8},{16,20},{20,16},{24,28},{28,24},{1,5},{5... | collective-permute-start | bytes 5505032 | tf_op jit(solution)/shard_map/ppermute | solution.py:460
  35.0 4.8 %collective-permute-start.12 = (bf16[256,3584]{1,0:T(8,128)(2,1)}, bf16[256,3584]{1,0:T(8,128)(2,1)}, u32[]{:S(2)}, u32[]{:S(2)}) collective-permute-start(bf16[256,3584]{1,0:T(8,128)(2,1)} %get-tuple-element.32), channel_id=1, source_target_pairs={{0,4},{4,0},{8,12},{12,8},{16,20},{20,16},{24,28},{28,24},{1,5},{5... | collective-permute-start | bytes 5505032 | tf_op jit(solution)/shard_map/ppermute | solution.py:460
  36.1 7.8 %collective-permute-start.9 = (bf16[64,7168]{1,0:T(8,128)(2,1)}, bf16[64,7168]{1,0:T(8,128)(2,1)}, u32[]{:S(2)}, u32[]{:S(2)}) collective-permute-start(bf16[64,7168]{1,0:T(8,128)(2,1)} %refs_0_.7), channel_id=1, source_target_pairs={{0,4},{4,0},{8,12},{12,8},{16,20},{20,16},{24,28},{28,24},{1,5},{5... | collective-permute-start | bytes 2752520 | tf_op jit(solution)/shard_map/ppermute | solution.py:460
  36.1 11.9 %collective-permute-start.10 = (bf16[64,7168]{1,0:T(8,128)(2,1)}, bf16[64,7168]{1,0:T(8,128)(2,1)}, u32[]{:S(2)}, u32[]{:S(2)}) collective-permute-start(bf16[64,7168]{1,0:T(8,128)(2,1)} %collective-permute-done.7.refs_6_.refs_2_), channel_id=1, source_target_pairs={{0,4},{4,0},{8,12},{12,8},{16,20},{20,16},{24,28},{28,24},{1,5},{5... | collective-permute-start | bytes 2752520 | tf_op jit(solution)/shard_map/ppermute | solution.py:460
  36.6 13.5 %collective-permute-start.11 = (bf16[64,7168]{1,0:T(8,128)(2,1)}, bf16[64,7168]{1,0:T(8,128)(2,1)}, u32[]{:S(2)}, u32[]{:S(2)}) collective-permute-start(bf16[64,7168]{1,0:T(8,128)(2,1)} %collective-permute-done.5.refs_7_.refs_4_), channel_id=1, source_target_pairs={{0,4},{4,0},{8,12},{12,8},{16,20},{20,16},{24,28},{28,24},{1,5},{5... | collective-permute-start | bytes 2752520 | tf_op jit(solution)/shard_map/ppermute | solution.py:460
  36.7 25.2 %collective-permute-start.8 = (bf16[64,7168]{1,0:T(8,128)(2,1)}, bf16[64,7168]{1,0:T(8,128)(2,1)}, u32[]{:S(2)}, u32[]{:S(2)}) collective-permute-start(bf16[64,7168]{1,0:T(8,128)(2,1)} %collective-permute-done.7.refs_6_.refs_2_), channel_id=1, source_target_pairs={{8,16},{12,20},{16,8},{20,12},{0,4},{4,0},{24,28},{28,24},{9,17},{... | collective-permute-start | bytes 2752520 | tf_op jit(solution)/shard_map/ppermute | solution.py:474
  39.8 24.6 %collective-permute-start.6 = (bf16[64,7168]{1,0:T(8,128)(2,1)}, bf16[64,7168]{1,0:T(8,128)(2,1)}, u32[]{:S(2)}, u32[]{:S(2)}) collective-permute-start(bf16[64,7168]{1,0:T(8,128)(2,1)} %collective-permute-done.5.refs_7_.refs_4_), channel_id=1, source_target_pairs={{16,24},{20,28},{8,0},{12,4},{17,25},{21,29},{9,1},{13,5},{18,26},... | collective-permute-start | bytes 2752520 | tf_op jit(solution)/shard_map/ppermute | solution.py:474
  43.9 21.8 %collective-permute-start.4 = (bf16[64,3584]{1,0:T(8,128)(2,1)}, bf16[64,3584]{1,0:T(8,128)(2,1)}, u32[]{:S(2)}, u32[]{:S(2)}) collective-permute-start(bf16[64,3584]{1,0:T(8,128)(2,1)} %send_sums.6.refs_2_), channel_id=1, source_target_pairs={{0,8},{4,12},{24,16},{28,20},{1,9},{5,13},{25,17},{29,21},{2,10},{... | collective-permute-start | bytes 1376264 | tf_op jit(solution)/shard_map/ppermute | solution.py:474
  48.0 31.5 %collective-permute-start.16 = (bf16[64,3584]{1,0:T(8,128)(2,1)}, bf16[64,3584]{1,0:T(8,128)(2,1)}, u32[]{:S(2)}, u32[]{:S(2)}) collective-permute-start(bf16[64,3584]{1,0:T(8,128)(2,1)} %send_sums.7.refs_8_), channel_id=1, source_target_pairs={{0,8},{4,12},{24,16},{28,20},{1,9},{5,13},{25,17},{29,21},{2,10},{... | collective-permute-start | bytes 1376264 | tf_op jit(solution)/shard_map/ppermute | solution.py:474
  64.4 23.2 %collective-permute-start.15 = (bf16[64,7168]{1,0:T(8,128)(2,1)}, bf16[64,7168]{1,0:T(8,128)(2,1)}, u32[]{:S(2)}, u32[]{:S(2)}) collective-permute-start(bf16[64,7168]{1,0:T(8,128)(2,1)} %collective-permute-done.8.refs_5_), channel_id=1, source_target_pairs={{16,24},{20,28},{8,0},{12,4},{17,25},{21,29},{9,1},{13,5},{18,26},... | collective-permute-start | bytes 2752520 | tf_op jit(solution)/shard_map/ppermute | solution.py:474
  68.5 9.7 %copy-start = (bf16[512,1024]{1,0:T(8,128)(2,1)S(1)}, bf16[512,1024]{1,0:T(8,128)(2,1)}, u32[]{:S(2)}) copy-start(bf16[512,1024]{1,0:T(8,128)(2,1)} %get-tuple-element.54) | copy-start | bytes 3145732
  68.5 20.9 %collective-permute-start.13 = (bf16[64,3584]{1,0:T(8,128)(2,1)}, bf16[64,3584]{1,0:T(8,128)(2,1)}, u32[]{:S(2)}, u32[]{:S(2)}) collective-permute-start(bf16[64,3584]{1,0:T(8,128)(2,1)} %get-tuple-element.36.refs_3_), channel_id=1, source_target_pairs={{0,8},{4,12},{24,16},{28,20},{1,9},{5,13},{25,17},{29,21},{2,10},{... | collective-permute-start | bytes 1376264 | tf_op jit(solution)/shard_map/ppermute | solution.py:474
  74.5 14.8 %collective-permute-start.14 = (bf16[64,3584]{1,0:T(8,128)(2,1)}, bf16[64,3584]{1,0:T(8,128)(2,1)}, u32[]{:S(2)}, u32[]{:S(2)}) collective-permute-start(bf16[64,3584]{1,0:T(8,128)(2,1)} %get-tuple-element.37.refs_4_), channel_id=1, source_target_pairs={{8,16},{12,20},{16,8},{20,12},{0,4},{4,0},{24,28},{28,24},{9,17},{... | collective-permute-start | bytes 1376264 | tf_op jit(solution)/shard_map/ppermute | solution.py:474
  79.5 14.6 %collective-permute-start.21 = (bf16[64,7168]{1,0:T(8,128)(2,1)}, bf16[64,7168]{1,0:T(8,128)(2,1)}, u32[]{:S(2)}, u32[]{:S(2)}) collective-permute-start(bf16[64,7168]{1,0:T(8,128)(2,1)} %broadcast_select_fusion.refs_0_.refs_6_), channel_id=1, source_target_pairs={{0,4},{4,0},{8,12},{12,8},{16,20},{20,16},{24,28},{28,24},{1,5},{5... | collective-permute-start | bytes 2752520 | tf_op jit(solution)/shard_map/ppermute | solution.py:460
  82.3 24.4 %collective-permute-start.19 = (bf16[64,3584]{1,0:T(8,128)(2,1)}, bf16[64,3584]{1,0:T(8,128)(2,1)}, u32[]{:S(2)}, u32[]{:S(2)}) collective-permute-start(bf16[64,3584]{1,0:T(8,128)(2,1)} %get-tuple-element.40.refs_4_), channel_id=1, source_target_pairs={{0,8},{4,12},{24,16},{28,20},{1,9},{5,13},{25,17},{29,21},{2,10},{... | collective-permute-start | bytes 1376264 | tf_op jit(solution)/shard_map/ppermute | solution.py:474
  87.6 20.4 %collective-permute-start.20 = (bf16[64,3584]{1,0:T(8,128)(2,1)}, bf16[64,3584]{1,0:T(8,128)(2,1)}, u32[]{:S(2)}, u32[]{:S(2)}) collective-permute-start(bf16[64,3584]{1,0:T(8,128)(2,1)} %get-tuple-element.41.refs_5_), channel_id=1, source_target_pairs={{8,16},{12,20},{16,8},{20,12},{0,4},{4,0},{24,28},{28,24},{9,17},{... | collective-permute-start | bytes 1376264 | tf_op jit(solution)/shard_map/ppermute | solution.py:474
  89.4 5.1 %collective-permute-start.22 = (bf16[64,7168]{1,0:T(8,128)(2,1)}, bf16[64,7168]{1,0:T(8,128)(2,1)}, u32[]{:S(2)}, u32[]{:S(2)}) collective-permute-start(bf16[64,7168]{1,0:T(8,128)(2,1)} %collective-permute-done.15.refs_2_.refs_8_), channel_id=1, source_target_pairs={{0,4},{4,0},{8,12},{12,8},{16,20},{20,16},{24,28},{28,24},{1,5},{5... | collective-permute-start | bytes 2752520 | tf_op jit(solution)/shard_map/ppermute | solution.py:460
  92.3 18.8 %collective-permute-start.17 = (bf16[64,3584]{1,0:T(8,128)(2,1)}, bf16[64,3584]{1,0:T(8,128)(2,1)}, u32[]{:S(2)}, u32[]{:S(2)}) collective-permute-start(bf16[64,3584]{1,0:T(8,128)(2,1)} %get-tuple-element.42.refs_7_), channel_id=1, source_target_pairs={{0,8},{4,12},{16,24},{20,28},{8,0},{12,4},{24,16},{28,20},{1,9},{5... | collective-permute-start | bytes 1376264 | tf_op jit(solution)/shard_map/ppermute | solution.py:474
  94.1 17.6 %collective-permute-start.18 = (bf16[64,3584]{1,0:T(8,128)(2,1)}, bf16[64,3584]{1,0:T(8,128)(2,1)}, u32[]{:S(2)}, u32[]{:S(2)}) collective-permute-start(bf16[64,3584]{1,0:T(8,128)(2,1)} %get-tuple-element.43.refs_8_), channel_id=1, source_target_pairs={{8,16},{12,20},{16,8},{20,12},{0,4},{4,0},{24,28},{28,24},{9,17},{... | collective-permute-start | bytes 1376264 | tf_op jit(solution)/shard_map/ppermute | solution.py:474
  105.4 21.7 %collective-permute-start.25 = (bf16[128,1024]{1,0:T(8,128)(2,1)}, bf16[128,1024]{1,0:T(8,128)(2,1)}, u32[]{:S(2)}, u32[]{:S(2)}) collective-permute-start(bf16[128,1024]{1,0:T(8,128)(2,1)} %get-tuple-element.46.refs_5_), channel_id=1, source_target_pairs={{0,1},{1,0},{2,3},{3,2},{4,5},{5,4},{6,7},{7,6},{8,9},{9,8},{10,11... | collective-permute-start | bytes 786440 | tf_op jit(solution)/shard_map/ppermute | solution.py:461
  106.7 20.5 %collective-permute-start.26 = (bf16[128,1024]{1,0:T(8,128)(2,1)}, bf16[128,1024]{1,0:T(8,128)(2,1)}, u32[]{:S(2)}, u32[]{:S(2)}) collective-permute-start(bf16[128,1024]{1,0:T(8,128)(2,1)} %get-tuple-element.47.refs_6_), channel_id=1, source_target_pairs={{0,2},{1,3},{2,0},{3,1},{4,6},{5,7},{6,4},{7,5},{8,10},{9,11},{10,... | collective-permute-start | bytes 786440 | tf_op jit(solution)/shard_map/ppermute | solution.py:461
  107.9 19.2 %collective-permute-start.27 = (bf16[128,1024]{1,0:T(8,128)(2,1)}, bf16[128,1024]{1,0:T(8,128)(2,1)}, u32[]{:S(2)}, u32[]{:S(2)}) collective-permute-start(bf16[128,1024]{1,0:T(8,128)(2,1)} %get-tuple-element.48.refs_7_), channel_id=1, source_target_pairs={{0,3},{1,2},{2,1},{3,0},{4,7},{5,6},{6,5},{7,4},{8,11},{9,10},{10,... | collective-permute-start | bytes 786440 | tf_op jit(solution)/shard_map/ppermute | solution.py:461
  111.1 16.1 %collective-permute-start.23 = (bf16[64,3584]{1,0:T(8,128)(2,1)}, bf16[64,3584]{1,0:T(8,128)(2,1)}, u32[]{:S(2)}, u32[]{:S(2)}) collective-permute-start(bf16[64,3584]{1,0:T(8,128)(2,1)} %get-tuple-element.49), channel_id=1, source_target_pairs={{0,8},{4,12},{16,24},{20,28},{8,0},{12,4},{24,16},{28,20},{1,9},{5... | collective-permute-start | bytes 1376264 | tf_op jit(solution)/shard_map/ppermute | solution.py:474
  111.7 15.5 %collective-permute-start.24 = (bf16[64,3584]{1,0:T(8,128)(2,1)}, bf16[64,3584]{1,0:T(8,128)(2,1)}, u32[]{:S(2)}, u32[]{:S(2)}) collective-permute-start(bf16[64,3584]{1,0:T(8,128)(2,1)} %get-tuple-element.50), channel_id=1, source_target_pairs={{8,16},{12,20},{16,8},{20,12},{0,4},{4,0},{24,28},{28,24},{9,17},{... | collective-permute-start | bytes 1376264 | tf_op jit(solution)/shard_map/ppermute | solution.py:474

commit v6 on v5

--- a/solution.py
+++ b/solution.py
@@ -137,7 +137,7 @@
 
 
 def groups_of(steps):
-    ends = sorted({min(e, steps) for e in (1, 4, steps)})
+    ends = sorted({min(e, steps) for e in (2, steps)})
     return list(zip([0, *ends], ends))
 
 
@@ -339,9 +339,9 @@
     piece_refs, (xt_ref, keep_ref, out_ref, held, xt, kv, ov, sems, x_sems, o_sems) = refs[: len(pieces)], refs[len(pieces) :]
     steps, _, t = ov.shape
     loads = [pltpu.make_async_copy(xt_ref, xt, x_sems.at[0]), pltpu.make_async_copy(keep_ref, kv, x_sems.at[1])]
-    for copy in loads:
-        copy.start()
+    loads[0].start()
     start_pieces(n, place_ref, pieces, piece_refs, held, sems, t)
+    loads[1].start()
     groups = groups_of(steps)
     for copy in loads:
         copy.wait()

time: 132 us -> 132 us (level)
  no operation moved by 1% of the time
where the time goes in v6:
time: 132 us; the launch traced here: 131 us
  Pallas kernels  74.2 us (56%)
  starting transfers between devices  38.8 us (29%)
  waiting for transfers between devices  11.2 us (8%)
  other arithmetic  3.54 us (3%)
  local copies, waits for them, and re-layouts  2.2 us (2%)
    pallas_call x12, Pallas kernels, call(): pl.pallas_call(body, grid_spec=pltpu.PrefetchScalarGridSpec(num_scalar_pr...  74.2 us
    ppermute x15, starting transfers between devices, over(): return lax.ppermute(v, 'row', pairs)  30.1 us
    ppermute x6, waiting for transfers between devices, local(): lax.ppermute(v, 'col', [(i, i ^ k) for i in range(cols)])  6.9 us
    ppermute x6, starting transfers between devices, local(): lax.ppermute(v, 'col', [(i, i ^ k) for i in range(cols)])  6.14 us
    ppermute x15, waiting for transfers between devices, over(): return lax.ppermute(v, 'row', pairs)  4.3 us
  transfers between devices with their start and end apart: 28, of which 4 were waited for; matrix products, arithmetic and copies ran while one was open for 4% of the time, Pallas kernels for 54%

profile of v6, /device:TPU:1, one launch (start us, length us, event | category | flops | bytes accessed | tf_op | source)
XLA Modules:
  0.0 131.0 jit_solution(11140332721747685350)
XLA Ops:
  0.6 3.1 %collective-permute-start.2 = (bf16[128,1024]{1,0:T(8,128)(2,1)}, bf16[128,1024]{1,0:T(8,128)(2,1)}, u32[]{:S(2)}, u32[]{:S(2)}) collective-permute-start(bf16[128,1024]{1,0:T(8,128)(2,1)} %refs_0_.5), channel_id=1, source_target_pairs={{0,3},{1,2},{2,1},{3,0},{4,7},{5,6},{6,5},{7,4},{8,11},{9,10},{10,... | collective-permute-start | bytes 786440 | tf_op jit(solution)/shard_map/ppermute | solution.py:461
  3.7 0.2 collective-permute-start.1
  3.9 0.1 collective-permute-start
  4.1 1.4 %collective-permute-start.7 = (bf16[64,7168]{1,0:T(8,128)(2,1)}, bf16[64,7168]{1,0:T(8,128)(2,1)}, u32[]{:S(2)}, u32[]{:S(2)}) collective-permute-start(bf16[64,7168]{1,0:T(8,128)(2,1)} %refs_0_.7), channel_id=1, source_target_pairs={{0,8},{4,12},{16,24},{20,28},{8,0},{12,4},{24,16},{28,20},{1,9},{5... | collective-permute-start | bytes 2752520 | tf_op jit(solution)/shard_map/ppermute | solution.py:474
  5.5 1.8 %collective-permute-start.5 = (bf16[64,7168]{1,0:T(8,128)(2,1)}, bf16[64,7168]{1,0:T(8,128)(2,1)}, u32[]{:S(2)}, u32[]{:S(2)}) collective-permute-start(bf16[64,7168]{1,0:T(8,128)(2,1)} %refs_0_.7), channel_id=1, source_target_pairs={{8,16},{12,20},{16,8},{20,12},{0,4},{4,0},{24,28},{28,24},{9,17},{... | collective-permute-start | bytes 2752520 | tf_op jit(solution)/shard_map/ppermute | solution.py:474
  7.3 0.7 convert_element_type.3
  8.0 0.1 copy.7
  8.0 0.8 broadcast_bitcast_fusion.refs_5_.refs_7_.refs_11_
  8.9 0.7 pad_add_fusion.place_ref
  9.5 0.6 collective-permute-done.2.refs_3_
  10.1 6.3 %collective-permute-done.1.refs_2_ = bf16[128,1024]{1,0:T(8,128)(2,1)} collective-permute-done((bf16[128,1024]{1,0:T(8,128)(2,1)}, bf16[128,1024]{1,0:T(8,128)(2,1)}, u32[]{:S(2)}, u32[]{:S(2)}) %collective-permute-start.1) | collective-permute-done | bytes 262176 | tf_op jit(solution)/shard_map/ppermute | solution.py:461
  16.4 8.9 %forward.2 = (bf16[256,3584]{1,0:T(8,128)(2,1)}, bf16[256,3584]{1,0:T(8,128)(2,1)}, bf16[512,1024]{1,0:T(8,128)(2,1)}) custom-call(s32[3]{0:T(128)} %pad_add_fusion.place_ref, bf16[128,1024]{1,0:T(8,128)(2,1)} %refs_0_.5, bf16[128,1024]{1,0:T(8,128)(2,1)} %collective-permute-done.refs_1_, bf16[128,1024]{1,0:T(8,128)(2,1)} %collective-permute-done.1.refs_2_, ...), custom_call_target="tpu_custom_call" | custom-call | flops 1 | bytes 1 | tf_op jit(solution)/shard_map/forward/pallas_call | solution.py:87
  25.3 0.8 collective-permute-start.3
  26.2 8.8 %forward.3 = (bf16[256,3584]{1,0:T(8,128)(2,1)}, bf16[256,3584]{1,0:T(8,128)(2,1)}) custom-call(s32[3]{0:T(128)} %pad_add_fusion.place_ref, bf16[128,1024]{1,0:T(8,128)(2,1)} %refs_0_.5, bf16[128,1024]{1,0:T(8,128)(2,1)} %collective-permute-done.refs_1_, bf16[128,1024]{1,0:T(8,128)(2,1)} %collective-permute-done.1.refs_2_, ...), custom_call_target="tpu_custom_call" | custom-call | flops 99999997952 | bytes 99999997952 | tf_op jit(solution)/shard_map/forward/pallas_call | solution.py:87
  35.0 1.0 collective-permute-start.12
  36.1 0.1 collective-permute-start.9
  36.1 0.4 collective-permute-start.10
  36.6 0.1 collective-permute-start.11
  36.7 0.4 collective-permute-start.8
  37.1 2.7 %send_sums.6.refs_2_ = bf16[64,3584]{1,0:T(8,128)(2,1)} custom-call(s32[3]{0:T(128)} %pad_add_fusion.place_ref, bf16[256,3584]{1,0:T(8,128)(2,1)} %get-tuple-element.29.refs_0_, bf16[256,3584]{1,0:T(8,128)(2,1)} %collective-permute-done.3.refs_1_), custom_call_target="tpu_custom_call" | custom-call | flops 1 | bytes 1 | tf_op jit(solution)/shard_map/send_sums/pallas_call | solution.py:87
  39.8 1.3 collective-permute-start.6
  41.1 2.7 %send_sums.7.refs_8_ = bf16[64,3584]{1,0:T(8,128)(2,1)} custom-call(s32[3]{0:T(128)} %pad_add_fusion.place_ref, bf16[256,3584]{1,0:T(8,128)(2,1)} %get-tuple-element.31.refs_0_.refs_4_, bf16[256,3584]{1,0:T(8,128)(2,1)} %collective-permute-done.12.refs_1_.refs_5_, bf16[64,3584]{1,0:T(8,128)(2,1)} %send_sums.6.refs_2_), custom_call_target="tpu_custom_call" | custom-call | flops 1 | bytes 1 | tf_op jit(solution)/shard_map/send_sums/pallas_call | solution.py:87
  43.9 4.1 %collective-permute-start.4 = (bf16[64,3584]{1,0:T(8,128)(2,1)}, bf16[64,3584]{1,0:T(8,128)(2,1)}, u32[]{:S(2)}, u32[]{:S(2)}) collective-permute-start(bf16[64,3584]{1,0:T(8,128)(2,1)} %send_sums.6.refs_2_), channel_id=1, source_target_pairs={{0,8},{4,12},{24,16},{28,20},{1,9},{5,13},{25,17},{29,21},{2,10},{... | collective-permute-start | bytes 1376264 | tf_op jit(solution)/shard_map/ppermute | solution.py:474
  48.0 2.0 %collective-permute-start.16 = (bf16[64,3584]{1,0:T(8,128)(2,1)}, bf16[64,3584]{1,0:T(8,128)(2,1)}, u32[]{:S(2)}, u32[]{:S(2)}) collective-permute-start(bf16[64,3584]{1,0:T(8,128)(2,1)} %send_sums.7.refs_8_), channel_id=1, source_target_pairs={{0,8},{4,12},{24,16},{28,20},{1,9},{5,13},{25,17},{29,21},{2,10},{... | collective-permute-start | bytes 1376264 | tf_op jit(solution)/shard_map/ppermute | solution.py:474
  50.1 11.7 %early_rows.1.refs_3_.refs_6_ = bf16[384,1024]{1,0:T(8,128)(2,1)} custom-call(s32[3]{0:T(128)} %pad_add_fusion.place_ref, bf16[64,7168]{1,0:T(8,128)(2,1)} %refs_0_.7, bf16[64,7168]{1,0:T(8,128)(2,1)} %collective-permute-done.9.refs_1_, bf16[64,7168]{1,0:T(8,128)(2,1)} %collective-permute-done.7.refs_6_.refs_2_, ...), custom_call_target="tpu_custom_call" | custom-call | flops 99999997952 | bytes 99999997952 | tf_op jit(solution)/shard_map/early_rows/pallas_call | solution.py:87
  61.8 2.6 %collective-permute-done.6.refs_4_ = bf16[64,7168]{1,0:T(8,128)(2,1)} collective-permute-done((bf16[64,7168]{1,0:T(8,128)(2,1)}, bf16[64,7168]{1,0:T(8,128)(2,1)}, u32[]{:S(2)}, u32[]{:S(2)}) %collective-permute-start.6) | collective-permute-done | bytes 917536 | tf_op jit(solution)/shard_map/ppermute | solution.py:474
  64.4 1.3 collective-permute-start.15
  65.7 2.8 %send_sums.8 = (bf16[64,3584]{1,0:T(8,128)(2,1)}, bf16[64,3584]{1,0:T(8,128)(2,1)}) custom-call(s32[3]{0:T(128)} %pad_add_fusion.place_ref, bf16[256,3584]{1,0:T(8,128)(2,1)} %get-tuple-element.29.refs_0_, bf16[256,3584]{1,0:T(8,128)(2,1)} %collective-permute-done.3.refs_1_, bf16[64,3584]{1,0:T(8,128)(2,1)} %collective-permute-done.4.refs_2_, ...), custom_call_target="tpu_custom_call" | custom-call | flops 1 | bytes 1 | tf_op jit(solution)/shard_map/send_sums/pallas_call | solution.py:87
  68.5 6.1 %collective-permute-start.13 = (bf16[64,3584]{1,0:T(8,128)(2,1)}, bf16[64,3584]{1,0:T(8,128)(2,1)}, u32[]{:S(2)}, u32[]{:S(2)}) collective-permute-start(bf16[64,3584]{1,0:T(8,128)(2,1)} %get-tuple-element.36.refs_3_), channel_id=1, source_target_pairs={{0,8},{4,12},{24,16},{28,20},{1,9},{5,13},{25,17},{29,21},{2,10},{... | collective-permute-start | bytes 1376264 | tf_op jit(solution)/shard_map/ppermute | solution.py:474
  74.5 1.4 %collective-permute-start.14 = (bf16[64,3584]{1,0:T(8,128)(2,1)}, bf16[64,3584]{1,0:T(8,128)(2,1)}, u32[]{:S(2)}, u32[]{:S(2)}) collective-permute-start(bf16[64,3584]{1,0:T(8,128)(2,1)} %get-tuple-element.37.refs_4_), channel_id=1, source_target_pairs={{8,16},{12,20},{16,8},{20,12},{0,4},{4,0},{24,28},{28,24},{9,17},{... | collective-permute-start | bytes 1376264 | tf_op jit(solution)/shard_map/ppermute | solution.py:474
  76.0 2.2 %broadcast_select_fusion.refs_0_.refs_6_ = bf16[64,7168]{1,0:T(8,128)(2,1)} fusion(bf16[64,7168]{1,0:T(8,128)(2,1)} %collective-permute-done.6.refs_4_, bf16[64,7168]{1,0:T(8,128)(2,1)} %collective-permute-done.8.refs_5_, pred[]{:T(512)S(6)} %and.22), kind=kLoop, calls=%fused_computation | loop fusion | flops 458752 | bytes 2752513 | tf_op jit(solution)/shard_map/jit(_where)/select_n | solution.py:488
  78.2 1.3 copy.8
  79.5 2.8 %send_sums.9 = (bf16[64,3584]{1,0:T(8,128)(2,1)}, bf16[64,3584]{1,0:T(8,128)(2,1)}) custom-call(s32[3]{0:T(128)} %pad_add_fusion.place_ref, bf16[256,3584]{1,0:T(8,128)(2,1)} %get-tuple-element.31.refs_0_.refs_4_, bf16[256,3584]{1,0:T(8,128)(2,1)} %collective-permute-done.12.refs_1_.refs_5_, bf16[64,3584]{1,0:T(8,128)(2,1)} %collective-permute-done.16.refs_2_, ...), custom_call_target="tpu_custom_call" | custom-call | flops 1 | bytes 1 | tf_op jit(solution)/shard_map/send_sums/pallas_call | solution.py:87
  82.3 3.6 %collective-permute-start.19 = (bf16[64,3584]{1,0:T(8,128)(2,1)}, bf16[64,3584]{1,0:T(8,128)(2,1)}, u32[]{:S(2)}, u32[]{:S(2)}) collective-permute-start(bf16[64,3584]{1,0:T(8,128)(2,1)} %get-tuple-element.40.refs_4_), channel_id=1, source_target_pairs={{0,8},{4,12},{24,16},{28,20},{1,9},{5,13},{25,17},{29,21},{2,10},{... | collective-permute-start | bytes 1376264 | tf_op jit(solution)/shard_map/ppermute | solution.py:474
  85.9 1.7 %collective-permute-done.15.refs_2_.refs_8_ = bf16[64,7168]{1,0:T(8,128)(2,1)} collective-permute-done((bf16[64,7168]{1,0:T(8,128)(2,1)}, bf16[64,7168]{1,0:T(8,128)(2,1)}, u32[]{:S(2)}, u32[]{:S(2)}) %collective-permute-start.15) | collective-permute-done | bytes 917536 | tf_op jit(solution)/shard_map/ppermute | solution.py:474
  87.6 1.8 %collective-permute-start.20 = (bf16[64,3584]{1,0:T(8,128)(2,1)}, bf16[64,3584]{1,0:T(8,128)(2,1)}, u32[]{:S(2)}, u32[]{:S(2)}) collective-permute-start(bf16[64,3584]{1,0:T(8,128)(2,1)} %get-tuple-element.41.refs_5_), channel_id=1, source_target_pairs={{8,16},{12,20},{16,8},{20,12},{0,4},{4,0},{24,28},{28,24},{9,17},{... | collective-permute-start | bytes 1376264 | tf_op jit(solution)/shard_map/ppermute | solution.py:474
  89.4 2.9 %send_sums.10 = (bf16[64,3584]{1,0:T(8,128)(2,1)}, bf16[64,3584]{1,0:T(8,128)(2,1)}) custom-call(s32[3]{0:T(128)} %pad_add_fusion.place_ref, bf16[256,3584]{1,0:T(8,128)(2,1)} %get-tuple-element.29.refs_0_, bf16[256,3584]{1,0:T(8,128)(2,1)} %collective-permute-done.3.refs_1_, bf16[64,3584]{1,0:T(8,128)(2,1)} %collective-permute-done.13.refs_2_, ...), custom_call_target="tpu_custom_call" | custom-call | flops 99999997952 | bytes 99999997952 | tf_op jit(solution)/shard_map/send_sums/pallas_call | solution.py:87
  92.3 1.8 %collective-permute-start.17 = (bf16[64,3584]{1,0:T(8,128)(2,1)}, bf16[64,3584]{1,0:T(8,128)(2,1)}, u32[]{:S(2)}, u32[]{:S(2)}) collective-permute-start(bf16[64,3584]{1,0:T(8,128)(2,1)} %get-tuple-element.42.refs_7_), channel_id=1, source_target_pairs={{0,8},{4,12},{16,24},{20,28},{8,0},{12,4},{24,16},{28,20},{1,9},{5... | collective-permute-start | bytes 1376264 | tf_op jit(solution)/shard_map/ppermute | solution.py:474
  94.1 0.3 collective-permute-start.18
  94.4 11.0 %late_rows.1 = (bf16[128,1024]{1,0:T(8,128)(2,1)}, bf16[128,1024]{1,0:T(8,128)(2,1)}, bf16[128,1024]{1,0:T(8,128)(2,1)}, bf16[128,1024]{1,0:T(8,128)(2,1)}) custom-call(s32[3]{0:T(128)} %pad_add_fusion.place_ref, bf16[64,7168]{1,0:T(8,128)(2,1)} %broadcast_select_fusion.refs_0_.refs_6_, bf16[64,7168]{1,0:T(8,128)(2,1)} %collective-permute-done.21.refs_1_.refs_7_, ...), custom_call_target="tpu_custom_call" | custom-call | flops 99999997952 | bytes 99999997952 | tf_op jit(solution)/shard_map/late_rows/pallas_call | solution.py:87
  105.4 1.3 collective-permute-start.25
  106.7 1.2 collective-permute-start.26
  107.9 0.2 collective-permute-start.27
  108.1 2.9 %send_sums.11 = (bf16[64,3584]{1,0:T(8,128)(2,1)}, bf16[64,3584]{1,0:T(8,128)(2,1)}) custom-call(s32[3]{0:T(128)} %pad_add_fusion.place_ref, bf16[256,3584]{1,0:T(8,128)(2,1)} %get-tuple-element.31.refs_0_.refs_4_, bf16[256,3584]{1,0:T(8,128)(2,1)} %collective-permute-done.12.refs_1_.refs_5_, bf16[64,3584]{1,0:T(8,128)(2,1)} %collective-permute-done.19.refs_2_, ...), custom_call_target="tpu_custom_call" | custom-call | flops 1 | bytes 1 | tf_op jit(solution)/shard_map/send_sums/pallas_call | solution.py:87
  111.1 0.6 collective-permute-start.23
  111.7 2.2 %collective-permute-start.24 = (bf16[64,3584]{1,0:T(8,128)(2,1)}, bf16[64,3584]{1,0:T(8,128)(2,1)}, u32[]{:S(2)}, u32[]{:S(2)}) collective-permute-start(bf16[64,3584]{1,0:T(8,128)(2,1)} %get-tuple-element.50), channel_id=1, source_target_pairs={{8,16},{12,20},{16,8},{20,12},{0,4},{4,0},{24,28},{28,24},{9,17},{... | collective-permute-start | bytes 1376264 | tf_op jit(solution)/shard_map/ppermute | solution.py:474
  113.8 13.0 %weight_grad.1 = bf16[1024,7168]{1,0:T(8,128)(2,1)} custom-call(s32[3]{0:T(128)} %pad_add_fusion.place_ref, bf16[64,7168]{1,0:T(8,128)(2,1)} %refs_0_.7, bf16[64,7168]{1,0:T(8,128)(2,1)} %collective-permute-done.9.refs_1_, bf16[64,7168]{1,0:T(8,128)(2,1)} %collective-permute-done.7.refs_6_.refs_2_, bf16[64,7168]{1,0:T(8,128)(2,1)} %collective-permute-done.10.refs_3_, ...), custom_call_target="tpu_custom_call" | custom-call | flops 99999997952 | bytes 99999997952 | tf_op jit(solution)/shard_map/weight_grad/pallas_call | solution.py:87
  126.9 3.8 %finish.1 = (bf16[64,7168]{1,0:T(8,128)(2,1)}, bf16[128,1024]{1,0:T(8,128)(2,1)}) custom-call(s32[3]{0:T(128)} %pad_add_fusion.place_ref, bf16[256,3584]{1,0:T(8,128)(2,1)} %get-tuple-element.29.refs_0_, bf16[256,3584]{1,0:T(8,128)(2,1)} %collective-permute-done.3.refs_1_, bf16[64,3584]{1,0:T(8,128)(2,1)} %collective-permute-done.17.refs_2_, ...), custom_call_target="tpu_custom_call" | custom-call | flops 99999997952 | bytes 99999997952 | tf_op jit(solution)/shard_map/finish/pallas_call | solution.py:87
  (28 shorter events, 0.1 us)
Async XLA Ops:
  0.6 9.5 %collective-permute-start.2 = (bf16[128,1024]{1,0:T(8,128)(2,1)}, bf16[128,1024]{1,0:T(8,128)(2,1)}, u32[]{:S(2)}, u32[]{:S(2)}) collective-permute-start(bf16[128,1024]{1,0:T(8,128)(2,1)} %refs_0_.5), channel_id=1, source_target_pairs={{0,3},{1,2},{2,1},{3,0},{4,7},{5,6},{6,5},{7,4},{8,11},{9,10},{10,... | collective-permute-start | bytes 786440 | tf_op jit(solution)/shard_map/ppermute | solution.py:461
  3.7 12.7 %collective-permute-start.1 = (bf16[128,1024]{1,0:T(8,128)(2,1)}, bf16[128,1024]{1,0:T(8,128)(2,1)}, u32[]{:S(2)}, u32[]{:S(2)}) collective-permute-start(bf16[128,1024]{1,0:T(8,128)(2,1)} %refs_0_.5), channel_id=1, source_target_pairs={{0,2},{1,3},{2,0},{3,1},{4,6},{5,7},{6,4},{7,5},{8,10},{9,11},{10,... | collective-permute-start | bytes 786440 | tf_op jit(solution)/shard_map/ppermute | solution.py:461
  3.9 12.5 %collective-permute-start = (bf16[128,1024]{1,0:T(8,128)(2,1)}, bf16[128,1024]{1,0:T(8,128)(2,1)}, u32[]{:S(2)}, u32[]{:S(2)}) collective-permute-start(bf16[128,1024]{1,0:T(8,128)(2,1)} %refs_0_.5), channel_id=1, source_target_pairs={{0,1},{1,0},{2,3},{3,2},{4,5},{5,4},{6,7},{7,6},{8,9},{9,8},{10,11... | collective-permute-start | bytes 786440 | tf_op jit(solution)/shard_map/ppermute | solution.py:461
  4.1 22.1 %collective-permute-start.7 = (bf16[64,7168]{1,0:T(8,128)(2,1)}, bf16[64,7168]{1,0:T(8,128)(2,1)}, u32[]{:S(2)}, u32[]{:S(2)}) collective-permute-start(bf16[64,7168]{1,0:T(8,128)(2,1)} %refs_0_.7), channel_id=1, source_target_pairs={{0,8},{4,12},{16,24},{20,28},{8,0},{12,4},{24,16},{28,20},{1,9},{5... | collective-permute-start | bytes 2752520 | tf_op jit(solution)/shard_map/ppermute | solution.py:474
  5.5 20.7 %collective-permute-start.5 = (bf16[64,7168]{1,0:T(8,128)(2,1)}, bf16[64,7168]{1,0:T(8,128)(2,1)}, u32[]{:S(2)}, u32[]{:S(2)}) collective-permute-start(bf16[64,7168]{1,0:T(8,128)(2,1)} %refs_0_.7), channel_id=1, source_target_pairs={{8,16},{12,20},{16,8},{20,12},{0,4},{4,0},{24,28},{28,24},{9,17},{... | collective-permute-start | bytes 2752520 | tf_op jit(solution)/shard_map/ppermute | solution.py:474
  25.3 11.3 %collective-permute-start.3 = (bf16[256,3584]{1,0:T(8,128)(2,1)}, bf16[256,3584]{1,0:T(8,128)(2,1)}, u32[]{:S(2)}, u32[]{:S(2)}) collective-permute-start(bf16[256,3584]{1,0:T(8,128)(2,1)} %get-tuple-element.30), channel_id=1, source_target_pairs={{0,4},{4,0},{8,12},{12,8},{16,20},{20,16},{24,28},{28,24},{1,5},{5... | collective-permute-start | bytes 5505032 | tf_op jit(solution)/shard_map/ppermute | solution.py:460
  35.0 4.8 %collective-permute-start.12 = (bf16[256,3584]{1,0:T(8,128)(2,1)}, bf16[256,3584]{1,0:T(8,128)(2,1)}, u32[]{:S(2)}, u32[]{:S(2)}) collective-permute-start(bf16[256,3584]{1,0:T(8,128)(2,1)} %get-tuple-element.32), channel_id=1, source_target_pairs={{0,4},{4,0},{8,12},{12,8},{16,20},{20,16},{24,28},{28,24},{1,5},{5... | collective-permute-start | bytes 5505032 | tf_op jit(solution)/shard_map/ppermute | solution.py:460
  36.1 7.8 %collective-permute-start.9 = (bf16[64,7168]{1,0:T(8,128)(2,1)}, bf16[64,7168]{1,0:T(8,128)(2,1)}, u32[]{:S(2)}, u32[]{:S(2)}) collective-permute-start(bf16[64,7168]{1,0:T(8,128)(2,1)} %refs_0_.7), channel_id=1, source_target_pairs={{0,4},{4,0},{8,12},{12,8},{16,20},{20,16},{24,28},{28,24},{1,5},{5... | collective-permute-start | bytes 2752520 | tf_op jit(solution)/shard_map/ppermute | solution.py:460
  36.1 11.9 %collective-permute-start.10 = (bf16[64,7168]{1,0:T(8,128)(2,1)}, bf16[64,7168]{1,0:T(8,128)(2,1)}, u32[]{:S(2)}, u32[]{:S(2)}) collective-permute-start(bf16[64,7168]{1,0:T(8,128)(2,1)} %collective-permute-done.7.refs_6_.refs_2_), channel_id=1, source_target_pairs={{0,4},{4,0},{8,12},{12,8},{16,20},{20,16},{24,28},{28,24},{1,5},{5... | collective-permute-start | bytes 2752520 | tf_op jit(solution)/shard_map/ppermute | solution.py:460
  36.6 13.5 %collective-permute-start.11 = (bf16[64,7168]{1,0:T(8,128)(2,1)}, bf16[64,7168]{1,0:T(8,128)(2,1)}, u32[]{:S(2)}, u32[]{:S(2)}) collective-permute-start(bf16[64,7168]{1,0:T(8,128)(2,1)} %collective-permute-done.5.refs_7_.refs_4_), channel_id=1, source_target_pairs={{0,4},{4,0},{8,12},{12,8},{16,20},{20,16},{24,28},{28,24},{1,5},{5... | collective-permute-start | bytes 2752520 | tf_op jit(solution)/shard_map/ppermute | solution.py:460
  36.7 25.2 %collective-permute-start.8 = (bf16[64,7168]{1,0:T(8,128)(2,1)}, bf16[64,7168]{1,0:T(8,128)(2,1)}, u32[]{:S(2)}, u32[]{:S(2)}) collective-permute-start(bf16[64,7168]{1,0:T(8,128)(2,1)} %collective-permute-done.7.refs_6_.refs_2_), channel_id=1, source_target_pairs={{8,16},{12,20},{16,8},{20,12},{0,4},{4,0},{24,28},{28,24},{9,17},{... | collective-permute-start | bytes 2752520 | tf_op jit(solution)/shard_map/ppermute | solution.py:474
  39.8 24.6 %collective-permute-start.6 = (bf16[64,7168]{1,0:T(8,128)(2,1)}, bf16[64,7168]{1,0:T(8,128)(2,1)}, u32[]{:S(2)}, u32[]{:S(2)}) collective-permute-start(bf16[64,7168]{1,0:T(8,128)(2,1)} %collective-permute-done.5.refs_7_.refs_4_), channel_id=1, source_target_pairs={{16,24},{20,28},{8,0},{12,4},{17,25},{21,29},{9,1},{13,5},{18,26},... | collective-permute-start | bytes 2752520 | tf_op jit(solution)/shard_map/ppermute | solution.py:474
  43.9 21.8 %collective-permute-start.4 = (bf16[64,3584]{1,0:T(8,128)(2,1)}, bf16[64,3584]{1,0:T(8,128)(2,1)}, u32[]{:S(2)}, u32[]{:S(2)}) collective-permute-start(bf16[64,3584]{1,0:T(8,128)(2,1)} %send_sums.6.refs_2_), channel_id=1, source_target_pairs={{0,8},{4,12},{24,16},{28,20},{1,9},{5,13},{25,17},{29,21},{2,10},{... | collective-permute-start | bytes 1376264 | tf_op jit(solution)/shard_map/ppermute | solution.py:474
  48.0 31.5 %collective-permute-start.16 = (bf16[64,3584]{1,0:T(8,128)(2,1)}, bf16[64,3584]{1,0:T(8,128)(2,1)}, u32[]{:S(2)}, u32[]{:S(2)}) collective-permute-start(bf16[64,3584]{1,0:T(8,128)(2,1)} %send_sums.7.refs_8_), channel_id=1, source_target_pairs={{0,8},{4,12},{24,16},{28,20},{1,9},{5,13},{25,17},{29,21},{2,10},{... | collective-permute-start | bytes 1376264 | tf_op jit(solution)/shard_map/ppermute | solution.py:474
  64.4 23.2 %collective-permute-start.15 = (bf16[64,7168]{1,0:T(8,128)(2,1)}, bf16[64,7168]{1,0:T(8,128)(2,1)}, u32[]{:S(2)}, u32[]{:S(2)}) collective-permute-start(bf16[64,7168]{1,0:T(8,128)(2,1)} %collective-permute-done.8.refs_5_), channel_id=1, source_target_pairs={{16,24},{20,28},{8,0},{12,4},{17,25},{21,29},{9,1},{13,5},{18,26},... | collective-permute-start | bytes 2752520 | tf_op jit(solution)/shard_map/ppermute | solution.py:474
  68.5 9.7 %copy-start = (bf16[512,1024]{1,0:T(8,128)(2,1)S(1)}, bf16[512,1024]{1,0:T(8,128)(2,1)}, u32[]{:S(2)}) copy-start(bf16[512,1024]{1,0:T(8,128)(2,1)} %get-tuple-element.54) | copy-start | bytes 3145732
  68.5 20.9 %collective-permute-start.13 = (bf16[64,3584]{1,0:T(8,128)(2,1)}, bf16[64,3584]{1,0:T(8,128)(2,1)}, u32[]{:S(2)}, u32[]{:S(2)}) collective-permute-start(bf16[64,3584]{1,0:T(8,128)(2,1)} %get-tuple-element.36.refs_3_), channel_id=1, source_target_pairs={{0,8},{4,12},{24,16},{28,20},{1,9},{5,13},{25,17},{29,21},{2,10},{... | collective-permute-start | bytes 1376264 | tf_op jit(solution)/shard_map/ppermute | solution.py:474
  74.5 14.8 %collective-permute-start.14 = (bf16[64,3584]{1,0:T(8,128)(2,1)}, bf16[64,3584]{1,0:T(8,128)(2,1)}, u32[]{:S(2)}, u32[]{:S(2)}) collective-permute-start(bf16[64,3584]{1,0:T(8,128)(2,1)} %get-tuple-element.37.refs_4_), channel_id=1, source_target_pairs={{8,16},{12,20},{16,8},{20,12},{0,4},{4,0},{24,28},{28,24},{9,17},{... | collective-permute-start | bytes 1376264 | tf_op jit(solution)/shard_map/ppermute | solution.py:474
  79.5 14.6 %collective-permute-start.21 = (bf16[64,7168]{1,0:T(8,128)(2,1)}, bf16[64,7168]{1,0:T(8,128)(2,1)}, u32[]{:S(2)}, u32[]{:S(2)}) collective-permute-start(bf16[64,7168]{1,0:T(8,128)(2,1)} %broadcast_select_fusion.refs_0_.refs_6_), channel_id=1, source_target_pairs={{0,4},{4,0},{8,12},{12,8},{16,20},{20,16},{24,28},{28,24},{1,5},{5... | collective-permute-start | bytes 2752520 | tf_op jit(solution)/shard_map/ppermute | solution.py:460
  82.3 24.4 %collective-permute-start.19 = (bf16[64,3584]{1,0:T(8,128)(2,1)}, bf16[64,3584]{1,0:T(8,128)(2,1)}, u32[]{:S(2)}, u32[]{:S(2)}) collective-permute-start(bf16[64,3584]{1,0:T(8,128)(2,1)} %get-tuple-element.40.refs_4_), channel_id=1, source_target_pairs={{0,8},{4,12},{24,16},{28,20},{1,9},{5,13},{25,17},{29,21},{2,10},{... | collective-permute-start | bytes 1376264 | tf_op jit(solution)/shard_map/ppermute | solution.py:474
  87.6 20.4 %collective-permute-start.20 = (bf16[64,3584]{1,0:T(8,128)(2,1)}, bf16[64,3584]{1,0:T(8,128)(2,1)}, u32[]{:S(2)}, u32[]{:S(2)}) collective-permute-start(bf16[64,3584]{1,0:T(8,128)(2,1)} %get-tuple-element.41.refs_5_), channel_id=1, source_target_pairs={{8,16},{12,20},{16,8},{20,12},{0,4},{4,0},{24,28},{28,24},{9,17},{... | collective-permute-start | bytes 1376264 | tf_op jit(solution)/shard_map/ppermute | solution.py:474
  89.4 5.1 %collective-permute-start.22 = (bf16[64,7168]{1,0:T(8,128)(2,1)}, bf16[64,7168]{1,0:T(8,128)(2,1)}, u32[]{:S(2)}, u32[]{:S(2)}) collective-permute-start(bf16[64,7168]{1,0:T(8,128)(2,1)} %collective-permute-done.15.refs_2_.refs_8_), channel_id=1, source_target_pairs={{0,4},{4,0},{8,12},{12,8},{16,20},{20,16},{24,28},{28,24},{1,5},{5... | collective-permute-start | bytes 2752520 | tf_op jit(solution)/shard_map/ppermute | solution.py:460
  92.3 18.8 %collective-permute-start.17 = (bf16[64,3584]{1,0:T(8,128)(2,1)}, bf16[64,3584]{1,0:T(8,128)(2,1)}, u32[]{:S(2)}, u32[]{:S(2)}) collective-permute-start(bf16[64,3584]{1,0:T(8,128)(2,1)} %get-tuple-element.42.refs_7_), channel_id=1, source_target_pairs={{0,8},{4,12},{16,24},{20,28},{8,0},{12,4},{24,16},{28,20},{1,9},{5... | collective-permute-start | bytes 1376264 | tf_op jit(solution)/shard_map/ppermute | solution.py:474
  94.1 17.6 %collective-permute-start.18 = (bf16[64,3584]{1,0:T(8,128)(2,1)}, bf16[64,3584]{1,0:T(8,128)(2,1)}, u32[]{:S(2)}, u32[]{:S(2)}) collective-permute-start(bf16[64,3584]{1,0:T(8,128)(2,1)} %get-tuple-element.43.refs_8_), channel_id=1, source_target_pairs={{8,16},{12,20},{16,8},{20,12},{0,4},{4,0},{24,28},{28,24},{9,17},{... | collective-permute-start | bytes 1376264 | tf_op jit(solution)/shard_map/ppermute | solution.py:474
  105.4 21.5 %collective-permute-start.25 = (bf16[128,1024]{1,0:T(8,128)(2,1)}, bf16[128,1024]{1,0:T(8,128)(2,1)}, u32[]{:S(2)}, u32[]{:S(2)}) collective-permute-start(bf16[128,1024]{1,0:T(8,128)(2,1)} %get-tuple-element.46.refs_5_), channel_id=1, source_target_pairs={{0,1},{1,0},{2,3},{3,2},{4,5},{5,4},{6,7},{7,6},{8,9},{9,8},{10,11... | collective-permute-start | bytes 786440 | tf_op jit(solution)/shard_map/ppermute | solution.py:461
  106.7 20.2 %collective-permute-start.26 = (bf16[128,1024]{1,0:T(8,128)(2,1)}, bf16[128,1024]{1,0:T(8,128)(2,1)}, u32[]{:S(2)}, u32[]{:S(2)}) collective-permute-start(bf16[128,1024]{1,0:T(8,128)(2,1)} %get-tuple-element.47.refs_6_), channel_id=1, source_target_pairs={{0,2},{1,3},{2,0},{3,1},{4,6},{5,7},{6,4},{7,5},{8,10},{9,11},{10,... | collective-permute-start | bytes 786440 | tf_op jit(solution)/shard_map/ppermute | solution.py:461
  107.9 19.0 %collective-permute-start.27 = (bf16[128,1024]{1,0:T(8,128)(2,1)}, bf16[128,1024]{1,0:T(8,128)(2,1)}, u32[]{:S(2)}, u32[]{:S(2)}) collective-permute-start(bf16[128,1024]{1,0:T(8,128)(2,1)} %get-tuple-element.48.refs_7_), channel_id=1, source_target_pairs={{0,3},{1,2},{2,1},{3,0},{4,7},{5,6},{6,5},{7,4},{8,11},{9,10},{10,... | collective-permute-start | bytes 786440 | tf_op jit(solution)/shard_map/ppermute | solution.py:461
  111.1 15.9 %collective-permute-start.23 = (bf16[64,3584]{1,0:T(8,128)(2,1)}, bf16[64,3584]{1,0:T(8,128)(2,1)}, u32[]{:S(2)}, u32[]{:S(2)}) collective-permute-start(bf16[64,3584]{1,0:T(8,128)(2,1)} %get-tuple-element.49), channel_id=1, source_target_pairs={{0,8},{4,12},{16,24},{20,28},{8,0},{12,4},{24,16},{28,20},{1,9},{5... | collective-permute-start | bytes 1376264 | tf_op jit(solution)/shard_map/ppermute | solution.py:474
  111.7 15.3 %collective-permute-start.24 = (bf16[64,3584]{1,0:T(8,128)(2,1)}, bf16[64,3584]{1,0:T(8,128)(2,1)}, u32[]{:S(2)}, u32[]{:S(2)}) collective-permute-start(bf16[64,3584]{1,0:T(8,128)(2,1)} %get-tuple-element.50), channel_id=1, source_target_pairs={{8,16},{12,20},{16,8},{20,12},{0,4},{4,0},{24,28},{28,24},{9,17},{... | collective-permute-start | bytes 1376264 | tf_op jit(solution)/shard_map/ppermute | solution.py:474
